TPU v7x, 32 devices: a whole 2x2x4 slice. The times are simulated.
32 devices in a mesh: sfc: 16 (over z, x, core), sub: 2 (over y).
Axes of the slice: x: 2, y: 2, z: 4, core: 2. Of those that a mesh axis runs over, the one named last changes fastest.
Arguments:
- fine_state: float32 [16, 2, 2, 5, 512], P('sfc', 'sub'), as said below
- coarse_old: float32 [16, 2, 5, 512], P('sfc', 'sub'), as said below
- box_count: int32 [16, 2], P('sfc', 'sub'), may hold values from 1 to 2, as said below
- fine_links: int32 [16, 2, 2, 6], P('sfc', 'sub'), may hold values from -1 to 5, as said below
- coarse_links: int32 [16, 2, 2, 6, 4], P('sfc', 'sub'), may hold values from 0 to 4
Outputs:
- advanced_state: float32 [16, 2, 2, 5, 512], P('sfc', 'sub')
Inputs may be any that keep to these rules, and one draw needn't show every extreme that they name: Slots 0 to box_count - 1 of a device are live. Some device holds 2 live boxes in every draw. `fine_links`: A value v >= 0 names slot v mod 2 of the device at curve segment offset v div 2 - 1 (-1, 0 or +1) in the same group member, and that slot is live; the first segment has no offset -1 and the last no offset +1. Dead slots hold -1. Of one device's faces at most 2 take ghosts from offset -1 and at most 2 from offset +1; both bounds are reached in every draw. `fine_state`: mass and pressure of every cell are positive and of order one, each velocity component below one in magnitude. `coarse_old`: as for fine_state.
All inputs are finite; a program needn't handle non-finite values.
Results may differ from a plain program's by a relative error of at most 0.0003.
Values sent between devices are 32-bit elements; how exact they have to be, the bound alone decides.
No kernel may reach another device: no remote copies, remote signals or barrier semaphores. Data moves between devices by JAX's collectives and lax.ppermute only.
A program may use at most 64 MiB of HBM per device.

v0:
```python
import jax
import jax.numpy as jnp
import numpy as np
from jax import lax
from jax.sharding import PartitionSpec as P

B = 8


GAMMA = 1.4
FLOOR = 0.1
WENO_EPS = 1e-06
TIME_STEP = 0.1
FIELD_ORDER = ((0, 1, 2, 3, 4), (0, 2, 1, 3, 4), (0, 3, 1, 2, 4))
FIELD_BACK = ((0, 1, 2, 3, 4), (0, 2, 1, 3, 4), (0, 2, 3, 1, 4))
OPPOSITE = (1, 0, 3, 2, 5, 4)


def passed_along(value, axis, steps):
    count = lax.axis_size(axis)
    first, last = (max(0, -steps), min(count, count - steps))
    return lax.ppermute(value, axis, [(source, source + steps) for source in range(first, last)])


def primitives(conserved):
    density = jnp.maximum(conserved[:, 0], FLOOR)
    normal = conserved[:, 1] / density
    side_one = conserved[:, 2] / density
    side_two = conserved[:, 3] / density
    kinetic = 0.5 * density * (normal * normal + side_one * side_one + side_two * side_two)
    pressure = jnp.maximum((GAMMA - 1.0) * (conserved[:, 4] - kinetic), FLOOR)
    return jnp.stack([density, normal, side_one, side_two, pressure], axis=1)


def weno_face(far_left, near_left, centre, near_right, far_right):
    cand_a = (2.0 * far_left - 7.0 * near_left + 11.0 * centre) / 6.0
    cand_b = (-near_left + 5.0 * centre + 2.0 * near_right) / 6.0
    cand_c = (2.0 * centre + 5.0 * near_right - far_right) / 6.0
    smooth_a = (
        13.0 / 12.0 * (far_left - 2.0 * near_left + centre) ** 2
        + 0.25 * (far_left - 4.0 * near_left + 3.0 * centre) ** 2
    )
    smooth_b = (
        13.0 / 12.0 * (near_left - 2.0 * centre + near_right) ** 2
        + 0.25 * (near_left - near_right) ** 2
    )
    smooth_c = (
        13.0 / 12.0 * (centre - 2.0 * near_right + far_right) ** 2
        + 0.25 * (3.0 * centre - 4.0 * near_right + far_right) ** 2
    )
    weight_a = 0.1 / (WENO_EPS + smooth_a) ** 2
    weight_b = 0.6 / (WENO_EPS + smooth_b) ** 2
    weight_c = 0.3 / (WENO_EPS + smooth_c) ** 2
    return (weight_a * cand_a + weight_b * cand_b + weight_c * cand_c) / (
        weight_a + weight_b + weight_c
    )


def floor_faces(face_state):
    return jnp.concatenate(
        [
            jnp.maximum(face_state[:, :1], FLOOR),
            face_state[:, 1:4],
            jnp.maximum(face_state[:, 4:], FLOOR),
        ],
        axis=1,
    )


def side_terms(face_state):
    density = face_state[:, 0]
    normal = face_state[:, 1]
    side_one = face_state[:, 2]
    side_two = face_state[:, 3]
    pressure = face_state[:, 4]
    energy = pressure / (GAMMA - 1.0) + 0.5 * density * (
        normal * normal + side_one * side_one + side_two * side_two
    )
    sound_speed = jnp.sqrt(GAMMA * pressure / density)
    conserved = [density, density * normal, density * side_one, density * side_two, energy]
    face_flux = [
        density * normal,
        density * normal * normal + pressure,
        density * normal * side_one,
        density * normal * side_two,
        normal * (energy + pressure),
    ]
    return (
        density,
        normal,
        side_one,
        side_two,
        pressure,
        energy,
        sound_speed,
        conserved,
        face_flux,
    )


def star_flux(terms, wave_speed, contact):
    density, normal, side_one, side_two, pressure, energy, sound_speed, conserved, face_flux = terms
    mass_rate = density * (wave_speed - normal)
    factor = mass_rate / (wave_speed - contact)
    star_state = [
        factor,
        factor * contact,
        factor * side_one,
        factor * side_two,
        factor * (energy / density + (contact - normal) * (contact + pressure / mass_rate)),
    ]
    return [
        face_flux[field_number] + wave_speed * (star_state[field_number] - conserved[field_number])
        for field_number in range(5)
    ]


def hllc_flux(left_state, right_state):
    left_terms = side_terms(left_state)
    right_terms = side_terms(right_state)
    speed_left = jnp.minimum(left_terms[1] - left_terms[6], right_terms[1] - right_terms[6])
    speed_right = jnp.maximum(left_terms[1] + left_terms[6], right_terms[1] + right_terms[6])
    mass_left = left_terms[0] * (speed_left - left_terms[1])
    mass_right = right_terms[0] * (speed_right - right_terms[1])
    contact = (
        right_terms[4] - left_terms[4] + mass_left * left_terms[1] - mass_right * right_terms[1]
    ) / (mass_left - mass_right)
    star_left = star_flux(left_terms, speed_left, contact)
    star_right = star_flux(right_terms, speed_right, contact)
    result_list = []
    for field_number in range(5):
        chosen = jnp.where(
            speed_left >= 0.0,
            left_terms[8][field_number],
            jnp.where(
                contact >= 0.0,
                star_left[field_number],
                jnp.where(
                    speed_right >= 0.0, star_right[field_number], right_terms[8][field_number]
                ),
            ),
        )
        result_list.append(chosen)
    return jnp.stack(result_list, axis=1)


def sweep_along(extended, axis_number):
    primitive_cells = primitives(extended)
    face_count = extended.shape[axis_number] - 5
    pieces = [
        lax.slice_in_dim(primitive_cells, start_cell, start_cell + face_count, axis=axis_number)
        for start_cell in range(6)
    ]
    left_face = floor_faces(weno_face(pieces[0], pieces[1], pieces[2], pieces[3], pieces[4]))
    right_face = floor_faces(weno_face(pieces[5], pieces[4], pieces[3], pieces[2], pieces[1]))
    face_flux = hllc_flux(left_face, right_face)
    return lax.slice_in_dim(face_flux, 0, face_count - 1, axis=axis_number) - lax.slice_in_dim(
        face_flux, 1, face_count, axis=axis_number
    )


def face_slabs(field):
    slot_count = field.shape[0]
    edge_cells = field.shape[2]
    slab_list = []
    for face_number in range(6):
        axis_number = 2 + face_number // 2
        if face_number % 2 == 0:
            layers = lax.slice_in_dim(field, 0, 3, axis=axis_number)
        else:
            layers = lax.slice_in_dim(field, edge_cells - 3, edge_cells, axis=axis_number)
        layers = jnp.moveaxis(layers, axis_number, 2)
        slab_list.append(layers.reshape(slot_count, 5, -1))
    return jnp.stack(slab_list, axis=1)


def rate_of(field, ghosts):
    slot_count = field.shape[0]
    edge_cells = field.shape[2]
    change_sum = jnp.zeros(field.shape, jnp.float32)
    for direction in range(3):
        axis_number = 2 + direction
        lower_ghost = jnp.moveaxis(
            ghosts[:, 2 * direction].reshape(slot_count, 5, 3, edge_cells, edge_cells),
            2,
            axis_number,
        )
        upper_ghost = jnp.moveaxis(
            ghosts[:, 2 * direction + 1].reshape(slot_count, 5, 3, edge_cells, edge_cells),
            2,
            axis_number,
        )
        extended = jnp.concatenate([lower_ghost, field, upper_ghost], axis=axis_number)
        extended = extended[:, np.array(FIELD_ORDER[direction])]
        change = sweep_along(extended, axis_number)[:, np.array(FIELD_BACK[direction])]
        change_sum = change_sum + change
    return change_sum


def minmod(first_diff, second_diff):
    return (
        0.5
        * (jnp.sign(first_diff) + jnp.sign(second_diff))
        * jnp.minimum(jnp.abs(first_diff), jnp.abs(second_diff))
    )


def refine(region):
    interior = region[:, :, 1:-1, 1:-1, 1:-1]
    slope_x = minmod(
        region[:, :, 2:, 1:-1, 1:-1] - interior, interior - region[:, :, :-2, 1:-1, 1:-1]
    )
    slope_y = minmod(
        region[:, :, 1:-1, 2:, 1:-1] - interior, interior - region[:, :, 1:-1, :-2, 1:-1]
    )
    slope_z = minmod(
        region[:, :, 1:-1, 1:-1, 2:] - interior, interior - region[:, :, 1:-1, 1:-1, :-2]
    )
    quarter = jnp.array([-0.25, 0.25], dtype=jnp.float32)

    def spread(values):
        return values[:, :, :, None, :, None, :, None]

    children = (
        spread(interior)
        + spread(slope_x) * quarter.reshape(2, 1, 1, 1, 1)
        + spread(slope_y) * quarter.reshape(2, 1, 1)
        + spread(slope_z) * quarter
    )
    shape_in = interior.shape
    return children.reshape(
        shape_in[0], shape_in[1], 2 * shape_in[2], 2 * shape_in[3], 2 * shape_in[4]
    )


def coarse_ghosts(group_boxes, link_table):
    edge_cells = group_boxes.shape[2]
    slot_count = link_table.shape[0]
    zero_start = jnp.zeros((), jnp.int32)
    slab_list = []
    for face_number in range(6):
        direction = face_number // 2
        extent = tuple(
            (4 if axis_number == direction else edge_cells // 2 + 2 for axis_number in range(3))
        )

        def cut_region(link_entry):
            starts = (link_entry[0], zero_start, link_entry[1], link_entry[2], link_entry[3])
            return lax.dynamic_slice(group_boxes, starts, (1, 5) + extent)[0]

        region = jax.vmap(cut_region)(link_table[:, face_number])
        children = refine(region)
        reordered = jnp.moveaxis(children, 2 + direction, 2)
        reordered = reordered.reshape(slot_count, 5, 4, edge_cells * edge_cells)
        if face_number % 2 == 0:
            layers = reordered[:, :, 1:]
        else:
            layers = reordered[:, :, :3]
        slab_list.append(layers.reshape(slot_count, 5, -1))
    return jnp.stack(slab_list, axis=1)


def body(fine_state, coarse_old, box_count, fine_links, coarse_links):
    slot_count = fine_state.shape[2]
    states = fine_state[0, 0].reshape(slot_count, 5, B, B, B)
    old_group = lax.all_gather(coarse_old, "sub", axis=1, tiled=True)
    members = old_group.shape[1]
    old_boxes = old_group[0].reshape(members, 5, B, B, B)
    face_links = fine_links[0, 0]
    link_table = coarse_links[0, 0]
    live_count = box_count[0, 0]
    slot_ids = jnp.arange(slot_count, dtype=jnp.int32)[:, None]
    face_ids = jnp.arange(6, dtype=jnp.int32)[None, :]
    opposite = jnp.array(OPPOSITE, dtype=jnp.int32)[None, :]
    source = face_links // slot_count
    source_slot = face_links % slot_count
    linked = face_links >= 0
    local_row = source_slot * 6 + opposite
    coarse_row = slot_ids * 6 + face_ids
    block_id = jnp.where(source == 1, 0, jnp.where(source == 0, 1, 2)).astype(jnp.int32)
    position = jnp.where(
        linked, block_id * 6 * slot_count + local_row, 18 * slot_count + coarse_row
    )

    def neighbour_rows(exported):
        shifted = [passed_along(exported, "sfc", offset) for offset in (1, -1)]
        return (shifted[0], shifted[1])

    coarse_table = coarse_ghosts(old_boxes, link_table).reshape(6 * slot_count, 5, -1)

    def section(current):
        exported = face_slabs(current).reshape(6 * slot_count, 5, -1)
        from_below, from_above = neighbour_rows(exported)
        ghost_table = jnp.concatenate([exported, from_below, from_above, coarse_table], axis=0)
        ghosts = ghost_table[position]
        return rate_of(current, ghosts)

    first_rate = section(states)
    middle = states + TIME_STEP * first_rate
    second_rate = section(middle)
    updated = 0.5 * states + 0.5 * (middle + TIME_STEP * second_rate)
    updated = updated.reshape(slot_count, 5, B * B * B)
    live_mask = jnp.arange(slot_count, dtype=jnp.int32) < live_count
    updated = jnp.where(live_mask[:, None, None], updated, jnp.zeros_like(updated))
    return updated[None, None]


def solution(mesh):
    placed = (
        P("sfc", "sub", None, None, None),
        P("sfc", "sub", None, None),
        P("sfc", "sub"),
        P("sfc", "sub", None, None),
        P("sfc", "sub", None, None, None),
    )
    return jax.shard_map(
        body,
        mesh=mesh,
        in_specs=placed,
        out_specs=P("sfc", "sub", None, None, None),
        check_vma=False,
    )
```

profile of v0, /device:TPU:23, one launch (start us, length us, event | category | flops | bytes accessed | tf_op | source)
XLA Modules:
  0.0 84.0 jit_solution(11450521988856068573)
XLA Ops:
  0.0 0.9 %reshape_squeeze.42 = f32[2,5,8,8,8]{4,3,2,0,1:T(8,128)S(1)} reshape(f32[1,1,2,5,512]{4,2,3,1,0:T(2,128)} %param.36) | data formatting | bytes 40960 | tf_op jit(solution)/shard_map/reshape;squeeze | solution.py:265
  3.2 3.7 %collective-permute-start = (f32[12,5,192]{2,1,0:T(8,128)S(1)}, f32[12,5,192]{2,1,0:T(8,128)S(1)}, u32[]{:S(2)}, u32[]{:S(2)}) collective-permute-start(f32[12,5,192]{2,1,0:T(8,128)S(1)} %bitcast.378), channel_id=1, source_target_pairs={{0,2},{2,4},{4,6},{6,8},{8,10},{10,12},{12,14},{14,16},{16,18},{18... | collective-permute-start | bytes 138248 | tf_op jit(solution)/shard_map/ppermute | solution.py:22
  6.9 1.9 %collective-permute-start.1 = (f32[12,5,192]{2,1,0:T(8,128)S(1)}, f32[12,5,192]{2,1,0:T(8,128)S(1)}, u32[]{:S(2)}, u32[]{:S(2)}) collective-permute-start(f32[12,5,192]{2,1,0:T(8,128)S(1)} %bitcast.379), channel_id=1, source_target_pairs={{2,0},{4,2},{6,4},{8,6},{10,8},{12,10},{14,12},{16,14},{18,16},{20... | collective-permute-start | bytes 138248 | tf_op jit(solution)/shard_map/ppermute | solution.py:22
  9.6 3.2 %all_gather.3 = f32[1,2,5,512]{3,0,2,1:T(1,128)S(1)} all-gather(f32[1,1,5,512]{3,0,2,1:T(1,128)S(1)} %bitcast.389), channel_id=1, replica_groups=mesh['sfc'=16,'sub'=2] {'sub'}, dimensions={1}, use_global_device_ids=true | all-gather | bytes 30720 | tf_op jit(solution)/shard_map/all_gather | solution.py:266
  13.2 1.2 %gather_fusion.4 = f32[2,5,6,6,4]{1,0,4,3,2:T(2,128)S(1)} fusion(f32[2,5,8,8,8]{1,0,4,3,2:T(2,128)S(1)} %bitcast.324, s32[2]{0:T(128)S(1)} %get-tuple-element.161), kind=kCustom, calls=%fused_computation.4 | custom fusion | bytes 11560 | tf_op jit(solution)/shard_map/vmap()/gather | solution.py:249
  14.5 1.2 %gather_fusion.5 = f32[2,5,6,6,4]{1,0,4,3,2:T(2,128)S(1)} fusion(f32[2,5,8,8,8]{1,0,4,3,2:T(2,128)S(1)} %bitcast.325, s32[2]{0:T(128)S(1)} %get-tuple-element.160), kind=kCustom, calls=%fused_computation.5 | custom fusion | bytes 11560 | tf_op jit(solution)/shard_map/vmap()/gather | solution.py:249
  16.1 0.6 copy-done.2
  19.1 1.2 %gather_fusion.2 = f32[2,5,6,4,6]{1,0,4,3,2:T(2,128)S(1)} fusion(f32[2,5,8,8,8]{1,0,4,3,2:T(2,128)S(1)} %bitcast.326, s32[2]{0:T(128)S(1)} %get-tuple-element.163), kind=kCustom, calls=%fused_computation.2 | custom fusion | bytes 11560 | tf_op jit(solution)/shard_map/vmap()/gather | solution.py:249
  20.3 1.2 %gather_fusion.3 = f32[2,5,6,4,6]{1,0,4,3,2:T(2,128)S(1)} fusion(f32[2,5,8,8,8]{1,0,4,3,2:T(2,128)S(1)} %bitcast.327, s32[2]{0:T(128)S(1)} %get-tuple-element.162), kind=kCustom, calls=%fused_computation.3 | custom fusion | bytes 11560 | tf_op jit(solution)/shard_map/vmap()/gather | solution.py:249
  24.1 1.2 %gather_fusion = f32[2,5,4,6,6]{1,0,4,3,2:T(2,128)S(1)} fusion(f32[2,5,8,8,8]{1,0,4,3,2:T(2,128)S(1)} %bitcast.328, s32[2]{0:T(128)S(1)} %get-tuple-element.165), kind=kCustom, calls=%fused_computation | custom fusion | bytes 11560 | tf_op jit(solution)/shard_map/vmap()/gather | solution.py:249
  25.3 1.2 %gather_fusion.1 = f32[2,5,4,6,6]{1,0,4,3,2:T(2,128)S(1)} fusion(f32[2,5,8,8,8]{1,0,4,3,2:T(2,128)S(1)} %bitcast.329, s32[2]{0:T(128)S(1)} %get-tuple-element.164), kind=kCustom, calls=%fused_computation.1 | custom fusion | bytes 11560 | tf_op jit(solution)/shard_map/vmap()/gather | solution.py:249
  27.8 0.7 copy-done.4
  28.7 0.6 copy-done.7
  29.4 0.6 copy-done.5
  31.1 0.6 gather_fusion.6
  31.8 0.5 copy.406
  32.4 0.5 copy.407
  33.2 0.6 gather_fusion.9
  33.8 0.6 copy.409
  34.6 3.2 %fusion.33 = (f32[2,5,8,9,8]{4,3,2,0,1:T(8,128)S(1)}, f32[2,5,8,9,8]{4,3,2,0,1:T(8,128)S(1)}) fusion(f32[2,5,8,14,8]{4,3,2,0,1:T(8,128)S(1)} %constant_dynamic-update-slice_fusion.22), kind=kLoop, calls=%fused_computation.62 | loop fusion | flops 714240 | bytes 184320 | tf_op jit(solution)/shard_map/div | solution.py:54
  39.2 0.6 gather_fusion.10
  39.9 0.5 copy.402
  40.6 0.5 copy.404
  41.3 0.6 gather_fusion.7
  41.9 0.6 copy.405
  42.8 1.6 %fusion.77 = (f32[2,5,9,8,8]{4,3,2,0,1:T(8,128)S(1)}, f32[2,5,9,8,8]{4,3,2,0,1:T(8,128)S(1)}) fusion(f32[2,5,14,8,8]{4,3,2,0,1:T(8,128)S(1)} %constant_dynamic-update-slice_fusion.12), kind=kLoop, calls=%fused_computation.119 | loop fusion | flops 714240 | bytes 184320 | tf_op jit(solution)/shard_map/div | solution.py:54
  45.2 0.6 gather_fusion.8
  45.9 0.5 copy.410
  46.5 0.5 copy.411
  47.3 0.6 gather_fusion.11
  48.0 1.5 %fusion.101 = (f32[2,5,8,8,9]{4,3,2,0,1:T(8,128)S(1)}, f32[2,5,8,8,9]{4,3,2,0,1:T(8,128)S(1)}) fusion(f32[2,5,8,8,14]{4,3,2,0,1:T(8,128)S(1)} %constant_dynamic-update-slice_fusion.32), kind=kLoop, calls=%fused_computation.173 | loop fusion | flops 714240 | bytes 184320 | tf_op jit(solution)/shard_map/div | solution.py:54
  50.5 0.6 gather_fusion.12
  53.4 5.7 %collective-permute-start.2 = (f32[12,5,192]{2,1,0:T(8,128)S(1)}, f32[12,5,192]{2,1,0:T(8,128)S(1)}, u32[]{:S(2)}, u32[]{:S(2)}) collective-permute-start(f32[12,5,192]{2,1,0:T(8,128)S(1)} %bitcast.381), channel_id=1, source_target_pairs={{0,2},{2,4},{4,6},{6,8},{8,10},{10,12},{12,14},{14,16},{16,18},{18... | collective-permute-start | bytes 138248 | tf_op jit(solution)/shard_map/ppermute | solution.py:22
  59.1 2.1 %collective-permute-start.3 = (f32[12,5,192]{2,1,0:T(8,128)S(1)}, f32[12,5,192]{2,1,0:T(8,128)S(1)}, u32[]{:S(2)}, u32[]{:S(2)}) collective-permute-start(f32[12,5,192]{2,1,0:T(8,128)S(1)} %bitcast.382), channel_id=1, source_target_pairs={{2,0},{4,2},{6,4},{8,6},{10,8},{12,10},{14,12},{16,14},{18,16},{20... | collective-permute-start | bytes 138248 | tf_op jit(solution)/shard_map/ppermute | solution.py:22
  61.4 4.5 %collective-permute-done.3 = f32[12,5,192]{2,1,0:T(8,128)S(1)} collective-permute-done((f32[12,5,192]{2,1,0:T(8,128)S(1)}, f32[12,5,192]{2,1,0:T(8,128)S(1)}, u32[]{:S(2)}, u32[]{:S(2)}) %collective-permute-start.3) | collective-permute-done | bytes 46112 | tf_op jit(solution)/shard_map/ppermute | solution.py:22
  65.9 0.6 gather_fusion.13
  67.0 0.6 gather_fusion.16
  67.8 3.1 %fusion.11 = (f32[2,5,8,9,8]{4,3,2,0,1:T(8,128)S(1)}, f32[2,5,8,9,8]{4,3,2,0,1:T(8,128)S(1)}) fusion(f32[2,5,8,14,8]{4,3,2,0,1:T(8,128)S(1)} %constant_dynamic-update-slice_fusion.58), kind=kLoop, calls=%fused_computation.35 | loop fusion | flops 714240 | bytes 184320 | tf_op jit(solution)/shard_map/div | solution.py:54
  72.3 0.6 gather_fusion.17
  73.2 0.6 gather_fusion.14
  74.0 1.6 %fusion.55 = (f32[2,5,9,8,8]{4,3,2,0,1:T(8,128)S(1)}, f32[2,5,9,8,8]{4,3,2,0,1:T(8,128)S(1)}) fusion(f32[2,5,14,8,8]{4,3,2,0,1:T(8,128)S(1)} %constant_dynamic-update-slice_fusion.48), kind=kLoop, calls=%fused_computation.92 | loop fusion | flops 714240 | bytes 184320 | tf_op jit(solution)/shard_map/div | solution.py:54
  76.4 0.6 gather_fusion.15
  77.1 0.5 copy.427
  78.5 0.6 gather_fusion.18
  79.3 1.0 %add_divide_fusion.4 = (f32[2,5,8,8,9]{4,3,2,0,1:T(8,128)S(1)}, f32[2,5,8,8,9]{4,3,2,0,1:T(8,128)S(1)}) fusion(f32[2,5,8,8,14]{4,3,2,0,1:T(8,128)S(1)} %constant_dynamic-update-slice_fusion.68), kind=kLoop, calls=%fused_computation.158 | loop fusion | flops 449280 | bytes 184320 | tf_op jit(solution)/shard_map/div | solution.py:54
  80.2 0.6 fusion.89
  81.9 0.6 gather_fusion.19
  83.3 0.7 multiply_select_fusion
  (227 shorter events, 23.8 us)
Async XLA Ops:
  3.1 5.7 %copy-start = (s32[1,1,2,6,4]{3,4,2,1,0:T(4,128)S(1)}, s32[1,1,2,6,4]{3,4,2,1,0:T(4,128)}, u32[]{:S(2)}) copy-start(s32[1,1,2,6,4]{3,4,2,1,0:T(4,128)} %param.40) | copy-start | bytes 580
  3.2 27.9 %collective-permute-start = (f32[12,5,192]{2,1,0:T(8,128)S(1)}, f32[12,5,192]{2,1,0:T(8,128)S(1)}, u32[]{:S(2)}, u32[]{:S(2)}) collective-permute-start(f32[12,5,192]{2,1,0:T(8,128)S(1)} %bitcast.378), channel_id=1, source_target_pairs={{0,2},{2,4},{4,6},{6,8},{8,10},{10,12},{12,14},{14,16},{16,18},{18... | collective-permute-start | bytes 138248 | tf_op jit(solution)/shard_map/ppermute | solution.py:22
  6.9 24.1 %collective-permute-start.1 = (f32[12,5,192]{2,1,0:T(8,128)S(1)}, f32[12,5,192]{2,1,0:T(8,128)S(1)}, u32[]{:S(2)}, u32[]{:S(2)}) collective-permute-start(f32[12,5,192]{2,1,0:T(8,128)S(1)} %bitcast.379), channel_id=1, source_target_pairs={{2,0},{4,2},{6,4},{8,6},{10,8},{12,10},{14,12},{16,14},{18,16},{20... | collective-permute-start | bytes 138248 | tf_op jit(solution)/shard_map/ppermute | solution.py:22
  8.9 0.7 copy-start.3
  16.0 0.7 copy-start.2
  27.8 0.7 copy-start.4
  27.8 0.7 copy-start.8
  28.7 0.7 copy-start.7
  29.3 0.7 copy-start.5
  29.3 0.7 copy-start.6
  53.4 8.1 %collective-permute-start.2 = (f32[12,5,192]{2,1,0:T(8,128)S(1)}, f32[12,5,192]{2,1,0:T(8,128)S(1)}, u32[]{:S(2)}, u32[]{:S(2)}) collective-permute-start(f32[12,5,192]{2,1,0:T(8,128)S(1)} %bitcast.381), channel_id=1, source_target_pairs={{0,2},{2,4},{4,6},{6,8},{8,10},{10,12},{12,14},{14,16},{16,18},{18... | collective-permute-start | bytes 138248 | tf_op jit(solution)/shard_map/ppermute | solution.py:22
  59.1 6.8 %collective-permute-start.3 = (f32[12,5,192]{2,1,0:T(8,128)S(1)}, f32[12,5,192]{2,1,0:T(8,128)S(1)}, u32[]{:S(2)}, u32[]{:S(2)}) collective-permute-start(f32[12,5,192]{2,1,0:T(8,128)S(1)} %bitcast.382), channel_id=1, source_target_pairs={{2,0},{4,2},{6,4},{8,6},{10,8},{12,10},{14,12},{16,14},{18,16},{20... | collective-permute-start | bytes 138248 | tf_op jit(solution)/shard_map/ppermute | solution.py:22
  82.6 0.7 copy-start.1
where the time goes:
time: 84.4 us; the launch traced here: 84 us
  local copies, waits for them, and re-layouts  35.5 us (42%)
  other arithmetic  25.1 us (30%)
  starting transfers between devices  13.5 us (16%)
  waiting for transfers between devices  4.48 us (5%)
  blocking collectives  3.22 us (4%)
  between operations  2.21 us (3%)
    ppermute x4, starting transfers between devices, passed_along(): lax.ppermute(value, axis, [(source, source + steps) for source in range(f...  13.5 us
    div x7, other arithmetic, weno_face(): (weight_a * cand_a + weight_b * cand_b + weight_c * cand_c) / (weight_a +...  12 us
    gather x6, local copies, waits for them, and re-layouts, cut_region(): return lax.dynamic_slice(group_boxes, starts, (1, 5) + extent)[0]  7.02 us
    unnamed x54, other arithmetic  5.6 us
    gather x8, local copies, waits for them, and re-layouts, rate_of(): extended = extended[:, np.array(FIELD_ORDER[direction])]  4.64 us
    ppermute x4, waiting for transfers between devices, passed_along(): lax.ppermute(value, axis, [(source, source + steps) for source in range(f...  4.48 us
    unnamed x35, local copies, waits for them, and re-layouts  3.65 us
    gather x6, local copies, waits for them, and re-layouts, rate_of(): sweep_along(extended, axis_number)[:, np.array(FIELD_BACK[direction])]  3.42 us
  transfers between devices with their start and end apart: 4, of which 1 were waited for; matrix products, arithmetic and copies ran while one was open for 18% of the time, Pallas kernels for 0%

commit v1 on v0

v1 whole, which is shorter than its diff:
```python
import jax
import jax.numpy as jnp
from jax import lax
from jax.experimental import pallas as pl
from jax.experimental.pallas import tpu as pltpu
from jax.sharding import PartitionSpec as P

FIELDS = 5
ROWS = 8
LANES = 128
GAMMA = 1.4
FLOOR = 0.1
EPS4 = 4e-06
TIME_STEP = 0.1


def to_tiles(boxes):
    slots, fields = boxes.shape[2], boxes.shape[3]
    parts = boxes.reshape(slots, fields, -1, LANES)
    return parts.transpose(1, 2, 0, 3).reshape(-1, LANES)


def from_tiles(tiles, shape):
    slots, fields = shape[2], shape[3]
    parts = tiles.reshape(fields, -1, slots, LANES)
    return parts.transpose(2, 0, 1, 3).reshape(shape)


def in_vmem(value):
    return pltpu.with_memory_space_constraint(value, pltpu.VMEM)


def exchange(value, partner):
    count, members = lax.axis_size("sfc"), lax.axis_size("sub")
    pairs = []
    for segment in range(count):
        for member in range(members):
            other, other_member = partner(segment, member, count, members)
            pairs.append((segment * members + member, other * members + other_member))
    return lax.ppermute(value, ("sfc", "sub"), pairs)


def even_partner(segment, member, count, members):
    other = segment ^ 1
    return (other, member) if other < count else (segment, member)


def odd_partner(segment, member, count, members):
    other = ((segment - 1) ^ 1) + 1
    if 0 < segment and other < count:
        return (other, member)
    other_member = member ^ 1
    return (segment, other_member) if other_member < members else (segment, member)


def group_shift(steps):
    def partner(segment, member, count, members):
        return (segment, (member + steps) % members)

    return partner


def positions():
    sub = lax.broadcasted_iota(jnp.int32, (ROWS, LANES), 0)
    lane = lax.broadcasted_iota(jnp.int32, (ROWS, LANES), 1)
    return sub, lane


def gather_lanes(value, index):
    return jnp.take_along_axis(value, index, axis=1, mode="promise_in_bounds")


def roll_lanes(value, steps):
    return pltpu.roll(value, steps % LANES, 1)


def roll_rows(value, steps):
    return pltpu.roll(value, steps % ROWS, 0)


def reciprocal(value):
    guess = pl.reciprocal(value, approx=True)
    return guess * (2.0 - value * guess)


def primitives(mass, mom_x, mom_y, mom_z, energy):
    density = jnp.maximum(mass, FLOOR)
    inverse = reciprocal(density)
    vel_x, vel_y, vel_z = mom_x * inverse, mom_y * inverse, mom_z * inverse
    kinetic = 0.5 * density * (vel_x * vel_x + vel_y * vel_y + vel_z * vel_z)
    pressure = jnp.maximum((GAMMA - 1.0) * (energy - kinetic), FLOOR)
    return [density, vel_x, vel_y, vel_z, pressure]


def load_primitives(ref, base=0):
    return primitives(*[ref[pl.ds(base + ROWS * f, ROWS), :] for f in range(FIELDS)])


def minmod(p, q):
    return jnp.maximum(jnp.minimum(p, q), 0.0) + jnp.minimum(jnp.maximum(p, q), 0.0)


def prepare(links_ref, corner_ref, count_ref, *refs):
    coarse_refs, (ghost_ref, pick_ref, live_ref, table, lines) = refs[:-5], refs[-5:]
    members = len(coarse_refs)
    sub, lane = positions()
    low = lane < 64
    y, z = (lane >> 3) & 7, lane & 7
    me = lax.axis_index("sub")
    odd_segment = lax.axis_index("sfc") & 1

    for m in range(members):
        for j in range(4):
            table[m * 16 + j, 0:FIELDS, :] = coarse_refs[m][pl.ds(j, FIELDS, stride=4), :]
    for m in range(members):
        cells = [table[m * 16 + j] for j in range(4)]
        halves = [roll_lanes(c, 64) for c in cells]
        for j in range(4):
            u = cells[j]
            up = jnp.where(low, halves[j], halves[min(j + 1, 3)])
            down = jnp.where(low, halves[max(j - 1, 0)], halves[j])
            table[m * 16 + 4 + j] = 0.25 * minmod(up - u, u - down)
            table[m * 16 + 8 + j] = 0.25 * minmod(roll_lanes(u, -8) - u, u - roll_lanes(u, 8))
            table[m * 16 + 12 + j] = 0.25 * minmod(roll_lanes(u, -1) - u, u - roll_lanes(u, 1))

    sign_x = jnp.where(low, -1.0, 1.0)
    sign_y = jnp.where((y & 1) == 0, -1.0, 1.0)
    sign_z = jnp.where((z & 1) == 0, -1.0, 1.0)
    spread = (y >> 1) * 8 + (z >> 1)

    def children(slot, face, j):
        direction, minus = face // 2, face % 2 == 0
        start = [corner_ref[slot, face * 4 + 1 + a] + (-1 if minus and a == direction else 1) for a in range(3)]
        owner = me - corner_ref[slot, face * 4]
        owner = jnp.where(owner < 0, owner + members, owner)
        along = start[0] + j
        index = (spread + ((along & 1) * 64 + start[1] * 8 + start[2])) & (LANES - 1)
        row = owner * 16 + (along >> 1)
        parts = [gather_lanes(table[row + 4 * q], index) for q in range(4)]
        return parts[0] + sign_x * parts[1] + sign_y * parts[2] + sign_z * parts[3]

    for direction in range(3):
        for slot in range(2):
            for j in range(4):
                minus, plus = 2 * direction, 2 * direction + 1
                if direction == 0:
                    value = children(slot, minus if j >= 2 else plus, j)
                else:
                    lower = (y if direction == 1 else z) < 4
                    value = jnp.where(lower, children(slot, plus, j), children(slot, minus, j))
                rows = pl.ds(direction * 40 + j * 2 + slot, FIELDS, stride=ROWS)
                lines[rows, :] = value[0:FIELDS, :]
        made = load_primitives(lines, direction * 40)
        for f in range(FIELDS):
            ghost_ref[pl.ds(direction * 40 + f * ROWS, ROWS), :] = made[f]

    def choice(slot, face):
        link = links_ref[slot, face]
        offset = link >> 1
        below = jnp.where(offset == 0, 1, 0)
        block = jnp.where(offset == 1, 0, jnp.where(below == odd_segment, 1, 2))
        swapped = (link & 1) ^ slot
        return jnp.where(link < 0, 0, 1 + block * 2 + swapped)

    first = (sub & 1) == 0
    for direction in range(3):
        lower = (sub < 4) if direction == 0 else ((y if direction == 1 else z) < 4)
        minus = jnp.where(first, choice(0, 2 * direction), choice(1, 2 * direction))
        plus = jnp.where(first, choice(0, 2 * direction + 1), choice(1, 2 * direction + 1))
        pick_ref[pl.ds(direction * ROWS, ROWS), :] = jnp.where(lower, plus, minus)
    live_ref[...] = jnp.where((sub & 1) < count_ref[0, 0], 1, 0)


def weno(p):
    e = [p[k + 1] - p[k] for k in range(5)]
    d = [e[k + 1] - e[k] for k in range(4)]
    q = [(13.0 / 3.0) * (dk * dk) + EPS4 for dk in d]
    t1, t2, t3 = 3.0 * e[1], 3.0 * e[2], 3.0 * e[3]
    middle = 0.5 * (p[2] + p[3])

    def side(qa, sa, qb, sb, qc, sc, da, db, dc):
        a, b, c = qa + sa * sa, qb + sb * sb, qc + sc * sc
        bc, ac, ab = b * c, a * c, a * b
        wa, wb, wc = bc * bc, 6.0 * (ac * ac), 3.0 * (ab * ab)
        top = wa * (3.0 * db - 2.0 * da) + wb * db + wc * dc
        return middle - top * reciprocal(6.0 * (wa + wb + wc))

    left = side(q[0], t1 - e[0], q[1], e[1] + e[2], q[2], e[3] - t2, d[0], d[1], d[2])
    right = side(q[3], e[4] - t3, q[2], e[2] + e[3], q[1], t2 - e[1], d[3], d[2], d[1])
    return left, right


def hllc(left, right):
    rl, ul, vl, wl, pl_ = jnp.maximum(left[0], FLOOR), left[1], left[2], left[3], jnp.maximum(left[4], FLOOR)
    rr, ur, vr, wr, pr = jnp.maximum(right[0], FLOOR), right[1], right[2], right[3], jnp.maximum(right[4], FLOOR)
    gl, gr = GAMMA * pl_, GAMMA * pr
    cl, cr = gl * lax.rsqrt(gl * rl), gr * lax.rsqrt(gr * rr)
    speed_left = jnp.minimum(ul - cl, ur - cr)
    speed_right = jnp.maximum(ul + cl, ur + cr)
    ml, mr = rl * (speed_left - ul), rr * (speed_right - ur)
    contact = (pr - pl_ + ml * ul - mr * ur) * reciprocal(ml - mr)
    from_left = (speed_left >= 0.0) | (contact >= 0.0)
    r = jnp.where(from_left, rl, rr)
    u = jnp.where(from_left, ul, ur)
    v = jnp.where(from_left, vl, vr)
    w = jnp.where(from_left, wl, wr)
    p = jnp.where(from_left, pl_, pr)
    s = jnp.where(from_left, speed_left, speed_right)
    m = jnp.where(from_left, ml, mr)
    star = (speed_left < 0.0) & ((contact >= 0.0) | (speed_right >= 0.0))
    energy = p * (1.0 / (GAMMA - 1.0)) + 0.5 * r * (u * u + v * v + w * w)
    inverse = reciprocal(s - contact)
    star_p = p + m * (contact - u)
    star_e = ((s - u) * energy - p * u + star_p * contact) * inverse
    density = jnp.where(star, m * inverse, r)
    normal = jnp.where(star, contact, u)
    pressure = jnp.where(star, star_p, p)
    energy = jnp.where(star, star_e, energy)
    mass = density * normal
    return [mass, mass * normal + pressure, mass * v, mass * w, normal * (energy + pressure)]


def rate(own, blocks, ghost_ref, pick_ref):
    sub, lane = positions()
    low = lane < 64
    y, z = (lane >> 3) & 7, lane & 7
    half = lane & 64
    x = (sub >> 1) * 2 + (lane >> 6)
    even_row = (sub & 1) == 0

    candidates = []
    for block in blocks:
        candidates.append(block)
        candidates.append([jnp.where(even_row, roll_rows(v, -1), roll_rows(v, 1)) for v in block])
    ghosts = []
    for direction in range(3):
        pick = pick_ref[pl.ds(direction * ROWS, ROWS), :]
        wanted = [pick == c + 1 for c in range(len(candidates))]
        chosen = []
        for f in range(FIELDS):
            value = ghost_ref[pl.ds(direction * 40 + f * ROWS, ROWS), :]
            for c, candidate in enumerate(candidates):
                value = jnp.where(wanted[c], candidate[f], value)
            chosen.append(value)
        ghosts.append(chosen)

    def shifts_x(value):
        other = roll_lanes(value, 64)
        minus2, plus2 = roll_rows(other, 2), roll_rows(other, -2)
        return {
            -3: jnp.where(low, roll_rows(other, 4), minus2),
            -2: roll_rows(value, 2),
            -1: jnp.where(low, minus2, other),
            0: value,
            1: jnp.where(low, other, plus2),
            2: roll_rows(value, -2),
        }

    def index_along(direction, steps):
        if direction == 1:
            return half | (((y + steps) & 7) << 3) | z
        return half | (y << 3) | ((z + steps) & 7)

    ninth_x = low & (sub < 2)
    is_y = (lane >= 64) & (lane < 80)
    part, inner = ((lane >> 3) & 1) << 6, lane & 7

    def ninth_index(layer):
        return jnp.where(is_y, part | (layer << 3) | inner, part | (inner << 3) | layer)

    mains = [[], [], []]
    ninths = []
    for f in range(FIELDS):
        own_x, ghost_x = shifts_x(own[f]), shifts_x(ghosts[0][f])
        cells = []
        for k in range(6):
            s = k - 3
            outside = (x + s < 0) | (x + s > 7)
            cells.append(jnp.where(outside, ghost_x[s], own_x[s]) if s else own[f])
        mains[0].append(cells)
        for direction in (1, 2):
            place = y if direction == 1 else z
            cells = []
            for k in range(6):
                s = k - 3
                if s == 0:
                    cells.append(own[f])
                    continue
                outside = (place >= 8 + s) if s < 0 else (place < s)
                merged = jnp.where(outside, ghosts[direction][f], own[f])
                cells.append(gather_lanes(merged, index_along(direction, s)))
            mains[direction].append(cells)
        cells = []
        for k in range(6):
            if k < 3:
                beside = gather_lanes(own[f], ninth_index(5 + k))
                value = own_x[k - 3]
            else:
                index = ninth_index(k - 3)
                beside = jnp.where(is_y, gather_lanes(ghosts[1][f], index), gather_lanes(ghosts[2][f], index))
                value = ghost_x[k - 3]
            cells.append(jnp.where(ninth_x, value, beside))
        ninths.append(cells)

    orders = ((0, 1, 2, 3, 4), (0, 2, 1, 3, 4), (0, 3, 1, 2, 4))
    fluxes = []
    for direction in range(3):
        states = [weno(mains[direction][f]) for f in orders[direction]]
        fluxes.append(hllc([st[0] for st in states], [st[1] for st in states]))
    states = [weno(ninths[f]) for f in range(FIELDS)]
    is_z = lane >= 80

    def turned(side):
        values = [st[side] for st in states]
        normal = jnp.where(is_y, values[2], jnp.where(is_z, values[3], values[1]))
        one = jnp.where(is_y | is_z, values[1], values[2])
        two = jnp.where(is_z, values[2], values[3])
        return [values[0], normal, one, two, values[4]]

    last = hllc(turned(0), turned(1))

    back_index = (
        None,
        64 + ((lane >> 6) << 3) + z,
        80 + ((lane >> 6) << 3) + y,
    )
    backs = ((0, 1, 2, 3, 4), (0, 2, 1, 3, 4), (0, 2, 3, 1, 4))
    total = [None] * FIELDS
    for direction in range(3):
        for place in range(FIELDS):
            flux = fluxes[direction][place]
            if direction == 0:
                merged = roll_lanes(jnp.where(x == 0, last[place], flux), 64)
                after = jnp.where(low, merged, roll_rows(merged, -2))
            else:
                end = (y if direction == 1 else z) == 7
                after = jnp.where(
                    end,
                    gather_lanes(last[place], back_index[direction]),
                    gather_lanes(flux, index_along(direction, 1)),
                )
            change = flux - after
            f = backs[direction].index(place)
            total[f] = change if total[f] is None else total[f] + change
    return total


def first_stage(own_ref, even_ref, odd_ref, ghost_ref, pick_ref, out_ref):
    own = load_primitives(own_ref)
    change = rate(own, [own, load_primitives(even_ref), load_primitives(odd_ref)], ghost_ref, pick_ref)
    for f in range(FIELDS):
        rows = pl.ds(f * ROWS, ROWS)
        out_ref[rows, :] = own_ref[rows, :] + TIME_STEP * change[f]


def second_stage(start_ref, own_ref, even_ref, odd_ref, ghost_ref, pick_ref, live_ref, out_ref):
    own = load_primitives(own_ref)
    change = rate(own, [own, load_primitives(even_ref), load_primitives(odd_ref)], ghost_ref, pick_ref)
    live = live_ref[...] != 0
    for f in range(FIELDS):
        rows = pl.ds(f * ROWS, ROWS)
        value = 0.5 * start_ref[rows, :] + 0.5 * (own_ref[rows, :] + TIME_STEP * change[f])
        out_ref[rows, :] = jnp.where(live, value, 0.0)


def vmem_spec():
    return pl.BlockSpec(memory_space=pltpu.VMEM)


def smem_spec():
    return pl.BlockSpec(memory_space=pltpu.SMEM)


def body(fine_state, coarse_old, box_count, fine_links, coarse_links):
    members = lax.axis_size("sub")
    tile_rows = FIELDS * ROWS
    start = to_tiles(fine_state)
    coarse = coarse_old.reshape(-1, LANES)

    even = exchange(start, even_partner)
    odd = exchange(start, odd_partner)
    group = [coarse] + [exchange(coarse, group_shift(r)) for r in range(1, members)]

    ghosts, picks, live = pl.pallas_call(
        prepare,
        out_shape=(
            pltpu.VMEM((3 * tile_rows, LANES), jnp.float32),
            pltpu.VMEM((3 * ROWS, LANES), jnp.int32),
            pltpu.VMEM((ROWS, LANES), jnp.int32),
        ),
        in_specs=[smem_spec()] * 3 + [vmem_spec()] * members,
        out_specs=(vmem_spec(),) * 3,
        scratch_shapes=[
            pltpu.VMEM((members * 16, ROWS, LANES), jnp.float32),
            pltpu.VMEM((3 * tile_rows, LANES), jnp.float32),
        ],
        name="prepare",
    )(
        fine_links.reshape(2, 6),
        coarse_links.reshape(2, 24),
        box_count,
        *[in_vmem(c) for c in group],
    )

    middle = pl.pallas_call(
        first_stage,
        out_shape=pltpu.VMEM((tile_rows, LANES), jnp.float32),
        in_specs=[vmem_spec()] * 5,
        out_specs=vmem_spec(),
        name="first_stage",
    )(in_vmem(start), in_vmem(even), in_vmem(odd), in_vmem(ghosts), in_vmem(picks))

    even = exchange(middle, even_partner)
    odd = exchange(middle, odd_partner)
    result = pl.pallas_call(
        second_stage,
        out_shape=jax.ShapeDtypeStruct((tile_rows, LANES), jnp.float32),
        in_specs=[vmem_spec()] * 7,
        out_specs=vmem_spec(),
        name="second_stage",
    )(
        in_vmem(start),
        in_vmem(middle),
        in_vmem(even),
        in_vmem(odd),
        in_vmem(ghosts),
        in_vmem(picks),
        in_vmem(live),
    )
    return from_tiles(result, fine_state.shape)


def solution(mesh):
    placed = (
        P("sfc", "sub", None, None, None),
        P("sfc", "sub", None, None),
        P("sfc", "sub"),
        P("sfc", "sub", None, None),
        P("sfc", "sub", None, None, None),
    )
    return jax.shard_map(
        body,
        mesh=mesh,
        in_specs=placed,
        out_specs=P("sfc", "sub", None, None, None),
        check_vma=False,
    )
```

time: 84.4 us -> 14.6 us (0.17)
  the two profiles are of different devices: /device:TPU:23 before, /device:TPU:0 now
where the time goes in v1:
time: 14.6 us; the launch traced here: 14.4 us
  starting transfers between devices  6.37 us (44%)
  Pallas kernels  2.92 us (20%)
  waiting for transfers between devices  2.9 us (20%)
  local copies, waits for them, and re-layouts  0.75 us (5%)
  other arithmetic  0.73 us (5%)
  between operations  0.72 us (5%)
    ppermute x5, starting transfers between devices, exchange(): return lax.ppermute(value, ('sfc', 'sub'), pairs)  6.37 us
    ppermute x5, waiting for transfers between devices, exchange(): return lax.ppermute(value, ('sfc', 'sub'), pairs)  2.9 us
    pallas_call x1, Pallas kernels, body(): pl.pallas_call(prepare, out_shape=(pltpu.VMEM((3 * tile_rows, LANES), jnp...  1.22 us
    pallas_call x1, Pallas kernels, body(): pl.pallas_call(second_stage, out_shape=jax.ShapeDtypeStruct((tile_rows, L...  1.15 us
    unnamed x1, other arithmetic  0.73 us
    reshape x1, local copies, waits for them, and re-layouts, body(): coarse_links.reshape(2, 24)  0.64 us
    pallas_call x1, Pallas kernels, body(): pl.pallas_call(first_stage, out_shape=pltpu.VMEM((tile_rows, LANES), jnp....  0.54 us
  transfers between devices with their start and end apart: 5, of which 2 were waited for; matrix products, arithmetic and copies ran while one was open for 10% of the time, Pallas kernels for 8%

profile of v1, /device:TPU:0, one launch (start us, length us, event | category | flops | bytes accessed | tf_op | source)
XLA Modules:
  0.0 14.4 jit_solution(12903283520466956428)
XLA Ops:
  0.0 3.0 %collective-permute-start.1 = (f32[40,128]{1,0:T(8,128)}, f32[40,128]{1,0:T(8,128)S(1)}, u32[]{:S(2)}, u32[]{:S(2)}) collective-permute-start(f32[40,128]{1,0:T(8,128)} %bitcast.11), channel_id=1, source_target_pairs={{0,1},{1,0},{2,4},{3,5},{4,2},{5,3},{6,8},{7,9},{8,6},{9,7},{10,12... | collective-permute-start | bytes 61448 | tf_op jit(solution)/shard_map/ppermute | solution.py:40
  3.0 0.1 collective-permute-start
  3.1 0.7 %reduce = f32[5,512]{1,0:T(8,128)S(1)} reduce(f32[1,1,5,512]{3,1,2,0:T(1,128)} %param.6, f32[]{:T(128)} %constant.5), dimensions={0,1}, to_apply=%param.6.reduce_sub_computation | reduce | bytes 20484 | tf_op args[1]
  3.8 0.0 copy-start.1
  3.8 1.6 %collective-permute-start.2 = (f32[20,128]{1,0:T(8,128)S(1)}, f32[20,128]{1,0:T(8,128)S(1)}, u32[]{:S(2)}, u32[]{:S(2)}) collective-permute-start(f32[20,128]{1,0:T(8,128)S(1)} %reshape.25.refs_0_), channel_id=1, source_target_pairs={{0,1},{1,0},{2,3},{3,2},{4,5},{5,4},{6,7},{7,6},{8,9},{9,8},{10,11... | collective-permute-start | bytes 30728 | tf_op jit(solution)/shard_map/ppermute | solution.py:40
  6.1 0.0 copy-done.1
  6.1 0.1 copy.10
  6.2 0.0 copy-start
  6.2 0.6 %reshape.24.corner_ref = s32[2,24]{1,0:T(2,128)} reshape(s32[1,1,2,6,4]{4,3,2,1,0:T(8,128)S(1)} %copy.10) | data formatting | bytes 384 | tf_op jit(solution)/shard_map/reshape | solution.py:400
  6.8 0.8 %collective-permute-done.2.refs_1_ = f32[20,128]{1,0:T(8,128)S(1)} collective-permute-done((f32[20,128]{1,0:T(8,128)S(1)}, f32[20,128]{1,0:T(8,128)S(1)}, u32[]{:S(2)}, u32[]{:S(2)}) %collective-permute-start.2) | collective-permute-done | bytes 10272 | tf_op jit(solution)/shard_map/ppermute | solution.py:40
  7.6 1.2 %prepare.1 = (f32[120,128]{1,0:T(8,128)S(1)}, s32[24,128]{1,0:T(8,128)S(1)}, s32[8,128]{1,0:T(8,128)S(1)}) custom-call(s32[2,6]{1,0:T(2,128)} %bitcast.15, s32[2,24]{1,0:T(2,128)} %reshape.24.corner_ref, s32[1,1]{1,0:T(1,128)S(6)} %copy.12.count_ref, f32[20,128]{1,0:T(8,128)S(1)} %reshape.25.refs_0_, f32[20,128]{1,0:T(8,128)S(1)} %collective-permute-done.2.refs_1_), custom_call_target="tpu_custom_call" | custom-call | tf_op jit(solution)/shard_map/prepare/pallas_call | solution.py:384
  8.8 0.0 collective-permute-done.1.odd_ref
  8.8 0.0 collective-permute-done.even_ref
  8.8 0.0 copy-done
  8.8 0.5 %first_stage.1.own_ref = f32[40,128]{1,0:T(8,128)S(1)} custom-call(f32[40,128]{1,0:T(8,128)S(1)} %bitcast.13, f32[40,128]{1,0:T(8,128)S(1)} %collective-permute-done.even_ref, f32[40,128]{1,0:T(8,128)S(1)} %collective-permute-done.1.odd_ref, f32[120,128]{1,0:T(8,128)S(1)} %get-tuple-element.8.ghost_ref, s32[24,128]{1,0:T(8,128)S(1)} %get-tuple-element.9.pick_ref), custom_call_target="tpu_custom_call" | custom-call | tf_op jit(solution)/shard_map/first_stage/pallas_call | solution.py:405
  9.4 1.6 %collective-permute-start.4 = (f32[40,128]{1,0:T(8,128)S(1)}, f32[40,128]{1,0:T(8,128)S(1)}, u32[]{:S(2)}, u32[]{:S(2)}) collective-permute-start(f32[40,128]{1,0:T(8,128)S(1)} %first_stage.1.own_ref), channel_id=1, source_target_pairs={{0,1},{1,0},{2,4},{3,5},{4,2},{5,3},{6,8},{7,9},{8,6},{9,7},{10,12... | collective-permute-start | bytes 61448 | tf_op jit(solution)/shard_map/ppermute | solution.py:40
  11.0 0.1 collective-permute-start.3
  11.1 2.1 %collective-permute-done.4.odd_ref = f32[40,128]{1,0:T(8,128)S(1)} collective-permute-done((f32[40,128]{1,0:T(8,128)S(1)}, f32[40,128]{1,0:T(8,128)S(1)}, u32[]{:S(2)}, u32[]{:S(2)}) %collective-permute-start.4) | collective-permute-done | bytes 20512 | tf_op jit(solution)/shard_map/ppermute | solution.py:40
  13.2 0.0 collective-permute-done.3.even_ref
  13.2 1.2 %second_stage.1 = f32[40,128]{1,0:T(8,128)} custom-call(f32[40,128]{1,0:T(8,128)S(1)} %bitcast.14, f32[40,128]{1,0:T(8,128)S(1)} %first_stage.1.own_ref, f32[40,128]{1,0:T(8,128)S(1)} %collective-permute-done.3.even_ref, f32[40,128]{1,0:T(8,128)S(1)} %collective-permute-done.4.odd_ref, f32[120,128]{1,0:T(8,128)S(1)} %get-tuple-element.8.ghost_ref, ...), custom_call_target="tpu_custom_call" | custom-call | tf_op jit(solution)/shard_map/second_stage/pallas_call | solution.py:415
  (1 shorter events, 0.0 us)
Async XLA Ops:
  0.0 8.8 %collective-permute-start.1 = (f32[40,128]{1,0:T(8,128)}, f32[40,128]{1,0:T(8,128)S(1)}, u32[]{:S(2)}, u32[]{:S(2)}) collective-permute-start(f32[40,128]{1,0:T(8,128)} %bitcast.11), channel_id=1, source_target_pairs={{0,1},{1,0},{2,4},{3,5},{4,2},{5,3},{6,8},{7,9},{8,6},{9,7},{10,12... | collective-permute-start | bytes 61448 | tf_op jit(solution)/shard_map/ppermute | solution.py:40
  3.0 5.8 %collective-permute-start = (f32[40,128]{1,0:T(8,128)}, f32[40,128]{1,0:T(8,128)S(1)}, u32[]{:S(2)}, u32[]{:S(2)}) collective-permute-start(f32[40,128]{1,0:T(8,128)} %bitcast.12), channel_id=1, source_target_pairs={{0,2},{1,3},{2,0},{3,1},{4,6},{5,7},{6,4},{7,5},{8,10},{9,11},{10,... | collective-permute-start | bytes 61448 | tf_op jit(solution)/shard_map/ppermute | solution.py:40
  3.8 2.3 %copy-start.1 = (s32[1,1,2,6,4]{3,4,2,1,0:T(4,128)S(1)}, s32[1,1,2,6,4]{3,4,2,1,0:T(4,128)}, u32[]{:S(2)}) copy-start(s32[1,1,2,6,4]{3,4,2,1,0:T(4,128)} %param.9) | copy-start | bytes 580
  3.8 3.8 %collective-permute-start.2 = (f32[20,128]{1,0:T(8,128)S(1)}, f32[20,128]{1,0:T(8,128)S(1)}, u32[]{:S(2)}, u32[]{:S(2)}) collective-permute-start(f32[20,128]{1,0:T(8,128)S(1)} %reshape.25.refs_0_), channel_id=1, source_target_pairs={{0,1},{1,0},{2,3},{3,2},{4,5},{5,4},{6,7},{7,6},{8,9},{9,8},{10,11... | collective-permute-start | bytes 30728 | tf_op jit(solution)/shard_map/ppermute | solution.py:40
  6.2 2.7 %copy-start = (f32[1,1,2,5,512]{4,2,3,1,0:T(2,128)S(1)}, f32[1,1,2,5,512]{4,2,3,1,0:T(2,128)}, u32[]{:S(2)}) copy-start(f32[1,1,2,5,512]{4,2,3,1,0:T(2,128)} %param.5) | copy-start | bytes 61444
  9.4 3.8 %collective-permute-start.4 = (f32[40,128]{1,0:T(8,128)S(1)}, f32[40,128]{1,0:T(8,128)S(1)}, u32[]{:S(2)}, u32[]{:S(2)}) collective-permute-start(f32[40,128]{1,0:T(8,128)S(1)} %first_stage.1.own_ref), channel_id=1, source_target_pairs={{0,1},{1,0},{2,4},{3,5},{4,2},{5,3},{6,8},{7,9},{8,6},{9,7},{10,12... | collective-permute-start | bytes 61448 | tf_op jit(solution)/shard_map/ppermute | solution.py:40
  11.0 2.3 %collective-permute-start.3 = (f32[40,128]{1,0:T(8,128)S(1)}, f32[40,128]{1,0:T(8,128)S(1)}, u32[]{:S(2)}, u32[]{:S(2)}) collective-permute-start(f32[40,128]{1,0:T(8,128)S(1)} %first_stage.1.own_ref), channel_id=1, source_target_pairs={{0,2},{1,3},{2,0},{3,1},{4,6},{5,7},{6,4},{7,5},{8,10},{9,11},{10,... | collective-permute-start | bytes 61448 | tf_op jit(solution)/shard_map/ppermute | solution.py:40

commit v2 on v1

--- a/solution.py
+++ b/solution.py
@@ -28,6 +28,10 @@
 
 def in_vmem(value):
     return pltpu.with_memory_space_constraint(value, pltpu.VMEM)
+
+
+def in_smem(value):
+    return pltpu.with_memory_space_constraint(value, pltpu.SMEM)
 
 
 def exchange(value, partner):
@@ -100,28 +104,64 @@
     return jnp.maximum(jnp.minimum(p, q), 0.0) + jnp.minimum(jnp.maximum(p, q), 0.0)
 
 
-def prepare(links_ref, corner_ref, count_ref, *refs):
-    coarse_refs, (ghost_ref, pick_ref, live_ref, table, lines) = refs[:-5], refs[-5:]
-    members = len(coarse_refs)
+def slopes(table, base, low):
+    cells = [table[base + j] for j in range(4)]
+    halves = [roll_lanes(c, 64) for c in cells]
+    for j in range(4):
+        u = cells[j]
+        up = jnp.where(low, halves[j], halves[min(j + 1, 3)])
+        down = jnp.where(low, halves[max(j - 1, 0)], halves[j])
+        table[base + 4 + j] = 0.25 * minmod(up - u, u - down)
+        table[base + 8 + j] = 0.25 * minmod(roll_lanes(u, -8) - u, u - roll_lanes(u, 8))
+        table[base + 12 + j] = 0.25 * minmod(roll_lanes(u, -1) - u, u - roll_lanes(u, 1))
+
+
+def spread_fields(table, base, coarse_ref):
+    for j in range(4):
+        for f in range(FIELDS):
+            table[base + j, f : f + 1, :] = coarse_ref[f * 4 + j]
+
+
+def read_links(links_in, corner_in, coarse_in, start_in, pick_ref, table, corner_ref, own_ref, links_ref, coarse_ref, sems):
+    copies = (links_in, links_ref), (corner_in, corner_ref), (coarse_in, coarse_ref), (start_in, own_ref)
+    fetches = [pltpu.make_async_copy(src, dst, sems.at[i]) for i, (src, dst) in enumerate(copies)]
+    for fetch in fetches:
+        fetch.start()
+    sub, lane = positions()
+    y, z = (lane >> 3) & 7, lane & 7
+    odd_segment = lax.axis_index("sfc") & 1
+    for fetch in fetches:
+        fetch.wait()
+    spread_fields(table, 0, coarse_ref)
+    slopes(table, 0, lane < 64)
+
+    def choice(slot, face):
+        link = links_ref[slot, face]
+        offset = link >> 1
+        below = jnp.where(offset == 0, 1, 0)
+        block = jnp.where(offset == 1, 0, jnp.where(below == odd_segment, 1, 2))
+        swapped = (link & 1) ^ slot
+        return jnp.where(link < 0, 0, 1 + block * 2 + swapped)
+
+    first = (sub & 1) == 0
+    for direction in range(3):
+        lower = (sub < 4) if direction == 0 else ((y if direction == 1 else z) < 4)
+        minus = jnp.where(first, choice(0, 2 * direction), choice(1, 2 * direction))
+        plus = jnp.where(first, choice(0, 2 * direction + 1), choice(1, 2 * direction + 1))
+        pick_ref[pl.ds(direction * ROWS, ROWS), :] = jnp.where(lower, plus, minus)
+
+
+def interpolate(corner_ref, own_table, *refs):
+    coarse_refs, (ghost_ref, table, lines) = refs[:-3], refs[-3:]
+    members = len(coarse_refs) + 1
     sub, lane = positions()
     low = lane < 64
     y, z = (lane >> 3) & 7, lane & 7
     me = lax.axis_index("sub")
-    odd_segment = lax.axis_index("sfc") & 1
-
-    for m in range(members):
-        for j in range(4):
-            table[m * 16 + j, 0:FIELDS, :] = coarse_refs[m][pl.ds(j, FIELDS, stride=4), :]
-    for m in range(members):
-        cells = [table[m * 16 + j] for j in range(4)]
-        halves = [roll_lanes(c, 64) for c in cells]
-        for j in range(4):
-            u = cells[j]
-            up = jnp.where(low, halves[j], halves[min(j + 1, 3)])
-            down = jnp.where(low, halves[max(j - 1, 0)], halves[j])
-            table[m * 16 + 4 + j] = 0.25 * minmod(up - u, u - down)
-            table[m * 16 + 8 + j] = 0.25 * minmod(roll_lanes(u, -8) - u, u - roll_lanes(u, 8))
-            table[m * 16 + 12 + j] = 0.25 * minmod(roll_lanes(u, -1) - u, u - roll_lanes(u, 1))
+    table[0:16] = own_table[...]
+    for m, coarse_ref in enumerate(coarse_refs):
+        spread_fields(table, (m + 1) * 16, coarse_ref)
+        slopes(table, (m + 1) * 16, low)
 
     sign_x = jnp.where(low, -1.0, 1.0)
     sign_y = jnp.where((y & 1) == 0, -1.0, 1.0)
@@ -130,8 +170,8 @@
 
     def children(slot, face, j):
         direction, minus = face // 2, face % 2 == 0
-        start = [corner_ref[slot, face * 4 + 1 + a] + (-1 if minus and a == direction else 1) for a in range(3)]
-        owner = me - corner_ref[slot, face * 4]
+        start = [corner_ref[slot, 1 + a, face] + (-1 if minus and a == direction else 1) for a in range(3)]
+        owner = me - corner_ref[slot, 0, face]
         owner = jnp.where(owner < 0, owner + members, owner)
         along = start[0] + j
         index = (spread + ((along & 1) * 64 + start[1] * 8 + start[2])) & (LANES - 1)
@@ -153,22 +193,6 @@
         made = load_primitives(lines, direction * 40)
         for f in range(FIELDS):
             ghost_ref[pl.ds(direction * 40 + f * ROWS, ROWS), :] = made[f]
-
-    def choice(slot, face):
-        link = links_ref[slot, face]
-        offset = link >> 1
-        below = jnp.where(offset == 0, 1, 0)
-        block = jnp.where(offset == 1, 0, jnp.where(below == odd_segment, 1, 2))
-        swapped = (link & 1) ^ slot
-        return jnp.where(link < 0, 0, 1 + block * 2 + swapped)
-
-    first = (sub & 1) == 0
-    for direction in range(3):
-        lower = (sub < 4) if direction == 0 else ((y if direction == 1 else z) < 4)
-        minus = jnp.where(first, choice(0, 2 * direction), choice(1, 2 * direction))
-        plus = jnp.where(first, choice(0, 2 * direction + 1), choice(1, 2 * direction + 1))
-        pick_ref[pl.ds(direction * ROWS, ROWS), :] = jnp.where(lower, plus, minus)
-    live_ref[...] = jnp.where((sub & 1) < count_ref[0, 0], 1, 0)
 
 
 def weno(p):
@@ -345,7 +369,7 @@
     return total
 
 
-def first_stage(own_ref, even_ref, odd_ref, ghost_ref, pick_ref, out_ref):
+def first_stage(own_ref, odd_ref, even_ref, ghost_ref, pick_ref, out_ref):
     own = load_primitives(own_ref)
     change = rate(own, [own, load_primitives(even_ref), load_primitives(odd_ref)], ghost_ref, pick_ref)
     for f in range(FIELDS):
@@ -353,10 +377,11 @@
         out_ref[rows, :] = own_ref[rows, :] + TIME_STEP * change[f]
 
 
-def second_stage(start_ref, own_ref, even_ref, odd_ref, ghost_ref, pick_ref, live_ref, out_ref):
+def second_stage(start_ref, own_ref, odd_ref, even_ref, ghost_ref, pick_ref, count_ref, out_ref):
     own = load_primitives(own_ref)
     change = rate(own, [own, load_primitives(even_ref), load_primitives(odd_ref)], ghost_ref, pick_ref)
-    live = live_ref[...] != 0
+    sub, _ = positions()
+    live = (sub & 1) < count_ref[0, 0]
     for f in range(FIELDS):
         rows = pl.ds(f * ROWS, ROWS)
         value = 0.5 * start_ref[rows, :] + 0.5 * (own_ref[rows, :] + TIME_STEP * change[f])
@@ -371,36 +396,55 @@
     return pl.BlockSpec(memory_space=pltpu.SMEM)
 
 
+def hbm_spec():
+    return pl.BlockSpec(memory_space=pltpu.HBM)
+
+
 def body(fine_state, coarse_old, box_count, fine_links, coarse_links):
     members = lax.axis_size("sub")
     tile_rows = FIELDS * ROWS
     start = to_tiles(fine_state)
-    coarse = coarse_old.reshape(-1, LANES)
-
+    coarse = coarse_old.transpose(0, 2, 1, 3).reshape(FIELDS, 1, -1, LANES).transpose(0, 2, 1, 3)
+    coarse = coarse.reshape(-1, 1, LANES)
+
+    odd = exchange(start, odd_partner)
+    group = [exchange(coarse, group_shift(r)) for r in range(1, members)]
+
+    picks, table, corners, own = pl.pallas_call(
+        read_links,
+        out_shape=(
+            pltpu.VMEM((3 * ROWS, LANES), jnp.int32),
+            pltpu.VMEM((16, ROWS, LANES), jnp.float32),
+            pltpu.SMEM((2, 4, 6), jnp.int32),
+            pltpu.VMEM((tile_rows, LANES), jnp.float32),
+        ),
+        in_specs=[hbm_spec()] * 4,
+        out_specs=(vmem_spec(), vmem_spec(), smem_spec(), vmem_spec()),
+        scratch_shapes=[
+            pltpu.SMEM((2, 6), jnp.int32),
+            pltpu.VMEM((FIELDS * 4, 1, LANES), jnp.float32),
+            pltpu.SemaphoreType.DMA((4,)),
+        ],
+        name="read_links",
+    )(
+        fine_links.reshape(2, 6),
+        coarse_links.transpose(0, 1, 2, 4, 3).reshape(2, 4, 6),
+        coarse,
+        start,
+    )
     even = exchange(start, even_partner)
-    odd = exchange(start, odd_partner)
-    group = [coarse] + [exchange(coarse, group_shift(r)) for r in range(1, members)]
-
-    ghosts, picks, live = pl.pallas_call(
-        prepare,
-        out_shape=(
-            pltpu.VMEM((3 * tile_rows, LANES), jnp.float32),
-            pltpu.VMEM((3 * ROWS, LANES), jnp.int32),
-            pltpu.VMEM((ROWS, LANES), jnp.int32),
-        ),
-        in_specs=[smem_spec()] * 3 + [vmem_spec()] * members,
-        out_specs=(vmem_spec(),) * 3,
+    ghosts = pl.pallas_call(
+        interpolate,
+        out_shape=pltpu.VMEM((3 * tile_rows, LANES), jnp.float32),
+        in_specs=[smem_spec()] + [vmem_spec()] * members,
+        out_specs=vmem_spec(),
         scratch_shapes=[
             pltpu.VMEM((members * 16, ROWS, LANES), jnp.float32),
             pltpu.VMEM((3 * tile_rows, LANES), jnp.float32),
         ],
-        name="prepare",
-    )(
-        fine_links.reshape(2, 6),
-        coarse_links.reshape(2, 24),
-        box_count,
-        *[in_vmem(c) for c in group],
-    )
+        name="interpolate",
+        cost_estimate=pl.CostEstimate(flops=10000000000, bytes_accessed=10000000000, transcendentals=0),
+    )(in_smem(corners), in_vmem(table), *[in_vmem(c) for c in group])
 
     middle = pl.pallas_call(
         first_stage,
@@ -408,24 +452,24 @@
         in_specs=[vmem_spec()] * 5,
         out_specs=vmem_spec(),
         name="first_stage",
-    )(in_vmem(start), in_vmem(even), in_vmem(odd), in_vmem(ghosts), in_vmem(picks))
+    )(in_vmem(own), in_vmem(odd), in_vmem(even), in_vmem(ghosts), in_vmem(picks))
 
     even = exchange(middle, even_partner)
     odd = exchange(middle, odd_partner)
     result = pl.pallas_call(
         second_stage,
         out_shape=jax.ShapeDtypeStruct((tile_rows, LANES), jnp.float32),
-        in_specs=[vmem_spec()] * 7,
+        in_specs=[vmem_spec()] * 6 + [smem_spec()],
         out_specs=vmem_spec(),
         name="second_stage",
     )(
-        in_vmem(start),
+        in_vmem(own),
         in_vmem(middle),
+        in_vmem(odd),
         in_vmem(even),
-        in_vmem(odd),
         in_vmem(ghosts),
         in_vmem(picks),
-        in_vmem(live),
+        box_count,
     )
     return from_tiles(result, fine_state.shape)
 

time: 14.6 us -> 12.7 us (0.87)
  local copies, waits for them, and re-layouts: 0.75 us -> 0 us
  other arithmetic: 0.73 us -> 0 us
  starting transfers between devices: 6.37 us -> 5.67 us
  Pallas kernels: 2.92 us -> 3.14 us
    unnamed x1 -> x0, other arithmetic: 0.73 us -> none
    ppermute x5, starting transfers between devices: 6.37 us -> 5.67 us  [exchange(): return lax.ppermute(value, ('sfc', 'sub'), pairs)]
    reshape x2 -> x0, local copies, waits for them, and re-layouts: 0.65 us -> none  [the longest x1 0.64 us: body(): coarse_links.reshape(2, 24)]
    pallas_call x1 -> x2, Pallas kernels: 1.22 us -> 1.44 us  [the longest x1 0.92 us: body(): pl.pallas_call(read_links, out_shape=(pltpu.VMEM((3 * ROWS, LANES), jnp.i...]
  transfers between devices with their start and end apart: 5 -> 5, of which waited for: 2 -> 2; matrix products, arithmetic and copies ran while one was open for 10% -> 0% of each run, Pallas kernels for 8% -> 12%
where the time goes in v2:
time: 12.7 us; the launch traced here: 12.5 us
  starting transfers between devices  5.67 us (45%)
  Pallas kernels  3.14 us (25%)
  waiting for transfers between devices  3.03 us (24%)
  between operations  0.68 us (5%)
    ppermute x5, starting transfers between devices, exchange(): return lax.ppermute(value, ('sfc', 'sub'), pairs)  5.67 us
    ppermute x5, waiting for transfers between devices, exchange(): return lax.ppermute(value, ('sfc', 'sub'), pairs)  3.03 us
    pallas_call x1, Pallas kernels, body(): pl.pallas_call(second_stage, out_shape=jax.ShapeDtypeStruct((tile_rows, L...  1.15 us
    pallas_call x1, Pallas kernels, body(): pl.pallas_call(read_links, out_shape=(pltpu.VMEM((3 * ROWS, LANES), jnp.i...  0.92 us
    pallas_call x1, Pallas kernels, body(): pl.pallas_call(first_stage, out_shape=pltpu.VMEM((tile_rows, LANES), jnp....  0.54 us
    pallas_call x1, Pallas kernels, body(): pl.pallas_call(interpolate, out_shape=pltpu.VMEM((3 * tile_rows, LANES),...  0.52 us
  transfers between devices with their start and end apart: 5, of which 2 were waited for; matrix products, arithmetic and copies ran while one was open for 0% of the time, Pallas kernels for 12%

profile of v2, /device:TPU:0, one launch (start us, length us, event | category | flops | bytes accessed | tf_op | source)
XLA Modules:
  0.0 12.5 jit_solution(1511523453994980379)
XLA Ops:
  0.0 3.0 %collective-permute-start.2 = (f32[20,1,128]{2,1,0:T(1,128)}, f32[20,1,128]{2,1,0:T(1,128)S(1)}, u32[]{:S(2)}, u32[]{:S(2)}) collective-permute-start(f32[20,1,128]{2,1,0:T(1,128)} %bitcast.18), channel_id=1, source_target_pairs={{0,1},{1,0},{2,3},{3,2},{4,5},{5,4},{6,7},{7,6},{8,9},{9,8},{10,11... | collective-permute-start | bytes 30728 | tf_op jit(solution)/shard_map/ppermute | solution.py:44
  3.0 0.0 collective-permute-start
  3.0 1.6 %collective-permute-start.1 = (f32[40,128]{1,0:T(8,128)}, f32[40,128]{1,0:T(8,128)S(1)}, u32[]{:S(2)}, u32[]{:S(2)}) collective-permute-start(f32[40,128]{1,0:T(8,128)} %bitcast.16), channel_id=1, source_target_pairs={{0,2},{1,3},{2,0},{3,1},{4,6},{5,7},{6,4},{7,5},{8,10},{9,11},{10,... | collective-permute-start | bytes 61448 | tf_op jit(solution)/shard_map/ppermute | solution.py:44
  4.6 0.9 %read_links.1 = (s32[24,128]{1,0:T(8,128)S(1)}, f32[16,8,128]{2,1,0:T(8,128)S(1)}, s32[2,4,6]{2,1,0:T(4,128)S(4)}, f32[40,128]{1,0:T(8,128)S(1)}) custom-call(s32[2,6]{1,0:T(2,128)} %bitcast.21, s32[2,4,6]{2,1,0:T(4,128)} %bitcast.20, f32[20,1,128]{2,1,0:T(1,128)} %bitcast.19, f32[40,128]{1,0:T(8,128)} %bitcast.17), custom_call_target="tpu_custom_call" | custom-call | tf_op jit(solution)/shard_map/read_links/pallas_call | solution.py:413
  5.5 0.0 collective-permute-done.2.refs_0_
  5.5 0.5 %interpolate.1.ghost_ref = f32[120,128]{1,0:T(8,128)S(1)} custom-call(s32[2,4,6]{2,1,0:T(4,128)S(4)} %get-tuple-element.10.corner_ref, f32[16,8,128]{2,1,0:T(8,128)S(1)} %get-tuple-element.11.own_table, f32[20,1,128]{2,1,0:T(1,128)S(1)} %collective-permute-done.2.refs_0_), custom_call_target="tpu_custom_call" | custom-call | flops 10000000000 | bytes 10000000000 | tf_op jit(solution)/shard_map/interpolate/pallas_call | solution.py:436
  6.0 0.9 %collective-permute-done.odd_ref = f32[40,128]{1,0:T(8,128)S(1)} collective-permute-done((f32[40,128]{1,0:T(8,128)}, f32[40,128]{1,0:T(8,128)S(1)}, u32[]{:S(2)}, u32[]{:S(2)}) %collective-permute-start) | collective-permute-done | bytes 20512 | tf_op jit(solution)/shard_map/ppermute | solution.py:44
  7.0 0.0 collective-permute-done.1.even_ref
  7.0 0.5 %first_stage.1.own_ref = f32[40,128]{1,0:T(8,128)S(1)} custom-call(f32[40,128]{1,0:T(8,128)S(1)} %get-tuple-element.9.own_ref.start_ref, f32[40,128]{1,0:T(8,128)S(1)} %collective-permute-done.odd_ref, f32[40,128]{1,0:T(8,128)S(1)} %collective-permute-done.1.even_ref, f32[120,128]{1,0:T(8,128)S(1)} %interpolate.1.ghost_ref, ...), custom_call_target="tpu_custom_call" | custom-call | tf_op jit(solution)/shard_map/first_stage/pallas_call | solution.py:449
  7.5 0.5 %collective-permute-start.3 = (f32[40,128]{1,0:T(8,128)S(1)}, f32[40,128]{1,0:T(8,128)S(1)}, u32[]{:S(2)}, u32[]{:S(2)}) collective-permute-start(f32[40,128]{1,0:T(8,128)S(1)} %first_stage.1.own_ref), channel_id=1, source_target_pairs={{0,1},{1,0},{2,4},{3,5},{4,2},{5,3},{6,8},{7,9},{8,6},{9,7},{10,12... | collective-permute-start | bytes 61448 | tf_op jit(solution)/shard_map/ppermute | solution.py:44
  8.0 0.6 %collective-permute-start.4 = (f32[40,128]{1,0:T(8,128)S(1)}, f32[40,128]{1,0:T(8,128)S(1)}, u32[]{:S(2)}, u32[]{:S(2)}) collective-permute-start(f32[40,128]{1,0:T(8,128)S(1)} %first_stage.1.own_ref), channel_id=1, source_target_pairs={{0,2},{1,3},{2,0},{3,1},{4,6},{5,7},{6,4},{7,5},{8,10},{9,11},{10,... | collective-permute-start | bytes 61448 | tf_op jit(solution)/shard_map/ppermute | solution.py:44
  9.3 2.1 %collective-permute-done.3.odd_ref = f32[40,128]{1,0:T(8,128)S(1)} collective-permute-done((f32[40,128]{1,0:T(8,128)S(1)}, f32[40,128]{1,0:T(8,128)S(1)}, u32[]{:S(2)}, u32[]{:S(2)}) %collective-permute-start.3) | collective-permute-done | bytes 20512 | tf_op jit(solution)/shard_map/ppermute | solution.py:44
  11.4 0.0 collective-permute-done.4.even_ref
  11.4 1.2 %second_stage.1 = f32[40,128]{1,0:T(8,128)} custom-call(f32[40,128]{1,0:T(8,128)S(1)} %get-tuple-element.9.own_ref.start_ref, f32[40,128]{1,0:T(8,128)S(1)} %first_stage.1.own_ref, f32[40,128]{1,0:T(8,128)S(1)} %collective-permute-done.3.odd_ref, f32[40,128]{1,0:T(8,128)S(1)} %collective-permute-done.4.even_ref, f32[120,128]{1,0:T(8,128)S(1)} %interpolate.1.ghost_ref, ...), custom_call_target="tpu_custom_call" | custom-call | tf_op jit(solution)/shard_map/second_stage/pallas_call | solution.py:459
Async XLA Ops:
  0.0 5.5 %collective-permute-start.2 = (f32[20,1,128]{2,1,0:T(1,128)}, f32[20,1,128]{2,1,0:T(1,128)S(1)}, u32[]{:S(2)}, u32[]{:S(2)}) collective-permute-start(f32[20,1,128]{2,1,0:T(1,128)} %bitcast.18), channel_id=1, source_target_pairs={{0,1},{1,0},{2,3},{3,2},{4,5},{5,4},{6,7},{7,6},{8,9},{9,8},{10,11... | collective-permute-start | bytes 30728 | tf_op jit(solution)/shard_map/ppermute | solution.py:44
  3.0 4.0 %collective-permute-start = (f32[40,128]{1,0:T(8,128)}, f32[40,128]{1,0:T(8,128)S(1)}, u32[]{:S(2)}, u32[]{:S(2)}) collective-permute-start(f32[40,128]{1,0:T(8,128)} %bitcast.15), channel_id=1, source_target_pairs={{0,1},{1,0},{2,4},{3,5},{4,2},{5,3},{6,8},{7,9},{8,6},{9,7},{10,12... | collective-permute-start | bytes 61448 | tf_op jit(solution)/shard_map/ppermute | solution.py:44
  3.0 4.0 %collective-permute-start.1 = (f32[40,128]{1,0:T(8,128)}, f32[40,128]{1,0:T(8,128)S(1)}, u32[]{:S(2)}, u32[]{:S(2)}) collective-permute-start(f32[40,128]{1,0:T(8,128)} %bitcast.16), channel_id=1, source_target_pairs={{0,2},{1,3},{2,0},{3,1},{4,6},{5,7},{6,4},{7,5},{8,10},{9,11},{10,... | collective-permute-start | bytes 61448 | tf_op jit(solution)/shard_map/ppermute | solution.py:44
  7.5 3.8 %collective-permute-start.3 = (f32[40,128]{1,0:T(8,128)S(1)}, f32[40,128]{1,0:T(8,128)S(1)}, u32[]{:S(2)}, u32[]{:S(2)}) collective-permute-start(f32[40,128]{1,0:T(8,128)S(1)} %first_stage.1.own_ref), channel_id=1, source_target_pairs={{0,1},{1,0},{2,4},{3,5},{4,2},{5,3},{6,8},{7,9},{8,6},{9,7},{10,12... | collective-permute-start | bytes 61448 | tf_op jit(solution)/shard_map/ppermute | solution.py:44
  8.0 3.4 %collective-permute-start.4 = (f32[40,128]{1,0:T(8,128)S(1)}, f32[40,128]{1,0:T(8,128)S(1)}, u32[]{:S(2)}, u32[]{:S(2)}) collective-permute-start(f32[40,128]{1,0:T(8,128)S(1)} %first_stage.1.own_ref), channel_id=1, source_target_pairs={{0,2},{1,3},{2,0},{3,1},{4,6},{5,7},{6,4},{7,5},{8,10},{9,11},{10,... | collective-permute-start | bytes 61448 | tf_op jit(solution)/shard_map/ppermute | solution.py:44

commit v3 on v2

--- a/solution.py
+++ b/solution.py
@@ -12,6 +12,8 @@
 FLOOR = 0.1
 EPS4 = 4e-06
 TIME_STEP = 0.1
+PARTS = ((0, 32), (32, 8))
+HERE, EVEN, ODD = 1, 3, 5
 
 
 def to_tiles(boxes):
@@ -74,17 +76,23 @@
     return jnp.take_along_axis(value, index, axis=1, mode="promise_in_bounds")
 
 
+def gather_rows(value, index):
+    return jnp.take_along_axis(value, index, axis=0, mode="promise_in_bounds")
+
+
 def roll_lanes(value, steps):
     return pltpu.roll(value, steps % LANES, 1)
 
 
 def roll_rows(value, steps):
-    return pltpu.roll(value, steps % ROWS, 0)
+    if steps % ROWS == 0:
+        return value
+    sub, _ = positions()
+    return gather_rows(value, (sub - steps) & 7)
 
 
 def reciprocal(value):
-    guess = pl.reciprocal(value, approx=True)
-    return guess * (2.0 - value * guess)
+    return 1.0 / value
 
 
 def primitives(mass, mom_x, mom_y, mom_z, energy):
@@ -94,6 +102,20 @@
     kinetic = 0.5 * density * (vel_x * vel_x + vel_y * vel_y + vel_z * vel_z)
     pressure = jnp.maximum((GAMMA - 1.0) * (energy - kinetic), FLOOR)
     return [density, vel_x, vel_y, vel_z, pressure]
+
+
+def load_parts(refs):
+    fields = []
+    for ref, (_, rows) in zip(refs, PARTS):
+        fields += [ref[pl.ds(at, ROWS), :] for at in range(0, rows, ROWS)]
+    return fields
+
+
+def store_parts(refs, fields):
+    fields = list(fields)
+    for ref, (_, rows) in zip(refs, PARTS):
+        for at in range(0, rows, ROWS):
+            ref[pl.ds(at, ROWS), :] = fields.pop(0)
 
 
 def load_primitives(ref, base=0):
@@ -122,8 +144,11 @@
             table[base + j, f : f + 1, :] = coarse_ref[f * 4 + j]
 
 
-def read_links(links_in, corner_in, coarse_in, start_in, pick_ref, table, corner_ref, own_ref, links_ref, coarse_ref, sems):
-    copies = (links_in, links_ref), (corner_in, corner_ref), (coarse_in, coarse_ref), (start_in, own_ref)
+def read_links(links_in, corner_in, coarse_in, start_in, pick_ref, table, corner_ref, code_ref, *refs):
+    own_refs, (links_ref, coarse_ref, sems) = refs[:-3], refs[-3:]
+    copies = [(links_in, links_ref), (corner_in, corner_ref), (coarse_in, coarse_ref)]
+    for own_ref, (first, rows) in zip(own_refs, PARTS):
+        copies.append((start_in.at[pl.ds(first, rows), :], own_ref))
     fetches = [pltpu.make_async_copy(src, dst, sems.at[i]) for i, (src, dst) in enumerate(copies)]
     for fetch in fetches:
         fetch.start()
@@ -143,11 +168,17 @@
         swapped = (link & 1) ^ slot
         return jnp.where(link < 0, 0, 1 + block * 2 + swapped)
 
+    codes = [[choice(slot, face) for face in range(6)] for slot in range(2)]
+    waits = jnp.int32(0)
+    for code in codes[0] + codes[1]:
+        waits = jnp.maximum(waits, jnp.where(code >= ODD, 1, 0))
+    code_ref[0, 0] = waits
+
     first = (sub & 1) == 0
     for direction in range(3):
         lower = (sub < 4) if direction == 0 else ((y if direction == 1 else z) < 4)
-        minus = jnp.where(first, choice(0, 2 * direction), choice(1, 2 * direction))
-        plus = jnp.where(first, choice(0, 2 * direction + 1), choice(1, 2 * direction + 1))
+        minus = jnp.where(first, codes[0][2 * direction], codes[1][2 * direction])
+        plus = jnp.where(first, codes[0][2 * direction + 1], codes[1][2 * direction + 1])
         pick_ref[pl.ds(direction * ROWS, ROWS), :] = jnp.where(lower, plus, minus)
 
 
@@ -195,23 +226,22 @@
             ghost_ref[pl.ds(direction * 40 + f * ROWS, ROWS), :] = made[f]
 
 
-def weno(p):
-    e = [p[k + 1] - p[k] for k in range(5)]
-    d = [e[k + 1] - e[k] for k in range(4)]
-    q = [(13.0 / 3.0) * (dk * dk) + EPS4 for dk in d]
-    t1, t2, t3 = 3.0 * e[1], 3.0 * e[2], 3.0 * e[3]
-    middle = 0.5 * (p[2] + p[3])
-
-    def side(qa, sa, qb, sb, qc, sc, da, db, dc):
-        a, b, c = qa + sa * sa, qb + sb * sb, qc + sc * sc
-        bc, ac, ab = b * c, a * c, a * b
-        wa, wb, wc = bc * bc, 6.0 * (ac * ac), 3.0 * (ab * ab)
-        top = wa * (3.0 * db - 2.0 * da) + wb * db + wc * dc
-        return middle - top * reciprocal(6.0 * (wa + wb + wc))
-
-    left = side(q[0], t1 - e[0], q[1], e[1] + e[2], q[2], e[3] - t2, d[0], d[1], d[2])
-    right = side(q[3], e[4] - t3, q[2], e[2] + e[3], q[1], t2 - e[1], d[3], d[2], d[1])
-    return left, right
+def weno(cells):
+    centre = cells[2]
+    e0, e1, e2, e3 = [cells[k + 1] - cells[k] for k in range(4)]
+    d1, d2, d3 = e1 - e0, e2 - e1, e3 - e2
+    below, above, across = 3.0 * e1 - e0, 3.0 * e2 - e3, e1 + e2
+    a = ((13.0 / 3.0) * (d1 * d1) + EPS4) + below * below
+    b = ((13.0 / 3.0) * (d2 * d2) + EPS4) + across * across
+    c = ((13.0 / 3.0) * (d3 * d3) + EPS4) + above * above
+    bc, ac, ab = b * c, a * c, a * b
+    bc, ac, ab = bc * bc, 6.0 * (ac * ac), ab * ab
+    bc3, ab3 = 3.0 * bc, 3.0 * ab
+    up = bc * (2.0 * below - e1) + ac * (across + e2) + ab3 * (above + e2)
+    down = ab * (2.0 * above - e2) + ac * (across + e1) + bc3 * (below + e1)
+    upper = centre + up * ((1.0 / 6.0) * reciprocal(bc + ac + ab3))
+    lower = centre - down * ((1.0 / 6.0) * reciprocal(ab + ac + bc3))
+    return upper, lower
 
 
 def hllc(left, right):
@@ -244,148 +274,190 @@
     return [mass, mass * normal + pressure, mass * v, mass * w, normal * (energy + pressure)]
 
 
-def rate(own, blocks, ghost_ref, pick_ref):
-    sub, lane = positions()
-    low = lane < 64
-    y, z = (lane >> 3) & 7, lane & 7
-    half = lane & 64
-    x = (sub >> 1) * 2 + (lane >> 6)
-    even_row = (sub & 1) == 0
-
-    candidates = []
-    for block in blocks:
-        candidates.append(block)
-        candidates.append([jnp.where(even_row, roll_rows(v, -1), roll_rows(v, 1)) for v in block])
-    ghosts = []
+class Turns:
+    def __init__(self):
+        sub, lane = positions()
+        self.sub = sub
+        y, z = (lane >> 3) & 7, lane & 7
+        high = lane >> 6
+        self.steps = (
+            (sub ^ high, lane ^ ((sub & 1) << 6), sub ^ high),
+            ((sub - y) & 7, (lane & 71) | (((sub - y) & 7) << 3), (sub + y) & 7),
+            ((sub - z) & 7, (lane & 120) | ((sub - z) & 7), (sub + z) & 7),
+        )
+
+    def __call__(self, direction, value):
+        before, across, after = self.steps[direction]
+        return gather_rows(gather_lanes(gather_rows(value, before), across), after)
+
+
+def swapped_slots(value, sub):
+    return gather_rows(value, sub ^ 1)
+
+
+OWN, GHOST, READY = 0, 15, 30
+
+
+def make_ready(ghost_ref, pick_ref, *refs):
+    own_refs, ready_ref = refs[:-1], refs[-1]
+    turn = Turns()
+    own = primitives(*load_parts(own_refs))
+    candidates = [own, [swapped_slots(v, turn.sub) for v in own]]
     for direction in range(3):
         pick = pick_ref[pl.ds(direction * ROWS, ROWS), :]
         wanted = [pick == c + 1 for c in range(len(candidates))]
-        chosen = []
+        remote = pick > len(candidates)
         for f in range(FIELDS):
-            value = ghost_ref[pl.ds(direction * 40 + f * ROWS, ROWS), :]
+            value = ghost_ref[pl.ds((direction * FIELDS + f) * ROWS, ROWS), :]
             for c, candidate in enumerate(candidates):
                 value = jnp.where(wanted[c], candidate[f], value)
-            chosen.append(value)
-        ghosts.append(chosen)
-
-    def shifts_x(value):
-        other = roll_lanes(value, 64)
-        minus2, plus2 = roll_rows(other, 2), roll_rows(other, -2)
-        return {
-            -3: jnp.where(low, roll_rows(other, 4), minus2),
-            -2: roll_rows(value, 2),
-            -1: jnp.where(low, minus2, other),
-            0: value,
-            1: jnp.where(low, other, plus2),
-            2: roll_rows(value, -2),
-        }
-
-    def index_along(direction, steps):
-        if direction == 1:
-            return half | (((y + steps) & 7) << 3) | z
-        return half | (y << 3) | ((z + steps) & 7)
-
-    ninth_x = low & (sub < 2)
-    is_y = (lane >= 64) & (lane < 80)
-    part, inner = ((lane >> 3) & 1) << 6, lane & 7
-
-    def ninth_index(layer):
-        return jnp.where(is_y, part | (layer << 3) | inner, part | (inner << 3) | layer)
-
-    mains = [[], [], []]
-    ninths = []
+            value = jnp.where(remote, 0.0, value)
+            tile = direction * FIELDS + f
+            ready_ref[pl.ds((GHOST + tile) * ROWS, ROWS), :] = turn(direction, value)
+            ready_ref[pl.ds((OWN + tile) * ROWS, ROWS), :] = turn(direction, own[f])
+
+
+def rate(blocks, ready_ref, pick_ref):
+    turn = Turns()
+    sub = turn.sub
+    first_row = sub == 0
+    candidates = []
+    for block in blocks:
+        candidates += [block, [swapped_slots(v, sub) for v in block]]
+
+    def line(direction, f):
+        pick = pick_ref[pl.ds(direction * ROWS, ROWS), :]
+        tile = direction * FIELDS + f
+        remote = jnp.zeros((ROWS, LANES), jnp.float32)
+        for c, candidate in enumerate(candidates):
+            remote = jnp.where(pick == EVEN + c, candidate[f], remote)
+        ghost = ready_ref[pl.ds((GHOST + tile) * ROWS, ROWS), :] + turn(direction, remote)
+        return ready_ref[pl.ds((OWN + tile) * ROWS, ROWS), :], ghost
+
+    is_x, is_y = (sub == 7) | first_row, (sub == 1) | (sub == 2)
+    places = (0, 2, 4)
+    sides = [[], [], []]
+    outer = []
     for f in range(FIELDS):
-        own_x, ghost_x = shifts_x(own[f]), shifts_x(ghosts[0][f])
-        cells = []
-        for k in range(6):
-            s = k - 3
-            outside = (x + s < 0) | (x + s > 7)
-            cells.append(jnp.where(outside, ghost_x[s], own_x[s]) if s else own[f])
-        mains[0].append(cells)
-        for direction in (1, 2):
-            place = y if direction == 1 else z
-            cells = []
-            for k in range(6):
-                s = k - 3
+        beside = []
+        for direction in range(3):
+            own, ghost = line(direction, f)
+            cells, around = [], []
+            for s in range(-2, 3):
                 if s == 0:
-                    cells.append(own[f])
+                    cells.append(own)
+                    around.append(ghost)
                     continue
-                outside = (place >= 8 + s) if s < 0 else (place < s)
-                merged = jnp.where(outside, ghosts[direction][f], own[f])
-                cells.append(gather_lanes(merged, index_along(direction, s)))
-            mains[direction].append(cells)
-        cells = []
-        for k in range(6):
-            if k < 3:
-                beside = gather_lanes(own[f], ninth_index(5 + k))
-                value = own_x[k - 3]
-            else:
-                index = ninth_index(k - 3)
-                beside = jnp.where(is_y, gather_lanes(ghosts[1][f], index), gather_lanes(ghosts[2][f], index))
-                value = ghost_x[k - 3]
-            cells.append(jnp.where(ninth_x, value, beside))
-        ninths.append(cells)
-
+                own_s, ghost_s = roll_rows(own, -s), roll_rows(ghost, -s)
+                outside = (sub + s < 0) | (sub + s > 7)
+                cells.append(jnp.where(outside, ghost_s, own_s))
+                at_first, at_last = (own_s, ghost_s) if s < 0 else (ghost_s, own_s)
+                around.append(jnp.where(first_row, at_first, at_last))
+            sides[direction].append(weno(cells))
+            beside.append(around)
+        outer.append(
+            weno(
+                [
+                    jnp.where(is_x, vx, jnp.where(is_y, roll_rows(vy, 2), roll_rows(vz, 4)))
+                    for vx, vy, vz in zip(*beside)
+                ]
+            )
+        )
+
+    ended = []
+    fluxes = []
     orders = ((0, 1, 2, 3, 4), (0, 2, 1, 3, 4), (0, 3, 1, 2, 4))
-    fluxes = []
     for direction in range(3):
-        states = [weno(mains[direction][f]) for f in orders[direction]]
-        fluxes.append(hllc([st[0] for st in states], [st[1] for st in states]))
-    states = [weno(ninths[f]) for f in range(FIELDS)]
-    is_z = lane >= 80
-
-    def turned(side):
-        values = [st[side] for st in states]
-        normal = jnp.where(is_y, values[2], jnp.where(is_z, values[3], values[1]))
-        one = jnp.where(is_y | is_z, values[1], values[2])
-        two = jnp.where(is_z, values[2], values[3])
+        rolled = [roll_rows(side[0], 1) for side in sides[direction]]
+        ended.append([roll_rows(v, places[direction]) for v in rolled])
+        lefts = [jnp.where(first_row, roll_rows(o[0], 1 - places[direction]), v) for o, v in zip(outer, rolled)]
+        rights = [side[1] for side in sides[direction]]
+        order = orders[direction]
+        fluxes.append(hllc([lefts[f] for f in order], [rights[f] for f in order]))
+
+    at_y, at_z = sub == 2, sub == 4
+
+    def turned(values):
+        normal = jnp.where(at_y, values[2], jnp.where(at_z, values[3], values[1]))
+        one = jnp.where(at_y | at_z, values[1], values[2])
+        two = jnp.where(at_z, values[2], values[3])
         return [values[0], normal, one, two, values[4]]
 
-    last = hllc(turned(0), turned(1))
-
-    back_index = (
-        None,
-        64 + ((lane >> 6) << 3) + z,
-        80 + ((lane >> 6) << 3) + y,
-    )
-    backs = ((0, 1, 2, 3, 4), (0, 2, 1, 3, 4), (0, 2, 3, 1, 4))
+    left_end = [jnp.where(at_y, ended[1][f], jnp.where(at_z, ended[2][f], ended[0][f])) for f in range(FIELDS)]
+    last = hllc(turned(left_end), turned([o[1] for o in outer]))
+
     total = [None] * FIELDS
     for direction in range(3):
-        for place in range(FIELDS):
+        for place, f in enumerate(orders[direction]):
             flux = fluxes[direction][place]
-            if direction == 0:
-                merged = roll_lanes(jnp.where(x == 0, last[place], flux), 64)
-                after = jnp.where(low, merged, roll_rows(merged, -2))
-            else:
-                end = (y if direction == 1 else z) == 7
-                after = jnp.where(
-                    end,
-                    gather_lanes(last[place], back_index[direction]),
-                    gather_lanes(flux, index_along(direction, 1)),
-                )
-            change = flux - after
-            f = backs[direction].index(place)
+            merged = jnp.where(first_row, roll_rows(last[place], -places[direction]), flux)
+            change = turn(direction, flux - roll_rows(merged, -1))
             total[f] = change if total[f] is None else total[f] + change
     return total
 
 
-def first_stage(own_ref, odd_ref, even_ref, ghost_ref, pick_ref, out_ref):
-    own = load_primitives(own_ref)
-    change = rate(own, [own, load_primitives(even_ref), load_primitives(odd_ref)], ghost_ref, pick_ref)
+def even_and_odd(even_refs, odd_refs):
+    blocks = [primitives(*load_parts(even_refs))]
+    return blocks + [load_primitives(ref) for ref in odd_refs]
+
+
+def middle_of(own_refs, even_refs, odd_refs, ready_ref, pick_ref, out_ref, part_refs):
+    own = load_parts(own_refs)
+    change = rate(even_and_odd(even_refs, odd_refs), ready_ref, pick_ref)
+    middle = [own[f] + TIME_STEP * change[f] for f in range(FIELDS)]
+    store_parts(part_refs, middle)
     for f in range(FIELDS):
-        rows = pl.ds(f * ROWS, ROWS)
-        out_ref[rows, :] = own_ref[rows, :] + TIME_STEP * change[f]
-
-
-def second_stage(start_ref, own_ref, odd_ref, even_ref, ghost_ref, pick_ref, count_ref, out_ref):
-    own = load_primitives(own_ref)
-    change = rate(own, [own, load_primitives(even_ref), load_primitives(odd_ref)], ghost_ref, pick_ref)
+        out_ref[pl.ds(f * ROWS, ROWS), :] = middle[f]
+
+
+def first_stage(waits_ref, ready_ref, pick_ref, *refs):
+    n = len(PARTS)
+    own_refs, even_refs, out_ref, part_refs = refs[:n], refs[n : 2 * n], refs[2 * n], refs[2 * n + 1 :]
+
+    @pl.when(waits_ref[0, 0] == 0)
+    def _():
+        middle_of(own_refs, even_refs, [], ready_ref, pick_ref, out_ref, part_refs)
+
+
+def first_stage_odd(waits_ref, ready_ref, pick_ref, *refs):
+    n = len(PARTS)
+    own_refs, even_refs, odd_ref, made = refs[:n], refs[n : 2 * n], refs[2 * n], refs[3 * n + 2 :]
+
+    @pl.when(waits_ref[0, 0] != 0)
+    def _():
+        middle_of(own_refs, even_refs, [odd_ref], ready_ref, pick_ref, made[0], made[1:])
+
+
+def advanced_of(start_refs, own_refs, even_refs, odd_refs, ready_ref, pick_ref, count_ref, out_ref, made_ref, sem):
+    start, own = load_parts(start_refs), load_parts(own_refs)
+    change = rate(even_and_odd(even_refs, odd_refs), ready_ref, pick_ref)
     sub, _ = positions()
     live = (sub & 1) < count_ref[0, 0]
     for f in range(FIELDS):
-        rows = pl.ds(f * ROWS, ROWS)
-        value = 0.5 * start_ref[rows, :] + 0.5 * (own_ref[rows, :] + TIME_STEP * change[f])
-        out_ref[rows, :] = jnp.where(live, value, 0.0)
+        value = 0.5 * start[f] + 0.5 * (own[f] + TIME_STEP * change[f])
+        made_ref[pl.ds(f * ROWS, ROWS), :] = jnp.where(live, value, 0.0)
+    copy = pltpu.make_async_copy(made_ref, out_ref, sem)
+    copy.start()
+    copy.wait()
+
+
+def second_stage(waits_ref, count_ref, ready_ref, pick_ref, *refs):
+    n = len(PARTS)
+    start_refs, own_refs, even_refs, (out_ref, made_ref, sem) = refs[:n], refs[n : 2 * n], refs[2 * n : 3 * n], refs[3 * n :]
+
+    @pl.when(waits_ref[0, 0] == 0)
+    def _():
+        advanced_of(start_refs, own_refs, even_refs, [], ready_ref, pick_ref, count_ref, out_ref, made_ref, sem)
+
+
+def second_stage_odd(waits_ref, count_ref, ready_ref, pick_ref, *refs):
+    n = len(PARTS)
+    start_refs, own_refs, even_refs = refs[:n], refs[n : 2 * n], refs[2 * n : 3 * n]
+    odd_ref, _, out_ref, made_ref, sem = refs[3 * n :]
+
+    @pl.when(waits_ref[0, 0] != 0)
+    def _():
+        advanced_of(start_refs, own_refs, even_refs, [odd_ref], ready_ref, pick_ref, count_ref, out_ref, made_ref, sem)
 
 
 def vmem_spec():
@@ -410,20 +482,21 @@
     odd = exchange(start, odd_partner)
     group = [exchange(coarse, group_shift(r)) for r in range(1, members)]
 
-    picks, table, corners, own = pl.pallas_call(
+    picks, table, corners, waits, *own = pl.pallas_call(
         read_links,
         out_shape=(
             pltpu.VMEM((3 * ROWS, LANES), jnp.int32),
             pltpu.VMEM((16, ROWS, LANES), jnp.float32),
             pltpu.SMEM((2, 4, 6), jnp.int32),
-            pltpu.VMEM((tile_rows, LANES), jnp.float32),
+            pltpu.SMEM((2, 6), jnp.int32),
+            *[pltpu.VMEM((rows, LANES), jnp.float32) for _, rows in PARTS],
         ),
         in_specs=[hbm_spec()] * 4,
-        out_specs=(vmem_spec(), vmem_spec(), smem_spec(), vmem_spec()),
+        out_specs=(vmem_spec(), vmem_spec(), smem_spec(), smem_spec()) + (vmem_spec(),) * len(PARTS),
         scratch_shapes=[
             pltpu.SMEM((2, 6), jnp.int32),
             pltpu.VMEM((FIELDS * 4, 1, LANES), jnp.float32),
-            pltpu.SemaphoreType.DMA((4,)),
+            pltpu.SemaphoreType.DMA((3 + len(PARTS),)),
         ],
         name="read_links",
     )(
@@ -432,7 +505,7 @@
         coarse,
         start,
     )
-    even = exchange(start, even_partner)
+    even = [in_vmem(exchange(part, even_partner)) for part in own]
     ghosts = pl.pallas_call(
         interpolate,
         out_shape=pltpu.VMEM((3 * tile_rows, LANES), jnp.float32),
@@ -446,31 +519,61 @@
         cost_estimate=pl.CostEstimate(flops=10000000000, bytes_accessed=10000000000, transcendentals=0),
     )(in_smem(corners), in_vmem(table), *[in_vmem(c) for c in group])
 
+    count = len(PARTS)
+    tiles = (tile_rows, LANES)
+    waits, picks, ghosts = in_smem(waits), in_vmem(picks), in_vmem(ghosts)
+    own = [in_vmem(part) for part in own]
+
+    def fold(parts):
+        ready = pl.pallas_call(
+            make_ready,
+            out_shape=pltpu.VMEM((READY * ROWS, LANES), jnp.float32),
+            in_specs=[vmem_spec()] * (2 + count),
+            out_specs=vmem_spec(),
+            name="fold",
+        )(ghosts, picks, *parts)
+        return in_vmem(ready)
+
+    made = (pltpu.VMEM(tiles, jnp.float32),) + tuple(pltpu.VMEM((rows, LANES), jnp.float32) for _, rows in PARTS)
+    ready = fold(own)
     middle = pl.pallas_call(
         first_stage,
-        out_shape=pltpu.VMEM((tile_rows, LANES), jnp.float32),
-        in_specs=[vmem_spec()] * 5,
-        out_specs=vmem_spec(),
+        out_shape=made,
+        in_specs=[smem_spec()] + [vmem_spec()] * (2 + 2 * count),
+        out_specs=(vmem_spec(),) * len(made),
         name="first_stage",
-    )(in_vmem(own), in_vmem(odd), in_vmem(even), in_vmem(ghosts), in_vmem(picks))
-
-    even = exchange(middle, even_partner)
+    )(waits, ready, picks, *own, *even)
+    middle, *parts = pl.pallas_call(
+        first_stage_odd,
+        out_shape=made,
+        in_specs=[smem_spec()] + [vmem_spec()] * (4 + 3 * count),
+        out_specs=(vmem_spec(),) * len(made),
+        input_output_aliases={4 + 2 * count + k: k for k in range(len(made))},
+        name="first_stage_odd",
+    )(waits, ready, picks, *own, *even, in_vmem(odd), *[in_vmem(m) for m in middle])
+
     odd = exchange(middle, odd_partner)
+    even = [in_vmem(exchange(part, even_partner)) for part in parts]
+    parts = [in_vmem(part) for part in parts]
+    ready = fold(parts)
+    scratch = [pltpu.VMEM(tiles, jnp.float32), pltpu.SemaphoreType.DMA(())]
     result = pl.pallas_call(
         second_stage,
-        out_shape=jax.ShapeDtypeStruct((tile_rows, LANES), jnp.float32),
-        in_specs=[vmem_spec()] * 6 + [smem_spec()],
-        out_specs=vmem_spec(),
+        out_shape=jax.ShapeDtypeStruct(tiles, jnp.float32),
+        in_specs=[smem_spec()] * 2 + [vmem_spec()] * (2 + 3 * count),
+        out_specs=hbm_spec(),
+        scratch_shapes=scratch,
         name="second_stage",
-    )(
-        in_vmem(own),
-        in_vmem(middle),
-        in_vmem(odd),
-        in_vmem(even),
-        in_vmem(ghosts),
-        in_vmem(picks),
-        box_count,
-    )
+    )(waits, box_count, ready, picks, *own, *parts, *even)
+    result = pl.pallas_call(
+        second_stage_odd,
+        out_shape=jax.ShapeDtypeStruct(tiles, jnp.float32),
+        in_specs=[smem_spec()] * 2 + [vmem_spec()] * (3 + 3 * count) + [hbm_spec()],
+        out_specs=hbm_spec(),
+        scratch_shapes=scratch,
+        input_output_aliases={5 + 3 * count: 0},
+        name="second_stage_odd",
+    )(waits, box_count, ready, picks, *own, *parts, *even, in_vmem(odd), result)
     return from_tiles(result, fine_state.shape)
 
 

time: 12.7 us -> 11.7 us (0.921)
  the two profiles are of different devices: /device:TPU:0 before, /device:TPU:16 now
where the time goes in v3:
time: 11.7 us; the launch traced here: 11.5 us
  starting transfers between devices  4.53 us (39%)
  Pallas kernels  3.23 us (28%)
  waiting for transfers between devices  3.08 us (26%)
  between operations  0.7 us (6%)
    ppermute x7, starting transfers between devices, exchange(): return lax.ppermute(value, ('sfc', 'sub'), pairs)  4.53 us
    ppermute x7, waiting for transfers between devices, exchange(): return lax.ppermute(value, ('sfc', 'sub'), pairs)  3.08 us
    pallas_call x1, Pallas kernels, body(): pl.pallas_call(second_stage_odd, out_shape=jax.ShapeDtypeStruct(tiles, jn...  1.07 us
    pallas_call x1, Pallas kernels, body(): pl.pallas_call(read_links, out_shape=(pltpu.VMEM((3 * ROWS, LANES), jnp.i...  0.94 us
    pallas_call x1, Pallas kernels, body(): pl.pallas_call(interpolate, out_shape=pltpu.VMEM((3 * tile_rows, LANES),...  0.52 us
    pallas_call x1, Pallas kernels, body(): pl.pallas_call(first_stage_odd, out_shape=made, in_specs=[smem_spec()] +...  0.45 us
    pallas_call x2, Pallas kernels, fold(): pl.pallas_call(make_ready, out_shape=pltpu.VMEM((READY * ROWS, LANES), jn...  0.24 us
  transfers between devices with their start and end apart: 7, of which 4 were waited for; matrix products, arithmetic and copies ran while one was open for 0% of the time, Pallas kernels for 15%

profile of v3, /device:TPU:16, one launch (start us, length us, event | category | flops | bytes accessed | tf_op | source)
XLA Modules:
  0.0 11.5 jit_solution(2147993303644078701)
XLA Ops:
  0.0 1.5 %collective-permute-start = (f32[20,1,128]{2,1,0:T(1,128)}, f32[20,1,128]{2,1,0:T(1,128)S(1)}, u32[]{:S(2)}, u32[]{:S(2)}) collective-permute-start(f32[20,1,128]{2,1,0:T(1,128)} %bitcast.17), channel_id=1, source_target_pairs={{0,1},{1,0},{2,3},{3,2},{4,5},{5,4},{6,7},{7,6},{8,9},{9,8},{10,11... | collective-permute-start | bytes 30728 | tf_op jit(solution)/shard_map/ppermute | solution.py:46
  1.5 0.5 %collective-permute-start.3 = (f32[40,128]{1,0:T(8,128)}, f32[40,128]{1,0:T(8,128)S(1)}, u32[]{:S(2)}, u32[]{:S(2)}) collective-permute-start(f32[40,128]{1,0:T(8,128)} %bitcast.15), channel_id=1, source_target_pairs={{0,1},{1,0},{2,4},{3,5},{4,2},{5,3},{6,8},{7,9},{8,6},{9,7},{10,12... | collective-permute-start | bytes 61448 | tf_op jit(solution)/shard_map/ppermute | solution.py:46
  2.1 0.9 %read_links.1 = (s32[24,128]{1,0:T(8,128)S(1)}, f32[16,8,128]{2,1,0:T(8,128)S(1)}, s32[2,4,6]{2,1,0:T(4,128)S(4)}, s32[2,6]{1,0:T(2,128)S(4)}, f32[32,128]{1,0:T(8,128)S(1)}, /*index=5*/f32[8,128]{1,0:T(8,128)S(1)}) custom-call(s32[2,6]{1,0:T(2,128)} %bitcast.20, s32[2,4,6]{2,1,0:T(4,128)} %bitcast.19, f32[20,1,128]{2,1,0:T(1,128)} %bitcast.18, ...), custom_call_target="tpu_custom_call" | custom-call | tf_op jit(solution)/shard_map/read_links/pallas_call | solution.py:485
  3.0 1.1 %collective-permute-start.1 = (f32[32,128]{1,0:T(8,128)S(1)}, f32[32,128]{1,0:T(8,128)S(1)}, u32[]{:S(2)}, u32[]{:S(2)}) collective-permute-start(f32[32,128]{1,0:T(8,128)S(1)} %get-tuple-element.21.refs_0_), channel_id=1, source_target_pairs={{0,2},{1,3},{2,0},{3,1},{4,6},{5,7},{6,4},{7,5},{8,10},{9,11},{10,... | collective-permute-start | bytes 49160 | tf_op jit(solution)/shard_map/ppermute | solution.py:46
  4.1 0.1 collective-permute-start.2
  4.2 0.0 collective-permute-done.refs_0_
  4.2 0.5 %interpolate.1.ghost_ref = f32[120,128]{1,0:T(8,128)S(1)} custom-call(s32[2,4,6]{2,1,0:T(4,128)S(4)} %get-tuple-element.18.corner_ref, f32[16,8,128]{2,1,0:T(8,128)S(1)} %get-tuple-element.19.own_table, f32[20,1,128]{2,1,0:T(1,128)S(1)} %collective-permute-done.refs_0_), custom_call_target="tpu_custom_call" | custom-call | flops 10000000000 | bytes 10000000000 | tf_op jit(solution)/shard_map/interpolate/pallas_call | solution.py:509
  4.7 0.1 %fold.2.ready_ref = f32[240,128]{1,0:T(8,128)S(1)} custom-call(f32[120,128]{1,0:T(8,128)S(1)} %interpolate.1.ghost_ref, s32[24,128]{1,0:T(8,128)S(1)} %get-tuple-element.20.pick_ref, f32[32,128]{1,0:T(8,128)S(1)} %get-tuple-element.21.refs_0_, f32[8,128]{1,0:T(8,128)S(1)} %get-tuple-element.22.refs_1_), custom_call_target="tpu_custom_call" | custom-call | tf_op jit(solution)/shard_map/fold/pallas_call | solution.py:528
  4.9 0.4 %collective-permute-done.2.refs_3_ = f32[8,128]{1,0:T(8,128)S(1)} collective-permute-done((f32[8,128]{1,0:T(8,128)S(1)}, f32[8,128]{1,0:T(8,128)S(1)}, u32[]{:S(2)}, u32[]{:S(2)}) %collective-permute-start.2) | collective-permute-done | bytes 4128 | tf_op jit(solution)/shard_map/ppermute | solution.py:46
  5.3 0.0 collective-permute-done.1.refs_2_
  5.3 0.5 %collective-permute-done.3.refs_4_ = f32[40,128]{1,0:T(8,128)S(1)} collective-permute-done((f32[40,128]{1,0:T(8,128)}, f32[40,128]{1,0:T(8,128)S(1)}, u32[]{:S(2)}, u32[]{:S(2)}) %collective-permute-start.3) | collective-permute-done | bytes 20512 | tf_op jit(solution)/shard_map/ppermute | solution.py:46
  5.8 0.4 %first_stage_odd.1 = (f32[40,128]{1,0:T(8,128)S(1)}, f32[32,128]{1,0:T(8,128)S(1)}, f32[8,128]{1,0:T(8,128)S(1)}) custom-call(s32[2,6]{1,0:T(2,128)S(4)} %get-tuple-element.17.waits_ref, f32[240,128]{1,0:T(8,128)S(1)} %fold.2.ready_ref, s32[24,128]{1,0:T(8,128)S(1)} %get-tuple-element.20.pick_ref, ...), custom_call_target="tpu_custom_call", output_to_operand_aliasing={{0}: (8, {}), {1}: (9, {}), {2}: (10, {})} | custom-call | tf_op jit(solution)/shard_map/first_stage_odd/pallas_call | solution.py:546
  6.3 0.7 %collective-permute-start.6 = (f32[40,128]{1,0:T(8,128)S(1)}, f32[40,128]{1,0:T(8,128)S(1)}, u32[]{:S(2)}, u32[]{:S(2)}) collective-permute-start(f32[40,128]{1,0:T(8,128)S(1)} %get-tuple-element.28), channel_id=1, source_target_pairs={{0,1},{1,0},{2,4},{3,5},{4,2},{5,3},{6,8},{7,9},{8,6},{9,7},{10,12... | collective-permute-start | bytes 61448 | tf_op jit(solution)/shard_map/ppermute | solution.py:46
  7.0 0.5 %collective-permute-start.4 = (f32[32,128]{1,0:T(8,128)S(1)}, f32[32,128]{1,0:T(8,128)S(1)}, u32[]{:S(2)}, u32[]{:S(2)}) collective-permute-start(f32[32,128]{1,0:T(8,128)S(1)} %get-tuple-element.26.refs_0_.refs_2_), channel_id=1, source_target_pairs={{0,2},{1,3},{2,0},{3,1},{4,6},{5,7},{6,4},{7,5},{8,10},{9,11},{10,... | collective-permute-start | bytes 49160 | tf_op jit(solution)/shard_map/ppermute | solution.py:46
  7.5 0.0 collective-permute-start.5
  8.2 0.1 %fold.3.ready_ref = f32[240,128]{1,0:T(8,128)S(1)} custom-call(f32[120,128]{1,0:T(8,128)S(1)} %interpolate.1.ghost_ref, s32[24,128]{1,0:T(8,128)S(1)} %get-tuple-element.20.pick_ref, f32[32,128]{1,0:T(8,128)S(1)} %get-tuple-element.26.refs_0_.refs_2_, f32[8,128]{1,0:T(8,128)S(1)} %get-tuple-element.27.refs_1_.refs_3_), custom_call_target="tpu_custom_call" | custom-call | tf_op jit(solution)/shard_map/fold/pallas_call | solution.py:528
  8.3 0.4 %collective-permute-done.5.refs_5_ = f32[8,128]{1,0:T(8,128)S(1)} collective-permute-done((f32[8,128]{1,0:T(8,128)S(1)}, f32[8,128]{1,0:T(8,128)S(1)}, u32[]{:S(2)}, u32[]{:S(2)}) %collective-permute-start.5) | collective-permute-done | bytes 4128 | tf_op jit(solution)/shard_map/ppermute | solution.py:46
  8.7 0.0 collective-permute-done.4.refs_4_
  8.7 1.8 %collective-permute-done.6.refs_6_ = f32[40,128]{1,0:T(8,128)S(1)} collective-permute-done((f32[40,128]{1,0:T(8,128)S(1)}, f32[40,128]{1,0:T(8,128)S(1)}, u32[]{:S(2)}, u32[]{:S(2)}) %collective-permute-start.6) | collective-permute-done | bytes 20512 | tf_op jit(solution)/shard_map/ppermute | solution.py:46
  10.5 1.1 %second_stage_odd.1 = f32[40,128]{1,0:T(8,128)} custom-call(s32[2,6]{1,0:T(2,128)S(4)} %get-tuple-element.17.waits_ref, s32[1,1]{1,0:T(1,128)S(6)} %copy.16.count_ref, f32[240,128]{1,0:T(8,128)S(1)} %fold.3.ready_ref, s32[24,128]{1,0:T(8,128)S(1)} %get-tuple-element.20.pick_ref, ...), custom_call_target="tpu_custom_call", output_to_operand_aliasing={{}: (11, {})} | custom-call | tf_op jit(solution)/shard_map/second_stage_odd/pallas_call | solution.py:568
  (2 shorter events, 0.0 us)
Async XLA Ops:
  0.0 4.2 %collective-permute-start = (f32[20,1,128]{2,1,0:T(1,128)}, f32[20,1,128]{2,1,0:T(1,128)S(1)}, u32[]{:S(2)}, u32[]{:S(2)}) collective-permute-start(f32[20,1,128]{2,1,0:T(1,128)} %bitcast.17), channel_id=1, source_target_pairs={{0,1},{1,0},{2,3},{3,2},{4,5},{5,4},{6,7},{7,6},{8,9},{9,8},{10,11... | collective-permute-start | bytes 30728 | tf_op jit(solution)/shard_map/ppermute | solution.py:46
  1.5 4.3 %collective-permute-start.3 = (f32[40,128]{1,0:T(8,128)}, f32[40,128]{1,0:T(8,128)S(1)}, u32[]{:S(2)}, u32[]{:S(2)}) collective-permute-start(f32[40,128]{1,0:T(8,128)} %bitcast.15), channel_id=1, source_target_pairs={{0,1},{1,0},{2,4},{3,5},{4,2},{5,3},{6,8},{7,9},{8,6},{9,7},{10,12... | collective-permute-start | bytes 61448 | tf_op jit(solution)/shard_map/ppermute | solution.py:46
  3.0 2.3 %collective-permute-start.1 = (f32[32,128]{1,0:T(8,128)S(1)}, f32[32,128]{1,0:T(8,128)S(1)}, u32[]{:S(2)}, u32[]{:S(2)}) collective-permute-start(f32[32,128]{1,0:T(8,128)S(1)} %get-tuple-element.21.refs_0_), channel_id=1, source_target_pairs={{0,2},{1,3},{2,0},{3,1},{4,6},{5,7},{6,4},{7,5},{8,10},{9,11},{10,... | collective-permute-start | bytes 49160 | tf_op jit(solution)/shard_map/ppermute | solution.py:46
  4.1 1.2 %collective-permute-start.2 = (f32[8,128]{1,0:T(8,128)S(1)}, f32[8,128]{1,0:T(8,128)S(1)}, u32[]{:S(2)}, u32[]{:S(2)}) collective-permute-start(f32[8,128]{1,0:T(8,128)S(1)} %get-tuple-element.22.refs_1_), channel_id=1, source_target_pairs={{0,2},{1,3},{2,0},{3,1},{4,6},{5,7},{6,4},{7,5},{8,10},{9,11},{10,... | collective-permute-start | bytes 12296 | tf_op jit(solution)/shard_map/ppermute | solution.py:46
  6.3 4.2 %collective-permute-start.6 = (f32[40,128]{1,0:T(8,128)S(1)}, f32[40,128]{1,0:T(8,128)S(1)}, u32[]{:S(2)}, u32[]{:S(2)}) collective-permute-start(f32[40,128]{1,0:T(8,128)S(1)} %get-tuple-element.28), channel_id=1, source_target_pairs={{0,1},{1,0},{2,4},{3,5},{4,2},{5,3},{6,8},{7,9},{8,6},{9,7},{10,12... | collective-permute-start | bytes 61448 | tf_op jit(solution)/shard_map/ppermute | solution.py:46
  7.0 1.6 %collective-permute-start.4 = (f32[32,128]{1,0:T(8,128)S(1)}, f32[32,128]{1,0:T(8,128)S(1)}, u32[]{:S(2)}, u32[]{:S(2)}) collective-permute-start(f32[32,128]{1,0:T(8,128)S(1)} %get-tuple-element.26.refs_0_.refs_2_), channel_id=1, source_target_pairs={{0,2},{1,3},{2,0},{3,1},{4,6},{5,7},{6,4},{7,5},{8,10},{9,11},{10,... | collective-permute-start | bytes 49160 | tf_op jit(solution)/shard_map/ppermute | solution.py:46
  7.5 1.2 %collective-permute-start.5 = (f32[8,128]{1,0:T(8,128)S(1)}, f32[8,128]{1,0:T(8,128)S(1)}, u32[]{:S(2)}, u32[]{:S(2)}) collective-permute-start(f32[8,128]{1,0:T(8,128)S(1)} %get-tuple-element.27.refs_1_.refs_3_), channel_id=1, source_target_pairs={{0,2},{1,3},{2,0},{3,1},{4,6},{5,7},{6,4},{7,5},{8,10},{9,11},{10,... | collective-permute-start | bytes 12296 | tf_op jit(solution)/shard_map/ppermute | solution.py:46

commit v4 on v3

--- a/solution.py
+++ b/solution.py
@@ -126,39 +126,56 @@
     return jnp.maximum(jnp.minimum(p, q), 0.0) + jnp.minimum(jnp.maximum(p, q), 0.0)
 
 
-def slopes(table, base, low):
-    cells = [table[base + j] for j in range(4)]
+def build_table(coarse_ref, raw, table, base):
+    sub, lane = positions()
+    low = lane < 64
+    for j in range(4):
+        for f in range(FIELDS):
+            raw[j, f : f + 1, :] = coarse_ref[f * 4 + j]
+    cells = [raw[j] for j in range(4)]
     halves = [roll_lanes(c, 64) for c in cells]
     for j in range(4):
         u = cells[j]
         up = jnp.where(low, halves[j], halves[min(j + 1, 3)])
         down = jnp.where(low, halves[max(j - 1, 0)], halves[j])
-        table[base + 4 + j] = 0.25 * minmod(up - u, u - down)
-        table[base + 8 + j] = 0.25 * minmod(roll_lanes(u, -8) - u, u - roll_lanes(u, 8))
-        table[base + 12 + j] = 0.25 * minmod(roll_lanes(u, -1) - u, u - roll_lanes(u, 1))
-
-
-def spread_fields(table, base, coarse_ref):
-    for j in range(4):
-        for f in range(FIELDS):
-            table[base + j, f : f + 1, :] = coarse_ref[f * 4 + j]
-
-
-def read_links(links_in, corner_in, coarse_in, start_in, pick_ref, table, corner_ref, code_ref, *refs):
-    own_refs, (links_ref, coarse_ref, sems) = refs[:-3], refs[-3:]
+        slopes = (
+            0.25 * minmod(up - u, u - down),
+            0.25 * minmod(roll_lanes(u, -8) - u, u - roll_lanes(u, 8)),
+            0.25 * minmod(roll_lanes(u, -1) - u, u - roll_lanes(u, 1)),
+        )
+        along_x, along_y, along_z = slopes
+        swapped_x, swapped_y, swapped_z = [roll_lanes(v, 64) for v in slopes]
+        for x in (2 * j, 2 * j + 1):
+            if x in (0, 7):
+                continue
+            if x % 2 == 0:
+                value, slope = jnp.where(low, u, halves[j]), jnp.where(low, along_x, swapped_x)
+                sides = jnp.where(low, along_y, swapped_z)
+            else:
+                value, slope = jnp.where(low, halves[j], u), jnp.where(low, swapped_x, along_x)
+                sides = jnp.where(low, swapped_y, along_z)
+            value = jnp.where(low, value - slope, value + slope)
+            table[base + x] = jnp.where(sub < FIELDS, value, gather_rows(sides, (sub + 3) & 7))
+            table[base + 8 + x] = jnp.where(sub < FIELDS, sides, gather_rows(sides, (sub + 6) & 7))
+
+
+def fetch(links_in, corner_in, coarse_in, start_in, links_ref, corner_ref, coarse_ref, *refs):
+    own_refs, sems = refs[:-1], refs[-1]
     copies = [(links_in, links_ref), (corner_in, corner_ref), (coarse_in, coarse_ref)]
     for own_ref, (first, rows) in zip(own_refs, PARTS):
         copies.append((start_in.at[pl.ds(first, rows), :], own_ref))
     fetches = [pltpu.make_async_copy(src, dst, sems.at[i]) for i, (src, dst) in enumerate(copies)]
-    for fetch in fetches:
-        fetch.start()
+    for copy in fetches:
+        copy.start()
+    for copy in fetches:
+        copy.wait()
+
+
+def read_links(links_ref, coarse_ref, pick_ref, table, code_ref, raw):
     sub, lane = positions()
     y, z = (lane >> 3) & 7, lane & 7
     odd_segment = lax.axis_index("sfc") & 1
-    for fetch in fetches:
-        fetch.wait()
-    spread_fields(table, 0, coarse_ref)
-    slopes(table, 0, lane < 64)
+    build_table(coarse_ref, raw, table, 0)
 
     def choice(slot, face):
         link = links_ref[slot, face]
@@ -183,42 +200,44 @@
 
 
 def interpolate(corner_ref, own_table, *refs):
-    coarse_refs, (ghost_ref, table, lines) = refs[:-3], refs[-3:]
+    coarse_refs, (ghost_ref, table, raw, lines) = refs[:-4], refs[-4:]
     members = len(coarse_refs) + 1
     sub, lane = positions()
-    low = lane < 64
     y, z = (lane >> 3) & 7, lane & 7
     me = lax.axis_index("sub")
     table[0:16] = own_table[...]
     for m, coarse_ref in enumerate(coarse_refs):
-        spread_fields(table, (m + 1) * 16, coarse_ref)
-        slopes(table, (m + 1) * 16, low)
-
-    sign_x = jnp.where(low, -1.0, 1.0)
+        build_table(coarse_ref, raw, table, (m + 1) * 16)
+
     sign_y = jnp.where((y & 1) == 0, -1.0, 1.0)
     sign_z = jnp.where((z & 1) == 0, -1.0, 1.0)
     spread = (y >> 1) * 8 + (z >> 1)
-
-    def children(slot, face, j):
+    upper, whole = jnp.where(sub < FIELDS, lane & 64, 0), jnp.where(sub < FIELDS, 64, 0)
+
+    def finder(slot, face):
         direction, minus = face // 2, face % 2 == 0
         start = [corner_ref[slot, 1 + a, face] + (-1 if minus and a == direction else 1) for a in range(3)]
         owner = me - corner_ref[slot, 0, face]
         owner = jnp.where(owner < 0, owner + members, owner)
-        along = start[0] + j
-        index = (spread + ((along & 1) * 64 + start[1] * 8 + start[2])) & (LANES - 1)
-        row = owner * 16 + (along >> 1)
-        parts = [gather_lanes(table[row + 4 * q], index) for q in range(4)]
-        return parts[0] + sign_x * parts[1] + sign_y * parts[2] + sign_z * parts[3]
+        index = (spread + (start[1] * 8 + start[2])) & 63
+        first, second, row = index | upper, index | whole, owner * 16 + start[0]
+
+        def find(j):
+            return gather_lanes(table[row + j], first), gather_lanes(table[row + 8 + j], second)
+
+        return find
 
     for direction in range(3):
         for slot in range(2):
+            minus, plus = finder(slot, 2 * direction), finder(slot, 2 * direction + 1)
             for j in range(4):
-                minus, plus = 2 * direction, 2 * direction + 1
                 if direction == 0:
-                    value = children(slot, minus if j >= 2 else plus, j)
+                    value, sides = (minus if j >= 2 else plus)(j)
                 else:
                     lower = (y if direction == 1 else z) < 4
-                    value = jnp.where(lower, children(slot, plus, j), children(slot, minus, j))
+                    value, sides = [jnp.where(lower, p, m) for p, m in zip(plus(j), minus(j))]
+                along_y = jnp.where(sub < 3, gather_rows(value, (sub + 5) & 7), gather_rows(sides, (sub + 2) & 7))
+                value = value + sign_y * along_y + sign_z * sides
                 rows = pl.ds(direction * 40 + j * 2 + slot, FIELDS, stride=ROWS)
                 lines[rows, :] = value[0:FIELDS, :]
         made = load_primitives(lines, direction * 40)
@@ -480,25 +499,20 @@
     coarse = coarse.reshape(-1, 1, LANES)
 
     odd = exchange(start, odd_partner)
-    group = [exchange(coarse, group_shift(r)) for r in range(1, members)]
-
-    picks, table, corners, waits, *own = pl.pallas_call(
-        read_links,
+    group = [in_vmem(exchange(coarse, group_shift(r))) for r in range(1, members)]
+
+    links, corners, own_coarse, *own = pl.pallas_call(
+        fetch,
         out_shape=(
-            pltpu.VMEM((3 * ROWS, LANES), jnp.int32),
-            pltpu.VMEM((16, ROWS, LANES), jnp.float32),
+            pltpu.SMEM((2, 6), jnp.int32),
             pltpu.SMEM((2, 4, 6), jnp.int32),
-            pltpu.SMEM((2, 6), jnp.int32),
+            pltpu.VMEM((FIELDS * 4, 1, LANES), jnp.float32),
             *[pltpu.VMEM((rows, LANES), jnp.float32) for _, rows in PARTS],
         ),
         in_specs=[hbm_spec()] * 4,
-        out_specs=(vmem_spec(), vmem_spec(), smem_spec(), smem_spec()) + (vmem_spec(),) * len(PARTS),
-        scratch_shapes=[
-            pltpu.SMEM((2, 6), jnp.int32),
-            pltpu.VMEM((FIELDS * 4, 1, LANES), jnp.float32),
-            pltpu.SemaphoreType.DMA((3 + len(PARTS),)),
-        ],
-        name="read_links",
+        out_specs=(smem_spec(), smem_spec(), vmem_spec()) + (vmem_spec(),) * len(PARTS),
+        scratch_shapes=[pltpu.SemaphoreType.DMA((3 + len(PARTS),))],
+        name="fetch",
     )(
         fine_links.reshape(2, 6),
         coarse_links.transpose(0, 1, 2, 4, 3).reshape(2, 4, 6),
@@ -506,6 +520,20 @@
         start,
     )
     even = [in_vmem(exchange(part, even_partner)) for part in own]
+    raw = pltpu.VMEM((4, ROWS, LANES), jnp.float32)
+    picks, table, waits = pl.pallas_call(
+        read_links,
+        out_shape=(
+            pltpu.VMEM((3 * ROWS, LANES), jnp.int32),
+            pltpu.VMEM((16, ROWS, LANES), jnp.float32),
+            pltpu.SMEM((2, 6), jnp.int32),
+        ),
+        in_specs=[smem_spec(), vmem_spec()],
+        out_specs=(vmem_spec(), vmem_spec(), smem_spec()),
+        scratch_shapes=[raw],
+        name="read_links",
+    )(in_smem(links), in_vmem(own_coarse))
+
     ghosts = pl.pallas_call(
         interpolate,
         out_shape=pltpu.VMEM((3 * tile_rows, LANES), jnp.float32),
@@ -513,11 +541,12 @@
         out_specs=vmem_spec(),
         scratch_shapes=[
             pltpu.VMEM((members * 16, ROWS, LANES), jnp.float32),
+            raw,
             pltpu.VMEM((3 * tile_rows, LANES), jnp.float32),
         ],
+        cost_estimate=pl.CostEstimate(flops=10**10, bytes_accessed=10**10, transcendentals=0),
         name="interpolate",
-        cost_estimate=pl.CostEstimate(flops=10000000000, bytes_accessed=10000000000, transcendentals=0),
-    )(in_smem(corners), in_vmem(table), *[in_vmem(c) for c in group])
+    )(in_smem(corners), in_vmem(table), *group)
 
     count = len(PARTS)
     tiles = (tile_rows, LANES)

time: 11.7 us -> 11.7 us (level)
    pallas_call x0 -> x1, Pallas kernels: none -> 0.8 us  [body(): pl.pallas_call(fetch, out_shape=(pltpu.SMEM((2, 6), jnp.int32), pltpu.SME...]
    pallas_call x1, Pallas kernels: 0.94 us -> 0.22 us  [body(): pl.pallas_call(read_links, out_shape=(pltpu.VMEM((3 * ROWS, LANES), jnp.i...]
where the time goes in v4:
time: 11.7 us; the launch traced here: 11.5 us
  starting transfers between devices  4.47 us (38%)
  Pallas kernels  3.27 us (28%)
  waiting for transfers between devices  3.08 us (26%)
  between operations  0.71 us (6%)
    ppermute x7, starting transfers between devices, exchange(): return lax.ppermute(value, ('sfc', 'sub'), pairs)  4.47 us
    ppermute x7, waiting for transfers between devices, exchange(): return lax.ppermute(value, ('sfc', 'sub'), pairs)  3.08 us
    pallas_call x1, Pallas kernels, body(): pl.pallas_call(second_stage_odd, out_shape=jax.ShapeDtypeStruct(tiles, jn...  1.07 us
    pallas_call x1, Pallas kernels, body(): pl.pallas_call(fetch, out_shape=(pltpu.SMEM((2, 6), jnp.int32), pltpu.SME...  0.8 us
    pallas_call x1, Pallas kernels, body(): pl.pallas_call(interpolate, out_shape=pltpu.VMEM((3 * tile_rows, LANES),...  0.48 us
    pallas_call x1, Pallas kernels, body(): pl.pallas_call(first_stage_odd, out_shape=made, in_specs=[smem_spec()] +...  0.45 us
    pallas_call x2, Pallas kernels, fold(): pl.pallas_call(make_ready, out_shape=pltpu.VMEM((READY * ROWS, LANES), jn...  0.24 us
  transfers between devices with their start and end apart: 7, of which 4 were waited for; matrix products, arithmetic and copies ran while one was open for 0% of the time, Pallas kernels for 15%

profile of v4, /device:TPU:16, one launch (start us, length us, event | category | flops | bytes accessed | tf_op | source)
XLA Modules:
  0.0 11.5 jit_solution(14045997122003051123)
XLA Ops:
  0.0 1.5 %collective-permute-start = (f32[20,1,128]{2,1,0:T(1,128)}, f32[20,1,128]{2,1,0:T(1,128)S(1)}, u32[]{:S(2)}, u32[]{:S(2)}) collective-permute-start(f32[20,1,128]{2,1,0:T(1,128)} %bitcast.17), channel_id=1, source_target_pairs={{0,1},{1,0},{2,3},{3,2},{4,5},{5,4},{6,7},{7,6},{8,9},{9,8},{10,11... | collective-permute-start | bytes 30728 | tf_op jit(solution)/shard_map/ppermute | solution.py:46
  1.5 0.5 %collective-permute-start.3 = (f32[40,128]{1,0:T(8,128)}, f32[40,128]{1,0:T(8,128)S(1)}, u32[]{:S(2)}, u32[]{:S(2)}) collective-permute-start(f32[40,128]{1,0:T(8,128)} %bitcast.15), channel_id=1, source_target_pairs={{0,1},{1,0},{2,4},{3,5},{4,2},{5,3},{6,8},{7,9},{8,6},{9,7},{10,12... | collective-permute-start | bytes 61448 | tf_op jit(solution)/shard_map/ppermute | solution.py:46
  2.1 0.8 %fetch.1 = (s32[2,6]{1,0:T(2,128)S(4)}, s32[2,4,6]{2,1,0:T(4,128)S(4)}, f32[20,1,128]{2,1,0:T(1,128)S(1)}, f32[32,128]{1,0:T(8,128)S(1)}, f32[8,128]{1,0:T(8,128)S(1)}) custom-call(s32[2,6]{1,0:T(2,128)} %bitcast.20, s32[2,4,6]{2,1,0:T(4,128)} %bitcast.19, f32[20,1,128]{2,1,0:T(1,128)} %bitcast.18, f32[40,128]{1,0:T(8,128)} %bitcast.16), custom_call_target="tpu_custom_call" | custom-call | tf_op jit(solution)/shard_map/fetch/pallas_call | solution.py:504
  2.9 1.1 %collective-permute-start.1 = (f32[32,128]{1,0:T(8,128)S(1)}, f32[32,128]{1,0:T(8,128)S(1)}, u32[]{:S(2)}, u32[]{:S(2)}) collective-permute-start(f32[32,128]{1,0:T(8,128)S(1)} %get-tuple-element.25.refs_0_), channel_id=1, source_target_pairs={{0,2},{1,3},{2,0},{3,1},{4,6},{5,7},{6,4},{7,5},{8,10},{9,11},{10,... | collective-permute-start | bytes 49160 | tf_op jit(solution)/shard_map/ppermute | solution.py:46
  4.0 0.1 collective-permute-start.2
  4.1 0.2 %read_links.1 = (s32[24,128]{1,0:T(8,128)S(1)}, f32[16,8,128]{2,1,0:T(8,128)S(1)}, s32[2,6]{1,0:T(2,128)S(4)}) custom-call(s32[2,6]{1,0:T(2,128)S(4)} %get-tuple-element.19.links_ref, f32[20,1,128]{2,1,0:T(1,128)S(1)} %get-tuple-element.20.coarse_ref), custom_call_target="tpu_custom_call" | custom-call | tf_op jit(solution)/shard_map/read_links/pallas_call | solution.py:524
  4.3 0.0 collective-permute-done.refs_0_
  4.3 0.5 %interpolate.1.ghost_ref = f32[120,128]{1,0:T(8,128)S(1)} custom-call(s32[2,4,6]{2,1,0:T(4,128)S(4)} %get-tuple-element.22.corner_ref, f32[16,8,128]{2,1,0:T(8,128)S(1)} %get-tuple-element.23.own_table, f32[20,1,128]{2,1,0:T(1,128)S(1)} %collective-permute-done.refs_0_), custom_call_target="tpu_custom_call" | custom-call | flops 10000000000 | bytes 10000000000 | tf_op jit(solution)/shard_map/interpolate/pallas_call | solution.py:537
  4.8 0.1 %fold.2.ready_ref = f32[240,128]{1,0:T(8,128)S(1)} custom-call(f32[120,128]{1,0:T(8,128)S(1)} %interpolate.1.ghost_ref, s32[24,128]{1,0:T(8,128)S(1)} %get-tuple-element.24.pick_ref, f32[32,128]{1,0:T(8,128)S(1)} %get-tuple-element.25.refs_0_, f32[8,128]{1,0:T(8,128)S(1)} %get-tuple-element.26.refs_1_), custom_call_target="tpu_custom_call" | custom-call | tf_op jit(solution)/shard_map/fold/pallas_call | solution.py:557
  4.9 0.2 %collective-permute-done.2.refs_3_ = f32[8,128]{1,0:T(8,128)S(1)} collective-permute-done((f32[8,128]{1,0:T(8,128)S(1)}, f32[8,128]{1,0:T(8,128)S(1)}, u32[]{:S(2)}, u32[]{:S(2)}) %collective-permute-start.2) | collective-permute-done | bytes 4128 | tf_op jit(solution)/shard_map/ppermute | solution.py:46
  5.2 0.0 collective-permute-done.1.refs_2_
  5.2 0.7 %collective-permute-done.3.refs_4_ = f32[40,128]{1,0:T(8,128)S(1)} collective-permute-done((f32[40,128]{1,0:T(8,128)}, f32[40,128]{1,0:T(8,128)S(1)}, u32[]{:S(2)}, u32[]{:S(2)}) %collective-permute-start.3) | collective-permute-done | bytes 20512 | tf_op jit(solution)/shard_map/ppermute | solution.py:46
  5.8 0.4 %first_stage_odd.1 = (f32[40,128]{1,0:T(8,128)S(1)}, f32[32,128]{1,0:T(8,128)S(1)}, f32[8,128]{1,0:T(8,128)S(1)}) custom-call(s32[2,6]{1,0:T(2,128)S(4)} %get-tuple-element.21.waits_ref, f32[240,128]{1,0:T(8,128)S(1)} %fold.2.ready_ref, s32[24,128]{1,0:T(8,128)S(1)} %get-tuple-element.24.pick_ref, ...), custom_call_target="tpu_custom_call", output_to_operand_aliasing={{0}: (8, {}), {1}: (9, {}), {2}: (10, {})} | custom-call | tf_op jit(solution)/shard_map/first_stage_odd/pallas_call | solution.py:575
  6.3 0.7 %collective-permute-start.6 = (f32[40,128]{1,0:T(8,128)S(1)}, f32[40,128]{1,0:T(8,128)S(1)}, u32[]{:S(2)}, u32[]{:S(2)}) collective-permute-start(f32[40,128]{1,0:T(8,128)S(1)} %get-tuple-element.32), channel_id=1, source_target_pairs={{0,1},{1,0},{2,4},{3,5},{4,2},{5,3},{6,8},{7,9},{8,6},{9,7},{10,12... | collective-permute-start | bytes 61448 | tf_op jit(solution)/shard_map/ppermute | solution.py:46
  7.0 0.4 %collective-permute-start.4 = (f32[32,128]{1,0:T(8,128)S(1)}, f32[32,128]{1,0:T(8,128)S(1)}, u32[]{:S(2)}, u32[]{:S(2)}) collective-permute-start(f32[32,128]{1,0:T(8,128)S(1)} %get-tuple-element.30.refs_0_.refs_2_), channel_id=1, source_target_pairs={{0,2},{1,3},{2,0},{3,1},{4,6},{5,7},{6,4},{7,5},{8,10},{9,11},{10,... | collective-permute-start | bytes 49160 | tf_op jit(solution)/shard_map/ppermute | solution.py:46
  7.4 0.1 %collective-permute-start.5 = (f32[8,128]{1,0:T(8,128)S(1)}, f32[8,128]{1,0:T(8,128)S(1)}, u32[]{:S(2)}, u32[]{:S(2)}) collective-permute-start(f32[8,128]{1,0:T(8,128)S(1)} %get-tuple-element.31.refs_1_.refs_3_), channel_id=1, source_target_pairs={{0,2},{1,3},{2,0},{3,1},{4,6},{5,7},{6,4},{7,5},{8,10},{9,11},{10,... | collective-permute-start | bytes 12296 | tf_op jit(solution)/shard_map/ppermute | solution.py:46
  8.1 0.1 %fold.3.ready_ref = f32[240,128]{1,0:T(8,128)S(1)} custom-call(f32[120,128]{1,0:T(8,128)S(1)} %interpolate.1.ghost_ref, s32[24,128]{1,0:T(8,128)S(1)} %get-tuple-element.24.pick_ref, f32[32,128]{1,0:T(8,128)S(1)} %get-tuple-element.30.refs_0_.refs_2_, f32[8,128]{1,0:T(8,128)S(1)} %get-tuple-element.31.refs_1_.refs_3_), custom_call_target="tpu_custom_call" | custom-call | tf_op jit(solution)/shard_map/fold/pallas_call | solution.py:557
  8.3 0.3 %collective-permute-done.5.refs_5_ = f32[8,128]{1,0:T(8,128)S(1)} collective-permute-done((f32[8,128]{1,0:T(8,128)S(1)}, f32[8,128]{1,0:T(8,128)S(1)}, u32[]{:S(2)}, u32[]{:S(2)}) %collective-permute-start.5) | collective-permute-done | bytes 4128 | tf_op jit(solution)/shard_map/ppermute | solution.py:46
  8.5 0.0 collective-permute-done.4.refs_4_
  8.5 1.9 %collective-permute-done.6.refs_6_ = f32[40,128]{1,0:T(8,128)S(1)} collective-permute-done((f32[40,128]{1,0:T(8,128)S(1)}, f32[40,128]{1,0:T(8,128)S(1)}, u32[]{:S(2)}, u32[]{:S(2)}) %collective-permute-start.6) | collective-permute-done | bytes 20512 | tf_op jit(solution)/shard_map/ppermute | solution.py:46
  10.5 1.1 %second_stage_odd.1 = f32[40,128]{1,0:T(8,128)} custom-call(s32[2,6]{1,0:T(2,128)S(4)} %get-tuple-element.21.waits_ref, s32[1,1]{1,0:T(1,128)S(6)} %copy.16.count_ref, f32[240,128]{1,0:T(8,128)S(1)} %fold.3.ready_ref, s32[24,128]{1,0:T(8,128)S(1)} %get-tuple-element.24.pick_ref, ...), custom_call_target="tpu_custom_call", output_to_operand_aliasing={{}: (11, {})} | custom-call | tf_op jit(solution)/shard_map/second_stage_odd/pallas_call | solution.py:597
  (2 shorter events, 0.0 us)
Async XLA Ops:
  0.0 4.3 %collective-permute-start = (f32[20,1,128]{2,1,0:T(1,128)}, f32[20,1,128]{2,1,0:T(1,128)S(1)}, u32[]{:S(2)}, u32[]{:S(2)}) collective-permute-start(f32[20,1,128]{2,1,0:T(1,128)} %bitcast.17), channel_id=1, source_target_pairs={{0,1},{1,0},{2,3},{3,2},{4,5},{5,4},{6,7},{7,6},{8,9},{9,8},{10,11... | collective-permute-start | bytes 30728 | tf_op jit(solution)/shard_map/ppermute | solution.py:46
  1.5 4.3 %collective-permute-start.3 = (f32[40,128]{1,0:T(8,128)}, f32[40,128]{1,0:T(8,128)S(1)}, u32[]{:S(2)}, u32[]{:S(2)}) collective-permute-start(f32[40,128]{1,0:T(8,128)} %bitcast.15), channel_id=1, source_target_pairs={{0,1},{1,0},{2,4},{3,5},{4,2},{5,3},{6,8},{7,9},{8,6},{9,7},{10,12... | collective-permute-start | bytes 61448 | tf_op jit(solution)/shard_map/ppermute | solution.py:46
  2.9 2.3 %collective-permute-start.1 = (f32[32,128]{1,0:T(8,128)S(1)}, f32[32,128]{1,0:T(8,128)S(1)}, u32[]{:S(2)}, u32[]{:S(2)}) collective-permute-start(f32[32,128]{1,0:T(8,128)S(1)} %get-tuple-element.25.refs_0_), channel_id=1, source_target_pairs={{0,2},{1,3},{2,0},{3,1},{4,6},{5,7},{6,4},{7,5},{8,10},{9,11},{10,... | collective-permute-start | bytes 49160 | tf_op jit(solution)/shard_map/ppermute | solution.py:46
  4.0 1.2 %collective-permute-start.2 = (f32[8,128]{1,0:T(8,128)S(1)}, f32[8,128]{1,0:T(8,128)S(1)}, u32[]{:S(2)}, u32[]{:S(2)}) collective-permute-start(f32[8,128]{1,0:T(8,128)S(1)} %get-tuple-element.26.refs_1_), channel_id=1, source_target_pairs={{0,2},{1,3},{2,0},{3,1},{4,6},{5,7},{6,4},{7,5},{8,10},{9,11},{10,... | collective-permute-start | bytes 12296 | tf_op jit(solution)/shard_map/ppermute | solution.py:46
  6.3 4.2 %collective-permute-start.6 = (f32[40,128]{1,0:T(8,128)S(1)}, f32[40,128]{1,0:T(8,128)S(1)}, u32[]{:S(2)}, u32[]{:S(2)}) collective-permute-start(f32[40,128]{1,0:T(8,128)S(1)} %get-tuple-element.32), channel_id=1, source_target_pairs={{0,1},{1,0},{2,4},{3,5},{4,2},{5,3},{6,8},{7,9},{8,6},{9,7},{10,12... | collective-permute-start | bytes 61448 | tf_op jit(solution)/shard_map/ppermute | solution.py:46
  7.0 1.6 %collective-permute-start.4 = (f32[32,128]{1,0:T(8,128)S(1)}, f32[32,128]{1,0:T(8,128)S(1)}, u32[]{:S(2)}, u32[]{:S(2)}) collective-permute-start(f32[32,128]{1,0:T(8,128)S(1)} %get-tuple-element.30.refs_0_.refs_2_), channel_id=1, source_target_pairs={{0,2},{1,3},{2,0},{3,1},{4,6},{5,7},{6,4},{7,5},{8,10},{9,11},{10,... | collective-permute-start | bytes 49160 | tf_op jit(solution)/shard_map/ppermute | solution.py:46
  7.4 1.2 %collective-permute-start.5 = (f32[8,128]{1,0:T(8,128)S(1)}, f32[8,128]{1,0:T(8,128)S(1)}, u32[]{:S(2)}, u32[]{:S(2)}) collective-permute-start(f32[8,128]{1,0:T(8,128)S(1)} %get-tuple-element.31.refs_1_.refs_3_), channel_id=1, source_target_pairs={{0,2},{1,3},{2,0},{3,1},{4,6},{5,7},{6,4},{7,5},{8,10},{9,11},{10,... | collective-permute-start | bytes 12296 | tf_op jit(solution)/shard_map/ppermute | solution.py:46

commit v5 on v4

--- a/solution.py
+++ b/solution.py
@@ -105,10 +105,7 @@
 
 
 def load_parts(refs):
-    fields = []
-    for ref, (_, rows) in zip(refs, PARTS):
-        fields += [ref[pl.ds(at, ROWS), :] for at in range(0, rows, ROWS)]
-    return fields
+    return [ref[pl.ds(at, ROWS), :] for ref in refs for at in range(0, ref.shape[0], ROWS)]
 
 
 def store_parts(refs, fields):
@@ -159,11 +156,8 @@
             table[base + 8 + x] = jnp.where(sub < FIELDS, sides, gather_rows(sides, (sub + 6) & 7))
 
 
-def fetch(links_in, corner_in, coarse_in, start_in, links_ref, corner_ref, coarse_ref, *refs):
-    own_refs, sems = refs[:-1], refs[-1]
-    copies = [(links_in, links_ref), (corner_in, corner_ref), (coarse_in, coarse_ref)]
-    for own_ref, (first, rows) in zip(own_refs, PARTS):
-        copies.append((start_in.at[pl.ds(first, rows), :], own_ref))
+def fetch(links_in, corner_in, coarse_in, start_in, links_ref, corner_ref, coarse_ref, own_ref, sems):
+    copies = [(links_in, links_ref), (corner_in, corner_ref), (coarse_in, coarse_ref), (start_in, own_ref)]
     fetches = [pltpu.make_async_copy(src, dst, sems.at[i]) for i, (src, dst) in enumerate(copies)]
     for copy in fetches:
         copy.start()
@@ -429,22 +423,18 @@
         out_ref[pl.ds(f * ROWS, ROWS), :] = middle[f]
 
 
-def first_stage(waits_ref, ready_ref, pick_ref, *refs):
-    n = len(PARTS)
-    own_refs, even_refs, out_ref, part_refs = refs[:n], refs[n : 2 * n], refs[2 * n], refs[2 * n + 1 :]
-
+def first_stage(waits_ref, ready_ref, pick_ref, own_ref, even_ref, *made):
     @pl.when(waits_ref[0, 0] == 0)
     def _():
-        middle_of(own_refs, even_refs, [], ready_ref, pick_ref, out_ref, part_refs)
-
-
-def first_stage_odd(waits_ref, ready_ref, pick_ref, *refs):
-    n = len(PARTS)
-    own_refs, even_refs, odd_ref, made = refs[:n], refs[n : 2 * n], refs[2 * n], refs[3 * n + 2 :]
+        middle_of([own_ref], [even_ref], [], ready_ref, pick_ref, made[0], made[1:])
+
+
+def first_stage_odd(waits_ref, ready_ref, pick_ref, own_ref, even_ref, odd_ref, *refs):
+    made = refs[len(refs) // 2 :]
 
     @pl.when(waits_ref[0, 0] != 0)
     def _():
-        middle_of(own_refs, even_refs, [odd_ref], ready_ref, pick_ref, made[0], made[1:])
+        middle_of([own_ref], [even_ref], [odd_ref], ready_ref, pick_ref, made[0], made[1:])
 
 
 def advanced_of(start_refs, own_refs, even_refs, odd_refs, ready_ref, pick_ref, count_ref, out_ref, made_ref, sem):
@@ -460,23 +450,22 @@
     copy.wait()
 
 
-def second_stage(waits_ref, count_ref, ready_ref, pick_ref, *refs):
+def second_stage(waits_ref, count_ref, ready_ref, pick_ref, start_ref, *refs):
     n = len(PARTS)
-    start_refs, own_refs, even_refs, (out_ref, made_ref, sem) = refs[:n], refs[n : 2 * n], refs[2 * n : 3 * n], refs[3 * n :]
+    own_refs, even_refs, (out_ref, made_ref, sem) = refs[:n], refs[n : 2 * n], refs[2 * n :]
 
     @pl.when(waits_ref[0, 0] == 0)
     def _():
-        advanced_of(start_refs, own_refs, even_refs, [], ready_ref, pick_ref, count_ref, out_ref, made_ref, sem)
-
-
-def second_stage_odd(waits_ref, count_ref, ready_ref, pick_ref, *refs):
+        advanced_of([start_ref], own_refs, even_refs, [], ready_ref, pick_ref, count_ref, out_ref, made_ref, sem)
+
+
+def second_stage_odd(waits_ref, count_ref, ready_ref, pick_ref, start_ref, *refs):
     n = len(PARTS)
-    start_refs, own_refs, even_refs = refs[:n], refs[n : 2 * n], refs[2 * n : 3 * n]
-    odd_ref, _, out_ref, made_ref, sem = refs[3 * n :]
+    own_refs, even_refs, (odd_ref, _, out_ref, made_ref, sem) = refs[:n], refs[n : 2 * n], refs[2 * n :]
 
     @pl.when(waits_ref[0, 0] != 0)
     def _():
-        advanced_of(start_refs, own_refs, even_refs, [odd_ref], ready_ref, pick_ref, count_ref, out_ref, made_ref, sem)
+        advanced_of([start_ref], own_refs, even_refs, [odd_ref], ready_ref, pick_ref, count_ref, out_ref, made_ref, sem)
 
 
 def vmem_spec():
@@ -501,17 +490,17 @@
     odd = exchange(start, odd_partner)
     group = [in_vmem(exchange(coarse, group_shift(r))) for r in range(1, members)]
 
-    links, corners, own_coarse, *own = pl.pallas_call(
+    links, corners, own_coarse, own = pl.pallas_call(
         fetch,
         out_shape=(
             pltpu.SMEM((2, 6), jnp.int32),
             pltpu.SMEM((2, 4, 6), jnp.int32),
             pltpu.VMEM((FIELDS * 4, 1, LANES), jnp.float32),
-            *[pltpu.VMEM((rows, LANES), jnp.float32) for _, rows in PARTS],
+            pltpu.VMEM((tile_rows, LANES), jnp.float32),
         ),
         in_specs=[hbm_spec()] * 4,
-        out_specs=(smem_spec(), smem_spec(), vmem_spec()) + (vmem_spec(),) * len(PARTS),
-        scratch_shapes=[pltpu.SemaphoreType.DMA((3 + len(PARTS),))],
+        out_specs=(smem_spec(), smem_spec(), vmem_spec(), vmem_spec()),
+        scratch_shapes=[pltpu.SemaphoreType.DMA((4,))],
         name="fetch",
     )(
         fine_links.reshape(2, 6),
@@ -519,7 +508,7 @@
         coarse,
         start,
     )
-    even = [in_vmem(exchange(part, even_partner)) for part in own]
+    even = in_vmem(exchange(own, even_partner))
     raw = pltpu.VMEM((4, ROWS, LANES), jnp.float32)
     picks, table, waits = pl.pallas_call(
         read_links,
@@ -551,35 +540,35 @@
     count = len(PARTS)
     tiles = (tile_rows, LANES)
     waits, picks, ghosts = in_smem(waits), in_vmem(picks), in_vmem(ghosts)
-    own = [in_vmem(part) for part in own]
+    own = in_vmem(own)
 
     def fold(parts):
         ready = pl.pallas_call(
             make_ready,
             out_shape=pltpu.VMEM((READY * ROWS, LANES), jnp.float32),
-            in_specs=[vmem_spec()] * (2 + count),
+            in_specs=[vmem_spec()] * (2 + len(parts)),
             out_specs=vmem_spec(),
             name="fold",
         )(ghosts, picks, *parts)
         return in_vmem(ready)
 
     made = (pltpu.VMEM(tiles, jnp.float32),) + tuple(pltpu.VMEM((rows, LANES), jnp.float32) for _, rows in PARTS)
-    ready = fold(own)
+    ready = fold([own])
     middle = pl.pallas_call(
         first_stage,
         out_shape=made,
-        in_specs=[smem_spec()] + [vmem_spec()] * (2 + 2 * count),
+        in_specs=[smem_spec()] + [vmem_spec()] * 4,
         out_specs=(vmem_spec(),) * len(made),
         name="first_stage",
-    )(waits, ready, picks, *own, *even)
+    )(waits, ready, picks, own, even)
     middle, *parts = pl.pallas_call(
         first_stage_odd,
         out_shape=made,
-        in_specs=[smem_spec()] + [vmem_spec()] * (4 + 3 * count),
+        in_specs=[smem_spec()] + [vmem_spec()] * (5 + len(made)),
         out_specs=(vmem_spec(),) * len(made),
-        input_output_aliases={4 + 2 * count + k: k for k in range(len(made))},
+        input_output_aliases={6 + k: k for k in range(len(made))},
         name="first_stage_odd",
-    )(waits, ready, picks, *own, *even, in_vmem(odd), *[in_vmem(m) for m in middle])
+    )(waits, ready, picks, own, even, in_vmem(odd), *[in_vmem(m) for m in middle])
 
     odd = exchange(middle, odd_partner)
     even = [in_vmem(exchange(part, even_partner)) for part in parts]
@@ -589,20 +578,20 @@
     result = pl.pallas_call(
         second_stage,
         out_shape=jax.ShapeDtypeStruct(tiles, jnp.float32),
-        in_specs=[smem_spec()] * 2 + [vmem_spec()] * (2 + 3 * count),
+        in_specs=[smem_spec()] * 2 + [vmem_spec()] * (3 + 2 * count),
         out_specs=hbm_spec(),
         scratch_shapes=scratch,
         name="second_stage",
-    )(waits, box_count, ready, picks, *own, *parts, *even)
+    )(waits, box_count, ready, picks, own, *parts, *even)
     result = pl.pallas_call(
         second_stage_odd,
         out_shape=jax.ShapeDtypeStruct(tiles, jnp.float32),
-        in_specs=[smem_spec()] * 2 + [vmem_spec()] * (3 + 3 * count) + [hbm_spec()],
+        in_specs=[smem_spec()] * 2 + [vmem_spec()] * (4 + 2 * count) + [hbm_spec()],
         out_specs=hbm_spec(),
         scratch_shapes=scratch,
-        input_output_aliases={5 + 3 * count: 0},
+        input_output_aliases={6 + 2 * count: 0},
         name="second_stage_odd",
-    )(waits, box_count, ready, picks, *own, *parts, *even, in_vmem(odd), result)
+    )(waits, box_count, ready, picks, own, *parts, *even, in_vmem(odd), result)
     return from_tiles(result, fine_state.shape)
 
 

time: 11.7 us -> 11.7 us (level)
  starting transfers between devices: 4.47 us -> 4.3 us
  waiting for transfers between devices: 3.08 us -> 3.22 us
    ppermute x7 -> x6, starting transfers between devices: 4.47 us -> 4.3 us  [exchange(): return lax.ppermute(value, ('sfc', 'sub'), pairs)]
    ppermute x7 -> x6, waiting for transfers between devices: 3.08 us -> 3.22 us  [exchange(): return lax.ppermute(value, ('sfc', 'sub'), pairs)]
  transfers between devices with their start and end apart: 7 -> 6, of which waited for: 4 -> 3; matrix products, arithmetic and copies ran while one was open for 0% -> 0% of each run, Pallas kernels for 15% -> 15%
where the time goes in v5:
time: 11.7 us; the launch traced here: 11.5 us
  starting transfers between devices  4.3 us (37%)
  Pallas kernels  3.28 us (28%)
  waiting for transfers between devices  3.22 us (28%)
  between operations  0.72 us (6%)
    ppermute x6, starting transfers between devices, exchange(): return lax.ppermute(value, ('sfc', 'sub'), pairs)  4.3 us
    ppermute x6, waiting for transfers between devices, exchange(): return lax.ppermute(value, ('sfc', 'sub'), pairs)  3.22 us
    pallas_call x1, Pallas kernels, body(): pl.pallas_call(second_stage_odd, out_shape=jax.ShapeDtypeStruct(tiles, jn...  1.07 us
    pallas_call x1, Pallas kernels, body(): pl.pallas_call(fetch, out_shape=(pltpu.SMEM((2, 6), jnp.int32), pltpu.SME...  0.8 us
    pallas_call x1, Pallas kernels, body(): pl.pallas_call(interpolate, out_shape=pltpu.VMEM((3 * tile_rows, LANES),...  0.48 us
    pallas_call x1, Pallas kernels, body(): pl.pallas_call(first_stage_odd, out_shape=made, in_specs=[smem_spec()] +...  0.45 us
    pallas_call x2, Pallas kernels, fold(): pl.pallas_call(make_ready, out_shape=pltpu.VMEM((READY * ROWS, LANES), jn...  0.24 us
  transfers between devices with their start and end apart: 6, of which 3 were waited for; matrix products, arithmetic and copies ran while one was open for 0% of the time, Pallas kernels for 15%

profile of v5, /device:TPU:16, one launch (start us, length us, event | category | flops | bytes accessed | tf_op | source)
XLA Modules:
  0.0 11.5 jit_solution(110448404675646535)
XLA Ops:
  0.0 1.5 %collective-permute-start = (f32[20,1,128]{2,1,0:T(1,128)}, f32[20,1,128]{2,1,0:T(1,128)S(1)}, u32[]{:S(2)}, u32[]{:S(2)}) collective-permute-start(f32[20,1,128]{2,1,0:T(1,128)} %bitcast.17), channel_id=1, source_target_pairs={{0,1},{1,0},{2,3},{3,2},{4,5},{5,4},{6,7},{7,6},{8,9},{9,8},{10,11... | collective-permute-start | bytes 30728 | tf_op jit(solution)/shard_map/ppermute | solution.py:46
  1.5 0.5 %collective-permute-start.2 = (f32[40,128]{1,0:T(8,128)}, f32[40,128]{1,0:T(8,128)S(1)}, u32[]{:S(2)}, u32[]{:S(2)}) collective-permute-start(f32[40,128]{1,0:T(8,128)} %bitcast.15), channel_id=1, source_target_pairs={{0,1},{1,0},{2,4},{3,5},{4,2},{5,3},{6,8},{7,9},{8,6},{9,7},{10,12... | collective-permute-start | bytes 61448 | tf_op jit(solution)/shard_map/ppermute | solution.py:46
  2.1 0.8 %fetch.1 = (s32[2,6]{1,0:T(2,128)S(4)}, s32[2,4,6]{2,1,0:T(4,128)S(4)}, f32[20,1,128]{2,1,0:T(1,128)S(1)}, f32[40,128]{1,0:T(8,128)S(1)}) custom-call(s32[2,6]{1,0:T(2,128)} %bitcast.20, s32[2,4,6]{2,1,0:T(4,128)} %bitcast.19, f32[20,1,128]{2,1,0:T(1,128)} %bitcast.18, f32[40,128]{1,0:T(8,128)} %bitcast.16), custom_call_target="tpu_custom_call" | custom-call | tf_op jit(solution)/shard_map/fetch/pallas_call | solution.py:493
  2.9 1.1 %collective-permute-start.1 = (f32[40,128]{1,0:T(8,128)S(1)}, f32[40,128]{1,0:T(8,128)S(1)}, u32[]{:S(2)}, u32[]{:S(2)}) collective-permute-start(f32[40,128]{1,0:T(8,128)S(1)} %get-tuple-element.24.refs_0_.own_ref.start_ref), channel_id=1, source_target_pairs={{0,2},{1,3},{2,0},{3,1},{4,6},{5,7},{6,4},{7,5},{8,10},{9,11},{10,... | collective-permute-start | bytes 61448 | tf_op jit(solution)/shard_map/ppermute | solution.py:46
  4.0 0.2 %read_links.1 = (s32[24,128]{1,0:T(8,128)S(1)}, f32[16,8,128]{2,1,0:T(8,128)S(1)}, s32[2,6]{1,0:T(2,128)S(4)}) custom-call(s32[2,6]{1,0:T(2,128)S(4)} %get-tuple-element.18.links_ref, f32[20,1,128]{2,1,0:T(1,128)S(1)} %get-tuple-element.19.coarse_ref), custom_call_target="tpu_custom_call" | custom-call | tf_op jit(solution)/shard_map/read_links/pallas_call | solution.py:513
  4.2 0.0 collective-permute-done.refs_0_
  4.2 0.5 %interpolate.1.ghost_ref = f32[120,128]{1,0:T(8,128)S(1)} custom-call(s32[2,4,6]{2,1,0:T(4,128)S(4)} %get-tuple-element.21.corner_ref, f32[16,8,128]{2,1,0:T(8,128)S(1)} %get-tuple-element.22.own_table, f32[20,1,128]{2,1,0:T(1,128)S(1)} %collective-permute-done.refs_0_), custom_call_target="tpu_custom_call" | custom-call | flops 10000000000 | bytes 10000000000 | tf_op jit(solution)/shard_map/interpolate/pallas_call | solution.py:526
  4.7 0.1 %fold.2.ready_ref = f32[240,128]{1,0:T(8,128)S(1)} custom-call(f32[120,128]{1,0:T(8,128)S(1)} %interpolate.1.ghost_ref, s32[24,128]{1,0:T(8,128)S(1)} %get-tuple-element.23.pick_ref, f32[40,128]{1,0:T(8,128)S(1)} %get-tuple-element.24.refs_0_.own_ref.start_ref), custom_call_target="tpu_custom_call" | custom-call | tf_op jit(solution)/shard_map/fold/pallas_call | solution.py:546
  4.9 0.0 collective-permute-done.1.even_ref
  4.9 1.0 %collective-permute-done.2.odd_ref = f32[40,128]{1,0:T(8,128)S(1)} collective-permute-done((f32[40,128]{1,0:T(8,128)}, f32[40,128]{1,0:T(8,128)S(1)}, u32[]{:S(2)}, u32[]{:S(2)}) %collective-permute-start.2) | collective-permute-done | bytes 20512 | tf_op jit(solution)/shard_map/ppermute | solution.py:46
  5.8 0.4 %first_stage_odd.1 = (f32[40,128]{1,0:T(8,128)S(1)}, f32[32,128]{1,0:T(8,128)S(1)}, f32[8,128]{1,0:T(8,128)S(1)}) custom-call(s32[2,6]{1,0:T(2,128)S(4)} %get-tuple-element.20.waits_ref, f32[240,128]{1,0:T(8,128)S(1)} %fold.2.ready_ref, s32[24,128]{1,0:T(8,128)S(1)} %get-tuple-element.23.pick_ref, ...), custom_call_target="tpu_custom_call", output_to_operand_aliasing={{0}: (6, {}), {1}: (7, {}), {2}: (8, {})} | custom-call | tf_op jit(solution)/shard_map/first_stage_odd/pallas_call | solution.py:564
  6.3 0.6 %collective-permute-start.5 = (f32[40,128]{1,0:T(8,128)S(1)}, f32[40,128]{1,0:T(8,128)S(1)}, u32[]{:S(2)}, u32[]{:S(2)}) collective-permute-start(f32[40,128]{1,0:T(8,128)S(1)} %get-tuple-element.30), channel_id=1, source_target_pairs={{0,1},{1,0},{2,4},{3,5},{4,2},{5,3},{6,8},{7,9},{8,6},{9,7},{10,12... | collective-permute-start | bytes 61448 | tf_op jit(solution)/shard_map/ppermute | solution.py:46
  6.9 0.2 %collective-permute-start.3 = (f32[32,128]{1,0:T(8,128)S(1)}, f32[32,128]{1,0:T(8,128)S(1)}, u32[]{:S(2)}, u32[]{:S(2)}) collective-permute-start(f32[32,128]{1,0:T(8,128)S(1)} %get-tuple-element.28.refs_0_), channel_id=1, source_target_pairs={{0,2},{1,3},{2,0},{3,1},{4,6},{5,7},{6,4},{7,5},{8,10},{9,11},{10,... | collective-permute-start | bytes 49160 | tf_op jit(solution)/shard_map/ppermute | solution.py:46
  7.1 0.3 %collective-permute-start.4 = (f32[8,128]{1,0:T(8,128)S(1)}, f32[8,128]{1,0:T(8,128)S(1)}, u32[]{:S(2)}, u32[]{:S(2)}) collective-permute-start(f32[8,128]{1,0:T(8,128)S(1)} %get-tuple-element.29.refs_1_), channel_id=1, source_target_pairs={{0,2},{1,3},{2,0},{3,1},{4,6},{5,7},{6,4},{7,5},{8,10},{9,11},{10,... | collective-permute-start | bytes 12296 | tf_op jit(solution)/shard_map/ppermute | solution.py:46
  8.1 0.1 %fold.3.ready_ref = f32[240,128]{1,0:T(8,128)S(1)} custom-call(f32[120,128]{1,0:T(8,128)S(1)} %interpolate.1.ghost_ref, s32[24,128]{1,0:T(8,128)S(1)} %get-tuple-element.23.pick_ref, f32[32,128]{1,0:T(8,128)S(1)} %get-tuple-element.28.refs_0_, f32[8,128]{1,0:T(8,128)S(1)} %get-tuple-element.29.refs_1_), custom_call_target="tpu_custom_call" | custom-call | tf_op jit(solution)/shard_map/fold/pallas_call | solution.py:546
  8.2 0.1 collective-permute-done.4.refs_3_
  8.2 0.0 collective-permute-done.3.refs_2_
  8.3 2.2 %collective-permute-done.5.refs_4_ = f32[40,128]{1,0:T(8,128)S(1)} collective-permute-done((f32[40,128]{1,0:T(8,128)S(1)}, f32[40,128]{1,0:T(8,128)S(1)}, u32[]{:S(2)}, u32[]{:S(2)}) %collective-permute-start.5) | collective-permute-done | bytes 20512 | tf_op jit(solution)/shard_map/ppermute | solution.py:46
  10.5 1.1 %second_stage_odd.1 = f32[40,128]{1,0:T(8,128)} custom-call(s32[2,6]{1,0:T(2,128)S(4)} %get-tuple-element.20.waits_ref, s32[1,1]{1,0:T(1,128)S(6)} %copy.16.count_ref, f32[240,128]{1,0:T(8,128)S(1)} %fold.3.ready_ref, s32[24,128]{1,0:T(8,128)S(1)} %get-tuple-element.23.pick_ref, ...), custom_call_target="tpu_custom_call", output_to_operand_aliasing={{}: (10, {})} | custom-call | tf_op jit(solution)/shard_map/second_stage_odd/pallas_call | solution.py:586
  (2 shorter events, 0.0 us)
Async XLA Ops:
  0.0 4.2 %collective-permute-start = (f32[20,1,128]{2,1,0:T(1,128)}, f32[20,1,128]{2,1,0:T(1,128)S(1)}, u32[]{:S(2)}, u32[]{:S(2)}) collective-permute-start(f32[20,1,128]{2,1,0:T(1,128)} %bitcast.17), channel_id=1, source_target_pairs={{0,1},{1,0},{2,3},{3,2},{4,5},{5,4},{6,7},{7,6},{8,9},{9,8},{10,11... | collective-permute-start | bytes 30728 | tf_op jit(solution)/shard_map/ppermute | solution.py:46
  1.5 4.3 %collective-permute-start.2 = (f32[40,128]{1,0:T(8,128)}, f32[40,128]{1,0:T(8,128)S(1)}, u32[]{:S(2)}, u32[]{:S(2)}) collective-permute-start(f32[40,128]{1,0:T(8,128)} %bitcast.15), channel_id=1, source_target_pairs={{0,1},{1,0},{2,4},{3,5},{4,2},{5,3},{6,8},{7,9},{8,6},{9,7},{10,12... | collective-permute-start | bytes 61448 | tf_op jit(solution)/shard_map/ppermute | solution.py:46
  2.9 2.0 %collective-permute-start.1 = (f32[40,128]{1,0:T(8,128)S(1)}, f32[40,128]{1,0:T(8,128)S(1)}, u32[]{:S(2)}, u32[]{:S(2)}) collective-permute-start(f32[40,128]{1,0:T(8,128)S(1)} %get-tuple-element.24.refs_0_.own_ref.start_ref), channel_id=1, source_target_pairs={{0,2},{1,3},{2,0},{3,1},{4,6},{5,7},{6,4},{7,5},{8,10},{9,11},{10,... | collective-permute-start | bytes 61448 | tf_op jit(solution)/shard_map/ppermute | solution.py:46
  6.3 4.2 %collective-permute-start.5 = (f32[40,128]{1,0:T(8,128)S(1)}, f32[40,128]{1,0:T(8,128)S(1)}, u32[]{:S(2)}, u32[]{:S(2)}) collective-permute-start(f32[40,128]{1,0:T(8,128)S(1)} %get-tuple-element.30), channel_id=1, source_target_pairs={{0,1},{1,0},{2,4},{3,5},{4,2},{5,3},{6,8},{7,9},{8,6},{9,7},{10,12... | collective-permute-start | bytes 61448 | tf_op jit(solution)/shard_map/ppermute | solution.py:46
  6.9 1.4 %collective-permute-start.3 = (f32[32,128]{1,0:T(8,128)S(1)}, f32[32,128]{1,0:T(8,128)S(1)}, u32[]{:S(2)}, u32[]{:S(2)}) collective-permute-start(f32[32,128]{1,0:T(8,128)S(1)} %get-tuple-element.28.refs_0_), channel_id=1, source_target_pairs={{0,2},{1,3},{2,0},{3,1},{4,6},{5,7},{6,4},{7,5},{8,10},{9,11},{10,... | collective-permute-start | bytes 49160 | tf_op jit(solution)/shard_map/ppermute | solution.py:46
  7.1 1.2 %collective-permute-start.4 = (f32[8,128]{1,0:T(8,128)S(1)}, f32[8,128]{1,0:T(8,128)S(1)}, u32[]{:S(2)}, u32[]{:S(2)}) collective-permute-start(f32[8,128]{1,0:T(8,128)S(1)} %get-tuple-element.29.refs_1_), channel_id=1, source_target_pairs={{0,2},{1,3},{2,0},{3,1},{4,6},{5,7},{6,4},{7,5},{8,10},{9,11},{10,... | collective-permute-start | bytes 12296 | tf_op jit(solution)/shard_map/ppermute | solution.py:46

commit v6 on v5

--- a/solution.py
+++ b/solution.py
@@ -10,7 +10,7 @@
 LANES = 128
 GAMMA = 1.4
 FLOOR = 0.1
-EPS4 = 4e-06
+WENO_EPS = 1e-06
 TIME_STEP = 0.1
 PARTS = ((0, 32), (32, 8))
 HERE, EVEN, ODD = 1, 3, 5
@@ -239,21 +239,24 @@
             ghost_ref[pl.ds(direction * 40 + f * ROWS, ROWS), :] = made[f]
 
 
-def weno(cells):
+def weno(cells, both=True):
     centre = cells[2]
     e0, e1, e2, e3 = [cells[k + 1] - cells[k] for k in range(4)]
     d1, d2, d3 = e1 - e0, e2 - e1, e3 - e2
-    below, above, across = 3.0 * e1 - e0, 3.0 * e2 - e3, e1 + e2
-    a = ((13.0 / 3.0) * (d1 * d1) + EPS4) + below * below
-    b = ((13.0 / 3.0) * (d2 * d2) + EPS4) + across * across
-    c = ((13.0 / 3.0) * (d3 * d3) + EPS4) + above * above
+    a = ((4.0 / 3.0) * (d1 * d1) + WENO_EPS) + e1 * (e1 + d1)
+    b = ((4.0 / 3.0) * (d2 * d2) + WENO_EPS) + e1 * e2
+    c = ((4.0 / 3.0) * (d3 * d3) + WENO_EPS) + e2 * (e2 - d3)
     bc, ac, ab = b * c, a * c, a * b
     bc, ac, ab = bc * bc, 6.0 * (ac * ac), ab * ab
-    bc3, ab3 = 3.0 * bc, 3.0 * ab
-    up = bc * (2.0 * below - e1) + ac * (across + e2) + ab3 * (above + e2)
-    down = ab * (2.0 * above - e2) + ac * (across + e1) + bc3 * (below + e1)
-    upper = centre + up * ((1.0 / 6.0) * reciprocal(bc + ac + ab3))
-    lower = centre - down * ((1.0 / 6.0) * reciprocal(ab + ac + bc3))
+    with_ab, with_bc = 3.0 * ab + ac, 3.0 * bc + ac
+    low, high = bc * d1, ab * d3
+    twice = 2.0 * (high - low)
+    up = with_bc * d2 + (twice + high)
+    upper = (centre + 0.5 * e2) - up * ((1.0 / 6.0) * reciprocal(bc + with_ab))
+    if not both:
+        return upper
+    down = with_ab * d2 + (low - twice)
+    lower = (centre - 0.5 * e1) - down * ((1.0 / 6.0) * reciprocal(ab + with_bc))
     return upper, lower
 
 
@@ -308,7 +311,8 @@
     return gather_rows(value, sub ^ 1)
 
 
-OWN, GHOST, READY = 0, 15, 30
+OWN, GHOST, SHIFTED, READY = 0, 15, 30, 90
+SHIFTS = (-2, -1, 1, 2)
 
 
 def make_ready(ghost_ref, pick_ref, *refs):
@@ -327,7 +331,10 @@
             value = jnp.where(remote, 0.0, value)
             tile = direction * FIELDS + f
             ready_ref[pl.ds((GHOST + tile) * ROWS, ROWS), :] = turn(direction, value)
-            ready_ref[pl.ds((OWN + tile) * ROWS, ROWS), :] = turn(direction, own[f])
+            cells = turn(direction, own[f])
+            ready_ref[pl.ds((OWN + tile) * ROWS, ROWS), :] = cells
+            for k, s in enumerate(SHIFTS):
+                ready_ref[pl.ds((SHIFTED + tile * len(SHIFTS) + k) * ROWS, ROWS), :] = roll_rows(cells, -s)
 
 
 def rate(blocks, ready_ref, pick_ref):
@@ -356,16 +363,23 @@
         for direction in range(3):
             own, ghost = line(direction, f)
             cells, around = [], []
+            rolled_own, rolled_ghost = {}, {}
             for s in range(-2, 3):
                 if s == 0:
                     cells.append(own)
-                    around.append(ghost)
                     continue
-                own_s, ghost_s = roll_rows(own, -s), roll_rows(ghost, -s)
+                shifted = SHIFTED + (direction * FIELDS + f) * len(SHIFTS) + SHIFTS.index(s)
+                own_s, ghost_s = ready_ref[pl.ds(shifted * ROWS, ROWS), :], roll_rows(ghost, -s)
                 outside = (sub + s < 0) | (sub + s > 7)
                 cells.append(jnp.where(outside, ghost_s, own_s))
-                at_first, at_last = (own_s, ghost_s) if s < 0 else (ghost_s, own_s)
-                around.append(jnp.where(first_row, at_first, at_last))
+                rolled_own[s], rolled_ghost[s] = own_s, ghost_s
+            for s in range(-2, 3):
+                if s == 0:
+                    around.append(ghost)
+                elif s < 0:
+                    around.append(jnp.where(first_row, rolled_ghost[-s], rolled_ghost[s]))
+                else:
+                    around.append(jnp.where(first_row, rolled_own[-s], rolled_own[s]))
             sides[direction].append(weno(cells))
             beside.append(around)
         outer.append(
@@ -373,7 +387,8 @@
                 [
                     jnp.where(is_x, vx, jnp.where(is_y, roll_rows(vy, 2), roll_rows(vz, 4)))
                     for vx, vy, vz in zip(*beside)
-                ]
+                ],
+                both=False,
             )
         )
 
@@ -383,7 +398,7 @@
     for direction in range(3):
         rolled = [roll_rows(side[0], 1) for side in sides[direction]]
         ended.append([roll_rows(v, places[direction]) for v in rolled])
-        lefts = [jnp.where(first_row, roll_rows(o[0], 1 - places[direction]), v) for o, v in zip(outer, rolled)]
+        lefts = [jnp.where(first_row, roll_rows(o, 1 - places[direction]), v) for o, v in zip(outer, rolled)]
         rights = [side[1] for side in sides[direction]]
         order = orders[direction]
         fluxes.append(hllc([lefts[f] for f in order], [rights[f] for f in order]))
@@ -397,7 +412,7 @@
         return [values[0], normal, one, two, values[4]]
 
     left_end = [jnp.where(at_y, ended[1][f], jnp.where(at_z, ended[2][f], ended[0][f])) for f in range(FIELDS)]
-    last = hllc(turned(left_end), turned([o[1] for o in outer]))
+    last = hllc(turned(left_end), turned(outer))
 
     total = [None] * FIELDS
     for direction in range(3):

time: 11.7 us -> 11.6 us (level)
  no operation moved by 1% of the time
where the time goes in v6:
time: 11.6 us; the launch traced here: 11.5 us
  starting transfers between devices  4.3 us (37%)
  Pallas kernels  3.23 us (28%)
  waiting for transfers between devices  3.22 us (28%)
  between operations  0.72 us (6%)
    ppermute x6, starting transfers between devices, exchange(): return lax.ppermute(value, ('sfc', 'sub'), pairs)  4.3 us
    ppermute x6, waiting for transfers between devices, exchange(): return lax.ppermute(value, ('sfc', 'sub'), pairs)  3.22 us
    pallas_call x1, Pallas kernels, body(): pl.pallas_call(second_stage_odd, out_shape=jax.ShapeDtypeStruct(tiles, jn...  1.04 us
    pallas_call x1, Pallas kernels, body(): pl.pallas_call(fetch, out_shape=(pltpu.SMEM((2, 6), jnp.int32), pltpu.SME...  0.8 us
    pallas_call x1, Pallas kernels, body(): pl.pallas_call(interpolate, out_shape=pltpu.VMEM((3 * tile_rows, LANES),...  0.48 us
    pallas_call x1, Pallas kernels, body(): pl.pallas_call(first_stage_odd, out_shape=made, in_specs=[smem_spec()] +...  0.41 us
    pallas_call x2, Pallas kernels, fold(): pl.pallas_call(make_ready, out_shape=pltpu.VMEM((READY * ROWS, LANES), jn...  0.26 us
  transfers between devices with their start and end apart: 6, of which 3 were waited for; matrix products, arithmetic and copies ran while one was open for 0% of the time, Pallas kernels for 15%

profile of v6, /device:TPU:16, one launch (start us, length us, event | category | flops | bytes accessed | tf_op | source)
XLA Modules:
  0.0 11.5 jit_solution(13504209438303768158)
XLA Ops:
  0.0 1.5 %collective-permute-start = (f32[20,1,128]{2,1,0:T(1,128)}, f32[20,1,128]{2,1,0:T(1,128)S(1)}, u32[]{:S(2)}, u32[]{:S(2)}) collective-permute-start(f32[20,1,128]{2,1,0:T(1,128)} %bitcast.17), channel_id=1, source_target_pairs={{0,1},{1,0},{2,3},{3,2},{4,5},{5,4},{6,7},{7,6},{8,9},{9,8},{10,11... | collective-permute-start | bytes 30728 | tf_op jit(solution)/shard_map/ppermute | solution.py:46
  1.5 0.5 %collective-permute-start.2 = (f32[40,128]{1,0:T(8,128)}, f32[40,128]{1,0:T(8,128)S(1)}, u32[]{:S(2)}, u32[]{:S(2)}) collective-permute-start(f32[40,128]{1,0:T(8,128)} %bitcast.15), channel_id=1, source_target_pairs={{0,1},{1,0},{2,4},{3,5},{4,2},{5,3},{6,8},{7,9},{8,6},{9,7},{10,12... | collective-permute-start | bytes 61448 | tf_op jit(solution)/shard_map/ppermute | solution.py:46
  2.1 0.8 %fetch.1 = (s32[2,6]{1,0:T(2,128)S(4)}, s32[2,4,6]{2,1,0:T(4,128)S(4)}, f32[20,1,128]{2,1,0:T(1,128)S(1)}, f32[40,128]{1,0:T(8,128)S(1)}) custom-call(s32[2,6]{1,0:T(2,128)} %bitcast.20, s32[2,4,6]{2,1,0:T(4,128)} %bitcast.19, f32[20,1,128]{2,1,0:T(1,128)} %bitcast.18, f32[40,128]{1,0:T(8,128)} %bitcast.16), custom_call_target="tpu_custom_call" | custom-call | tf_op jit(solution)/shard_map/fetch/pallas_call | solution.py:508
  2.9 1.1 %collective-permute-start.1 = (f32[40,128]{1,0:T(8,128)S(1)}, f32[40,128]{1,0:T(8,128)S(1)}, u32[]{:S(2)}, u32[]{:S(2)}) collective-permute-start(f32[40,128]{1,0:T(8,128)S(1)} %get-tuple-element.24.refs_0_.own_ref.start_ref), channel_id=1, source_target_pairs={{0,2},{1,3},{2,0},{3,1},{4,6},{5,7},{6,4},{7,5},{8,10},{9,11},{10,... | collective-permute-start | bytes 61448 | tf_op jit(solution)/shard_map/ppermute | solution.py:46
  4.0 0.2 %read_links.1 = (s32[24,128]{1,0:T(8,128)S(1)}, f32[16,8,128]{2,1,0:T(8,128)S(1)}, s32[2,6]{1,0:T(2,128)S(4)}) custom-call(s32[2,6]{1,0:T(2,128)S(4)} %get-tuple-element.18.links_ref, f32[20,1,128]{2,1,0:T(1,128)S(1)} %get-tuple-element.19.coarse_ref), custom_call_target="tpu_custom_call" | custom-call | tf_op jit(solution)/shard_map/read_links/pallas_call | solution.py:528
  4.2 0.0 collective-permute-done.refs_0_
  4.2 0.5 %interpolate.1.ghost_ref = f32[120,128]{1,0:T(8,128)S(1)} custom-call(s32[2,4,6]{2,1,0:T(4,128)S(4)} %get-tuple-element.21.corner_ref, f32[16,8,128]{2,1,0:T(8,128)S(1)} %get-tuple-element.22.own_table, f32[20,1,128]{2,1,0:T(1,128)S(1)} %collective-permute-done.refs_0_), custom_call_target="tpu_custom_call" | custom-call | flops 10000000000 | bytes 10000000000 | tf_op jit(solution)/shard_map/interpolate/pallas_call | solution.py:541
  4.7 0.1 %fold.2.ready_ref = f32[720,128]{1,0:T(8,128)S(1)} custom-call(f32[120,128]{1,0:T(8,128)S(1)} %interpolate.1.ghost_ref, s32[24,128]{1,0:T(8,128)S(1)} %get-tuple-element.23.pick_ref, f32[40,128]{1,0:T(8,128)S(1)} %get-tuple-element.24.refs_0_.own_ref.start_ref), custom_call_target="tpu_custom_call" | custom-call | tf_op jit(solution)/shard_map/fold/pallas_call | solution.py:561
  4.9 0.0 collective-permute-done.1.even_ref
  4.9 1.0 %collective-permute-done.2.odd_ref = f32[40,128]{1,0:T(8,128)S(1)} collective-permute-done((f32[40,128]{1,0:T(8,128)}, f32[40,128]{1,0:T(8,128)S(1)}, u32[]{:S(2)}, u32[]{:S(2)}) %collective-permute-start.2) | collective-permute-done | bytes 20512 | tf_op jit(solution)/shard_map/ppermute | solution.py:46
  5.8 0.4 %first_stage_odd.1 = (f32[40,128]{1,0:T(8,128)S(1)}, f32[32,128]{1,0:T(8,128)S(1)}, f32[8,128]{1,0:T(8,128)S(1)}) custom-call(s32[2,6]{1,0:T(2,128)S(4)} %get-tuple-element.20.waits_ref, f32[720,128]{1,0:T(8,128)S(1)} %fold.2.ready_ref, s32[24,128]{1,0:T(8,128)S(1)} %get-tuple-element.23.pick_ref, ...), custom_call_target="tpu_custom_call", output_to_operand_aliasing={{0}: (6, {}), {1}: (7, {}), {2}: (8, {})} | custom-call | tf_op jit(solution)/shard_map/first_stage_odd/pallas_call | solution.py:579
  6.3 0.6 %collective-permute-start.5 = (f32[40,128]{1,0:T(8,128)S(1)}, f32[40,128]{1,0:T(8,128)S(1)}, u32[]{:S(2)}, u32[]{:S(2)}) collective-permute-start(f32[40,128]{1,0:T(8,128)S(1)} %get-tuple-element.30), channel_id=1, source_target_pairs={{0,1},{1,0},{2,4},{3,5},{4,2},{5,3},{6,8},{7,9},{8,6},{9,7},{10,12... | collective-permute-start | bytes 61448 | tf_op jit(solution)/shard_map/ppermute | solution.py:46
  6.9 0.2 %collective-permute-start.3 = (f32[32,128]{1,0:T(8,128)S(1)}, f32[32,128]{1,0:T(8,128)S(1)}, u32[]{:S(2)}, u32[]{:S(2)}) collective-permute-start(f32[32,128]{1,0:T(8,128)S(1)} %get-tuple-element.28.refs_0_), channel_id=1, source_target_pairs={{0,2},{1,3},{2,0},{3,1},{4,6},{5,7},{6,4},{7,5},{8,10},{9,11},{10,... | collective-permute-start | bytes 49160 | tf_op jit(solution)/shard_map/ppermute | solution.py:46
  7.1 0.3 %collective-permute-start.4 = (f32[8,128]{1,0:T(8,128)S(1)}, f32[8,128]{1,0:T(8,128)S(1)}, u32[]{:S(2)}, u32[]{:S(2)}) collective-permute-start(f32[8,128]{1,0:T(8,128)S(1)} %get-tuple-element.29.refs_1_), channel_id=1, source_target_pairs={{0,2},{1,3},{2,0},{3,1},{4,6},{5,7},{6,4},{7,5},{8,10},{9,11},{10,... | collective-permute-start | bytes 12296 | tf_op jit(solution)/shard_map/ppermute | solution.py:46
  8.0 0.1 %fold.3.ready_ref = f32[720,128]{1,0:T(8,128)S(1)} custom-call(f32[120,128]{1,0:T(8,128)S(1)} %interpolate.1.ghost_ref, s32[24,128]{1,0:T(8,128)S(1)} %get-tuple-element.23.pick_ref, f32[32,128]{1,0:T(8,128)S(1)} %get-tuple-element.28.refs_0_, f32[8,128]{1,0:T(8,128)S(1)} %get-tuple-element.29.refs_1_), custom_call_target="tpu_custom_call" | custom-call | tf_op jit(solution)/shard_map/fold/pallas_call | solution.py:561
  8.2 0.1 collective-permute-done.4.refs_3_
  8.2 0.0 collective-permute-done.3.refs_2_
  8.2 2.2 %collective-permute-done.5.refs_4_ = f32[40,128]{1,0:T(8,128)S(1)} collective-permute-done((f32[40,128]{1,0:T(8,128)S(1)}, f32[40,128]{1,0:T(8,128)S(1)}, u32[]{:S(2)}, u32[]{:S(2)}) %collective-permute-start.5) | collective-permute-done | bytes 20512 | tf_op jit(solution)/shard_map/ppermute | solution.py:46
  10.4 1.0 %second_stage_odd.1 = f32[40,128]{1,0:T(8,128)} custom-call(s32[2,6]{1,0:T(2,128)S(4)} %get-tuple-element.20.waits_ref, s32[1,1]{1,0:T(1,128)S(6)} %copy.16.count_ref, f32[720,128]{1,0:T(8,128)S(1)} %fold.3.ready_ref, s32[24,128]{1,0:T(8,128)S(1)} %get-tuple-element.23.pick_ref, ...), custom_call_target="tpu_custom_call", output_to_operand_aliasing={{}: (10, {})} | custom-call | tf_op jit(solution)/shard_map/second_stage_odd/pallas_call | solution.py:601
  (2 shorter events, 0.0 us)
Async XLA Ops:
  0.0 4.2 %collective-permute-start = (f32[20,1,128]{2,1,0:T(1,128)}, f32[20,1,128]{2,1,0:T(1,128)S(1)}, u32[]{:S(2)}, u32[]{:S(2)}) collective-permute-start(f32[20,1,128]{2,1,0:T(1,128)} %bitcast.17), channel_id=1, source_target_pairs={{0,1},{1,0},{2,3},{3,2},{4,5},{5,4},{6,7},{7,6},{8,9},{9,8},{10,11... | collective-permute-start | bytes 30728 | tf_op jit(solution)/shard_map/ppermute | solution.py:46
  1.5 4.3 %collective-permute-start.2 = (f32[40,128]{1,0:T(8,128)}, f32[40,128]{1,0:T(8,128)S(1)}, u32[]{:S(2)}, u32[]{:S(2)}) collective-permute-start(f32[40,128]{1,0:T(8,128)} %bitcast.15), channel_id=1, source_target_pairs={{0,1},{1,0},{2,4},{3,5},{4,2},{5,3},{6,8},{7,9},{8,6},{9,7},{10,12... | collective-permute-start | bytes 61448 | tf_op jit(solution)/shard_map/ppermute | solution.py:46
  2.9 2.0 %collective-permute-start.1 = (f32[40,128]{1,0:T(8,128)S(1)}, f32[40,128]{1,0:T(8,128)S(1)}, u32[]{:S(2)}, u32[]{:S(2)}) collective-permute-start(f32[40,128]{1,0:T(8,128)S(1)} %get-tuple-element.24.refs_0_.own_ref.start_ref), channel_id=1, source_target_pairs={{0,2},{1,3},{2,0},{3,1},{4,6},{5,7},{6,4},{7,5},{8,10},{9,11},{10,... | collective-permute-start | bytes 61448 | tf_op jit(solution)/shard_map/ppermute | solution.py:46
  6.3 4.2 %collective-permute-start.5 = (f32[40,128]{1,0:T(8,128)S(1)}, f32[40,128]{1,0:T(8,128)S(1)}, u32[]{:S(2)}, u32[]{:S(2)}) collective-permute-start(f32[40,128]{1,0:T(8,128)S(1)} %get-tuple-element.30), channel_id=1, source_target_pairs={{0,1},{1,0},{2,4},{3,5},{4,2},{5,3},{6,8},{7,9},{8,6},{9,7},{10,12... | collective-permute-start | bytes 61448 | tf_op jit(solution)/shard_map/ppermute | solution.py:46
  6.9 1.4 %collective-permute-start.3 = (f32[32,128]{1,0:T(8,128)S(1)}, f32[32,128]{1,0:T(8,128)S(1)}, u32[]{:S(2)}, u32[]{:S(2)}) collective-permute-start(f32[32,128]{1,0:T(8,128)S(1)} %get-tuple-element.28.refs_0_), channel_id=1, source_target_pairs={{0,2},{1,3},{2,0},{3,1},{4,6},{5,7},{6,4},{7,5},{8,10},{9,11},{10,... | collective-permute-start | bytes 49160 | tf_op jit(solution)/shard_map/ppermute | solution.py:46
  7.1 1.2 %collective-permute-start.4 = (f32[8,128]{1,0:T(8,128)S(1)}, f32[8,128]{1,0:T(8,128)S(1)}, u32[]{:S(2)}, u32[]{:S(2)}) collective-permute-start(f32[8,128]{1,0:T(8,128)S(1)} %get-tuple-element.29.refs_1_), channel_id=1, source_target_pairs={{0,2},{1,3},{2,0},{3,1},{4,6},{5,7},{6,4},{7,5},{8,10},{9,11},{10,... | collective-permute-start | bytes 12296 | tf_op jit(solution)/shard_map/ppermute | solution.py:46

commit v7 on v6

--- a/solution.py
+++ b/solution.py
@@ -132,16 +132,15 @@
     cells = [raw[j] for j in range(4)]
     halves = [roll_lanes(c, 64) for c in cells]
     for j in range(4):
-        u = cells[j]
-        up = jnp.where(low, halves[j], halves[min(j + 1, 3)])
-        down = jnp.where(low, halves[max(j - 1, 0)], halves[j])
-        slopes = (
-            0.25 * minmod(up - u, u - down),
-            0.25 * minmod(roll_lanes(u, -8) - u, u - roll_lanes(u, 8)),
-            0.25 * minmod(roll_lanes(u, -1) - u, u - roll_lanes(u, 1)),
-        )
-        along_x, along_y, along_z = slopes
-        swapped_x, swapped_y, swapped_z = [roll_lanes(v, 64) for v in slopes]
+        u, other, after, before = cells[j], halves[j], min(j + 1, 3), max(j - 1, 0)
+
+        def slope_of(up, value, down):
+            return 0.25 * minmod(up - value, value - down)
+
+        along_x = slope_of(jnp.where(low, other, halves[after]), u, jnp.where(low, halves[before], other))
+        swapped_x = slope_of(jnp.where(low, cells[after], u), other, jnp.where(low, u, cells[before]))
+        along_y, along_z = [slope_of(roll_lanes(u, -n), u, roll_lanes(u, n)) for n in (8, 1)]
+        swapped_y, swapped_z = [slope_of(roll_lanes(u, 64 - n), other, roll_lanes(u, 64 + n)) for n in (8, 1)]
         for x in (2 * j, 2 * j + 1):
             if x in (0, 7):
                 continue
@@ -370,7 +369,7 @@
                     continue
                 shifted = SHIFTED + (direction * FIELDS + f) * len(SHIFTS) + SHIFTS.index(s)
                 own_s, ghost_s = ready_ref[pl.ds(shifted * ROWS, ROWS), :], roll_rows(ghost, -s)
-                outside = (sub + s < 0) | (sub + s > 7)
+                outside = (sub < -s) if s < 0 else (sub > 7 - s)
                 cells.append(jnp.where(outside, ghost_s, own_s))
                 rolled_own[s], rolled_ghost[s] = own_s, ghost_s
             for s in range(-2, 3):

time: 11.6 us -> 11.6 us (level)
  waiting for transfers between devices: 3.22 us -> 3.36 us
  Pallas kernels: 3.23 us -> 3.1 us
    ppermute x6, waiting for transfers between devices: 3.22 us -> 3.36 us  [exchange(): return lax.ppermute(value, ('sfc', 'sub'), pairs)]
  transfers between devices with their start and end apart: 6 -> 6, of which waited for: 3 -> 3; matrix products, arithmetic and copies ran while one was open for 0% -> 0% of each run, Pallas kernels for 15% -> 14%
where the time goes in v7:
time: 11.6 us; the launch traced here: 11.5 us
  starting transfers between devices  4.3 us (37%)
  waiting for transfers between devices  3.36 us (29%)
  Pallas kernels  3.1 us (27%)
  between operations  0.7 us (6%)
    ppermute x6, starting transfers between devices, exchange(): return lax.ppermute(value, ('sfc', 'sub'), pairs)  4.3 us
    ppermute x6, waiting for transfers between devices, exchange(): return lax.ppermute(value, ('sfc', 'sub'), pairs)  3.36 us
    pallas_call x1, Pallas kernels, body(): pl.pallas_call(second_stage_odd, out_shape=jax.ShapeDtypeStruct(tiles, jn...  1.03 us
    pallas_call x1, Pallas kernels, body(): pl.pallas_call(fetch, out_shape=(pltpu.SMEM((2, 6), jnp.int32), pltpu.SME...  0.8 us
    pallas_call x1, Pallas kernels, body(): pl.pallas_call(interpolate, out_shape=pltpu.VMEM((3 * tile_rows, LANES),...  0.42 us
    pallas_call x1, Pallas kernels, body(): pl.pallas_call(first_stage_odd, out_shape=made, in_specs=[smem_spec()] +...  0.41 us
    pallas_call x2, Pallas kernels, fold(): pl.pallas_call(make_ready, out_shape=pltpu.VMEM((READY * ROWS, LANES), jn...  0.26 us
  transfers between devices with their start and end apart: 6, of which 3 were waited for; matrix products, arithmetic and copies ran while one was open for 0% of the time, Pallas kernels for 14%

profile of v7, /device:TPU:16, one launch (start us, length us, event | category | flops | bytes accessed | tf_op | source)
XLA Modules:
  0.0 11.5 jit_solution(4756430972860039627)
XLA Ops:
  0.0 1.5 %collective-permute-start = (f32[20,1,128]{2,1,0:T(1,128)}, f32[20,1,128]{2,1,0:T(1,128)S(1)}, u32[]{:S(2)}, u32[]{:S(2)}) collective-permute-start(f32[20,1,128]{2,1,0:T(1,128)} %bitcast.17), channel_id=1, source_target_pairs={{0,1},{1,0},{2,3},{3,2},{4,5},{5,4},{6,7},{7,6},{8,9},{9,8},{10,11... | collective-permute-start | bytes 30728 | tf_op jit(solution)/shard_map/ppermute | solution.py:46
  1.5 0.5 %collective-permute-start.2 = (f32[40,128]{1,0:T(8,128)}, f32[40,128]{1,0:T(8,128)S(1)}, u32[]{:S(2)}, u32[]{:S(2)}) collective-permute-start(f32[40,128]{1,0:T(8,128)} %bitcast.15), channel_id=1, source_target_pairs={{0,1},{1,0},{2,4},{3,5},{4,2},{5,3},{6,8},{7,9},{8,6},{9,7},{10,12... | collective-permute-start | bytes 61448 | tf_op jit(solution)/shard_map/ppermute | solution.py:46
  2.1 0.8 %fetch.1 = (s32[2,6]{1,0:T(2,128)S(4)}, s32[2,4,6]{2,1,0:T(4,128)S(4)}, f32[20,1,128]{2,1,0:T(1,128)S(1)}, f32[40,128]{1,0:T(8,128)S(1)}) custom-call(s32[2,6]{1,0:T(2,128)} %bitcast.20, s32[2,4,6]{2,1,0:T(4,128)} %bitcast.19, f32[20,1,128]{2,1,0:T(1,128)} %bitcast.18, f32[40,128]{1,0:T(8,128)} %bitcast.16), custom_call_target="tpu_custom_call" | custom-call | tf_op jit(solution)/shard_map/fetch/pallas_call | solution.py:507
  2.9 1.1 %collective-permute-start.1 = (f32[40,128]{1,0:T(8,128)S(1)}, f32[40,128]{1,0:T(8,128)S(1)}, u32[]{:S(2)}, u32[]{:S(2)}) collective-permute-start(f32[40,128]{1,0:T(8,128)S(1)} %get-tuple-element.24.refs_0_.own_ref.start_ref), channel_id=1, source_target_pairs={{0,2},{1,3},{2,0},{3,1},{4,6},{5,7},{6,4},{7,5},{8,10},{9,11},{10,... | collective-permute-start | bytes 61448 | tf_op jit(solution)/shard_map/ppermute | solution.py:46
  4.0 0.2 %read_links.1 = (s32[24,128]{1,0:T(8,128)S(1)}, f32[16,8,128]{2,1,0:T(8,128)S(1)}, s32[2,6]{1,0:T(2,128)S(4)}) custom-call(s32[2,6]{1,0:T(2,128)S(4)} %get-tuple-element.18.links_ref, f32[20,1,128]{2,1,0:T(1,128)S(1)} %get-tuple-element.19.coarse_ref), custom_call_target="tpu_custom_call" | custom-call | tf_op jit(solution)/shard_map/read_links/pallas_call | solution.py:527
  4.2 0.0 collective-permute-done.refs_0_
  4.2 0.4 %interpolate.1.ghost_ref = f32[120,128]{1,0:T(8,128)S(1)} custom-call(s32[2,4,6]{2,1,0:T(4,128)S(4)} %get-tuple-element.21.corner_ref, f32[16,8,128]{2,1,0:T(8,128)S(1)} %get-tuple-element.22.own_table, f32[20,1,128]{2,1,0:T(1,128)S(1)} %collective-permute-done.refs_0_), custom_call_target="tpu_custom_call" | custom-call | flops 10000000000 | bytes 10000000000 | tf_op jit(solution)/shard_map/interpolate/pallas_call | solution.py:540
  4.6 0.1 %fold.2.ready_ref = f32[720,128]{1,0:T(8,128)S(1)} custom-call(f32[120,128]{1,0:T(8,128)S(1)} %interpolate.1.ghost_ref, s32[24,128]{1,0:T(8,128)S(1)} %get-tuple-element.23.pick_ref, f32[40,128]{1,0:T(8,128)S(1)} %get-tuple-element.24.refs_0_.own_ref.start_ref), custom_call_target="tpu_custom_call" | custom-call | tf_op jit(solution)/shard_map/fold/pallas_call | solution.py:560
  4.7 0.1 collective-permute-done.1.even_ref
  4.8 1.0 %collective-permute-done.2.odd_ref = f32[40,128]{1,0:T(8,128)S(1)} collective-permute-done((f32[40,128]{1,0:T(8,128)}, f32[40,128]{1,0:T(8,128)S(1)}, u32[]{:S(2)}, u32[]{:S(2)}) %collective-permute-start.2) | collective-permute-done | bytes 20512 | tf_op jit(solution)/shard_map/ppermute | solution.py:46
  5.8 0.4 %first_stage_odd.1 = (f32[40,128]{1,0:T(8,128)S(1)}, f32[32,128]{1,0:T(8,128)S(1)}, f32[8,128]{1,0:T(8,128)S(1)}) custom-call(s32[2,6]{1,0:T(2,128)S(4)} %get-tuple-element.20.waits_ref, f32[720,128]{1,0:T(8,128)S(1)} %fold.2.ready_ref, s32[24,128]{1,0:T(8,128)S(1)} %get-tuple-element.23.pick_ref, ...), custom_call_target="tpu_custom_call", output_to_operand_aliasing={{0}: (6, {}), {1}: (7, {}), {2}: (8, {})} | custom-call | tf_op jit(solution)/shard_map/first_stage_odd/pallas_call | solution.py:578
  6.3 0.6 %collective-permute-start.5 = (f32[40,128]{1,0:T(8,128)S(1)}, f32[40,128]{1,0:T(8,128)S(1)}, u32[]{:S(2)}, u32[]{:S(2)}) collective-permute-start(f32[40,128]{1,0:T(8,128)S(1)} %get-tuple-element.30), channel_id=1, source_target_pairs={{0,1},{1,0},{2,4},{3,5},{4,2},{5,3},{6,8},{7,9},{8,6},{9,7},{10,12... | collective-permute-start | bytes 61448 | tf_op jit(solution)/shard_map/ppermute | solution.py:46
  6.9 0.2 %collective-permute-start.3 = (f32[32,128]{1,0:T(8,128)S(1)}, f32[32,128]{1,0:T(8,128)S(1)}, u32[]{:S(2)}, u32[]{:S(2)}) collective-permute-start(f32[32,128]{1,0:T(8,128)S(1)} %get-tuple-element.28.refs_0_), channel_id=1, source_target_pairs={{0,2},{1,3},{2,0},{3,1},{4,6},{5,7},{6,4},{7,5},{8,10},{9,11},{10,... | collective-permute-start | bytes 49160 | tf_op jit(solution)/shard_map/ppermute | solution.py:46
  7.0 0.3 %collective-permute-start.4 = (f32[8,128]{1,0:T(8,128)S(1)}, f32[8,128]{1,0:T(8,128)S(1)}, u32[]{:S(2)}, u32[]{:S(2)}) collective-permute-start(f32[8,128]{1,0:T(8,128)S(1)} %get-tuple-element.29.refs_1_), channel_id=1, source_target_pairs={{0,2},{1,3},{2,0},{3,1},{4,6},{5,7},{6,4},{7,5},{8,10},{9,11},{10,... | collective-permute-start | bytes 12296 | tf_op jit(solution)/shard_map/ppermute | solution.py:46
  8.0 0.1 %fold.3.ready_ref = f32[720,128]{1,0:T(8,128)S(1)} custom-call(f32[120,128]{1,0:T(8,128)S(1)} %interpolate.1.ghost_ref, s32[24,128]{1,0:T(8,128)S(1)} %get-tuple-element.23.pick_ref, f32[32,128]{1,0:T(8,128)S(1)} %get-tuple-element.28.refs_0_, f32[8,128]{1,0:T(8,128)S(1)} %get-tuple-element.29.refs_1_), custom_call_target="tpu_custom_call" | custom-call | tf_op jit(solution)/shard_map/fold/pallas_call | solution.py:560
  8.1 0.0 collective-permute-done.4.refs_3_
  8.2 0.0 collective-permute-done.3.refs_2_
  8.2 2.2 %collective-permute-done.5.refs_4_ = f32[40,128]{1,0:T(8,128)S(1)} collective-permute-done((f32[40,128]{1,0:T(8,128)S(1)}, f32[40,128]{1,0:T(8,128)S(1)}, u32[]{:S(2)}, u32[]{:S(2)}) %collective-permute-start.5) | collective-permute-done | bytes 20512 | tf_op jit(solution)/shard_map/ppermute | solution.py:46
  10.4 1.0 %second_stage_odd.1 = f32[40,128]{1,0:T(8,128)} custom-call(s32[2,6]{1,0:T(2,128)S(4)} %get-tuple-element.20.waits_ref, s32[1,1]{1,0:T(1,128)S(6)} %copy.16.count_ref, f32[720,128]{1,0:T(8,128)S(1)} %fold.3.ready_ref, s32[24,128]{1,0:T(8,128)S(1)} %get-tuple-element.23.pick_ref, ...), custom_call_target="tpu_custom_call", output_to_operand_aliasing={{}: (10, {})} | custom-call | tf_op jit(solution)/shard_map/second_stage_odd/pallas_call | solution.py:600
  (2 shorter events, 0.0 us)
Async XLA Ops:
  0.0 4.2 %collective-permute-start = (f32[20,1,128]{2,1,0:T(1,128)}, f32[20,1,128]{2,1,0:T(1,128)S(1)}, u32[]{:S(2)}, u32[]{:S(2)}) collective-permute-start(f32[20,1,128]{2,1,0:T(1,128)} %bitcast.17), channel_id=1, source_target_pairs={{0,1},{1,0},{2,3},{3,2},{4,5},{5,4},{6,7},{7,6},{8,9},{9,8},{10,11... | collective-permute-start | bytes 30728 | tf_op jit(solution)/shard_map/ppermute | solution.py:46
  1.5 4.3 %collective-permute-start.2 = (f32[40,128]{1,0:T(8,128)}, f32[40,128]{1,0:T(8,128)S(1)}, u32[]{:S(2)}, u32[]{:S(2)}) collective-permute-start(f32[40,128]{1,0:T(8,128)} %bitcast.15), channel_id=1, source_target_pairs={{0,1},{1,0},{2,4},{3,5},{4,2},{5,3},{6,8},{7,9},{8,6},{9,7},{10,12... | collective-permute-start | bytes 61448 | tf_op jit(solution)/shard_map/ppermute | solution.py:46
  2.9 2.0 %collective-permute-start.1 = (f32[40,128]{1,0:T(8,128)S(1)}, f32[40,128]{1,0:T(8,128)S(1)}, u32[]{:S(2)}, u32[]{:S(2)}) collective-permute-start(f32[40,128]{1,0:T(8,128)S(1)} %get-tuple-element.24.refs_0_.own_ref.start_ref), channel_id=1, source_target_pairs={{0,2},{1,3},{2,0},{3,1},{4,6},{5,7},{6,4},{7,5},{8,10},{9,11},{10,... | collective-permute-start | bytes 61448 | tf_op jit(solution)/shard_map/ppermute | solution.py:46
  6.3 4.2 %collective-permute-start.5 = (f32[40,128]{1,0:T(8,128)S(1)}, f32[40,128]{1,0:T(8,128)S(1)}, u32[]{:S(2)}, u32[]{:S(2)}) collective-permute-start(f32[40,128]{1,0:T(8,128)S(1)} %get-tuple-element.30), channel_id=1, source_target_pairs={{0,1},{1,0},{2,4},{3,5},{4,2},{5,3},{6,8},{7,9},{8,6},{9,7},{10,12... | collective-permute-start | bytes 61448 | tf_op jit(solution)/shard_map/ppermute | solution.py:46
  6.9 1.3 %collective-permute-start.3 = (f32[32,128]{1,0:T(8,128)S(1)}, f32[32,128]{1,0:T(8,128)S(1)}, u32[]{:S(2)}, u32[]{:S(2)}) collective-permute-start(f32[32,128]{1,0:T(8,128)S(1)} %get-tuple-element.28.refs_0_), channel_id=1, source_target_pairs={{0,2},{1,3},{2,0},{3,1},{4,6},{5,7},{6,4},{7,5},{8,10},{9,11},{10,... | collective-permute-start | bytes 49160 | tf_op jit(solution)/shard_map/ppermute | solution.py:46
  7.0 1.2 %collective-permute-start.4 = (f32[8,128]{1,0:T(8,128)S(1)}, f32[8,128]{1,0:T(8,128)S(1)}, u32[]{:S(2)}, u32[]{:S(2)}) collective-permute-start(f32[8,128]{1,0:T(8,128)S(1)} %get-tuple-element.29.refs_1_), channel_id=1, source_target_pairs={{0,2},{1,3},{2,0},{3,1},{4,6},{5,7},{6,4},{7,5},{8,10},{9,11},{10,... | collective-permute-start | bytes 12296 | tf_op jit(solution)/shard_map/ppermute | solution.py:46

commit v8 on v7

--- a/solution.py
+++ b/solution.py
@@ -85,10 +85,7 @@
 
 
 def roll_rows(value, steps):
-    if steps % ROWS == 0:
-        return value
-    sub, _ = positions()
-    return gather_rows(value, (sub - steps) & 7)
+    return pltpu.roll(value, steps % ROWS, 0) if steps % ROWS else value
 
 
 def reciprocal(value):

time: 11.6 us -> 11.6 us (level)
  no operation moved by 1% of the time
where the time goes in v8:
time: 11.6 us; the launch traced here: 11.5 us
  starting transfers between devices  4.3 us (37%)
  waiting for transfers between devices  3.36 us (29%)
  Pallas kernels  3.1 us (27%)
  between operations  0.71 us (6%)
    ppermute x6, starting transfers between devices, exchange(): return lax.ppermute(value, ('sfc', 'sub'), pairs)  4.3 us
    ppermute x6, waiting for transfers between devices, exchange(): return lax.ppermute(value, ('sfc', 'sub'), pairs)  3.36 us
    pallas_call x1, Pallas kernels, body(): pl.pallas_call(second_stage_odd, out_shape=jax.ShapeDtypeStruct(tiles, jn...  1.03 us
    pallas_call x1, Pallas kernels, body(): pl.pallas_call(fetch, out_shape=(pltpu.SMEM((2, 6), jnp.int32), pltpu.SME...  0.8 us
    pallas_call x1, Pallas kernels, body(): pl.pallas_call(interpolate, out_shape=pltpu.VMEM((3 * tile_rows, LANES),...  0.42 us
    pallas_call x1, Pallas kernels, body(): pl.pallas_call(first_stage_odd, out_shape=made, in_specs=[smem_spec()] +...  0.41 us
    pallas_call x2, Pallas kernels, fold(): pl.pallas_call(make_ready, out_shape=pltpu.VMEM((READY * ROWS, LANES), jn...  0.26 us
  transfers between devices with their start and end apart: 6, of which 3 were waited for; matrix products, arithmetic and copies ran while one was open for 0% of the time, Pallas kernels for 14%

profile of v8, /device:TPU:16, one launch (start us, length us, event | category | flops | bytes accessed | tf_op | source)
XLA Modules:
  0.0 11.5 jit_solution(10144706438926937087)
XLA Ops:
  0.0 1.5 %collective-permute-start = (f32[20,1,128]{2,1,0:T(1,128)}, f32[20,1,128]{2,1,0:T(1,128)S(1)}, u32[]{:S(2)}, u32[]{:S(2)}) collective-permute-start(f32[20,1,128]{2,1,0:T(1,128)} %bitcast.17), channel_id=1, source_target_pairs={{0,1},{1,0},{2,3},{3,2},{4,5},{5,4},{6,7},{7,6},{8,9},{9,8},{10,11... | collective-permute-start | bytes 30728 | tf_op jit(solution)/shard_map/ppermute | solution.py:46
  1.5 0.5 %collective-permute-start.2 = (f32[40,128]{1,0:T(8,128)}, f32[40,128]{1,0:T(8,128)S(1)}, u32[]{:S(2)}, u32[]{:S(2)}) collective-permute-start(f32[40,128]{1,0:T(8,128)} %bitcast.15), channel_id=1, source_target_pairs={{0,1},{1,0},{2,4},{3,5},{4,2},{5,3},{6,8},{7,9},{8,6},{9,7},{10,12... | collective-permute-start | bytes 61448 | tf_op jit(solution)/shard_map/ppermute | solution.py:46
  2.1 0.8 %fetch.1 = (s32[2,6]{1,0:T(2,128)S(4)}, s32[2,4,6]{2,1,0:T(4,128)S(4)}, f32[20,1,128]{2,1,0:T(1,128)S(1)}, f32[40,128]{1,0:T(8,128)S(1)}) custom-call(s32[2,6]{1,0:T(2,128)} %bitcast.20, s32[2,4,6]{2,1,0:T(4,128)} %bitcast.19, f32[20,1,128]{2,1,0:T(1,128)} %bitcast.18, f32[40,128]{1,0:T(8,128)} %bitcast.16), custom_call_target="tpu_custom_call" | custom-call | tf_op jit(solution)/shard_map/fetch/pallas_call | solution.py:504
  2.9 1.1 %collective-permute-start.1 = (f32[40,128]{1,0:T(8,128)S(1)}, f32[40,128]{1,0:T(8,128)S(1)}, u32[]{:S(2)}, u32[]{:S(2)}) collective-permute-start(f32[40,128]{1,0:T(8,128)S(1)} %get-tuple-element.24.refs_0_.own_ref.start_ref), channel_id=1, source_target_pairs={{0,2},{1,3},{2,0},{3,1},{4,6},{5,7},{6,4},{7,5},{8,10},{9,11},{10,... | collective-permute-start | bytes 61448 | tf_op jit(solution)/shard_map/ppermute | solution.py:46
  4.0 0.2 %read_links.1 = (s32[24,128]{1,0:T(8,128)S(1)}, f32[16,8,128]{2,1,0:T(8,128)S(1)}, s32[2,6]{1,0:T(2,128)S(4)}) custom-call(s32[2,6]{1,0:T(2,128)S(4)} %get-tuple-element.18.links_ref, f32[20,1,128]{2,1,0:T(1,128)S(1)} %get-tuple-element.19.coarse_ref), custom_call_target="tpu_custom_call" | custom-call | tf_op jit(solution)/shard_map/read_links/pallas_call | solution.py:524
  4.2 0.0 collective-permute-done.refs_0_
  4.2 0.4 %interpolate.1.ghost_ref = f32[120,128]{1,0:T(8,128)S(1)} custom-call(s32[2,4,6]{2,1,0:T(4,128)S(4)} %get-tuple-element.21.corner_ref, f32[16,8,128]{2,1,0:T(8,128)S(1)} %get-tuple-element.22.own_table, f32[20,1,128]{2,1,0:T(1,128)S(1)} %collective-permute-done.refs_0_), custom_call_target="tpu_custom_call" | custom-call | flops 10000000000 | bytes 10000000000 | tf_op jit(solution)/shard_map/interpolate/pallas_call | solution.py:537
  4.6 0.1 %fold.2.ready_ref = f32[720,128]{1,0:T(8,128)S(1)} custom-call(f32[120,128]{1,0:T(8,128)S(1)} %interpolate.1.ghost_ref, s32[24,128]{1,0:T(8,128)S(1)} %get-tuple-element.23.pick_ref, f32[40,128]{1,0:T(8,128)S(1)} %get-tuple-element.24.refs_0_.own_ref.start_ref), custom_call_target="tpu_custom_call" | custom-call | tf_op jit(solution)/shard_map/fold/pallas_call | solution.py:557
  4.7 0.1 collective-permute-done.1.even_ref
  4.8 1.0 %collective-permute-done.2.odd_ref = f32[40,128]{1,0:T(8,128)S(1)} collective-permute-done((f32[40,128]{1,0:T(8,128)}, f32[40,128]{1,0:T(8,128)S(1)}, u32[]{:S(2)}, u32[]{:S(2)}) %collective-permute-start.2) | collective-permute-done | bytes 20512 | tf_op jit(solution)/shard_map/ppermute | solution.py:46
  5.8 0.4 %first_stage_odd.1 = (f32[40,128]{1,0:T(8,128)S(1)}, f32[32,128]{1,0:T(8,128)S(1)}, f32[8,128]{1,0:T(8,128)S(1)}) custom-call(s32[2,6]{1,0:T(2,128)S(4)} %get-tuple-element.20.waits_ref, f32[720,128]{1,0:T(8,128)S(1)} %fold.2.ready_ref, s32[24,128]{1,0:T(8,128)S(1)} %get-tuple-element.23.pick_ref, ...), custom_call_target="tpu_custom_call", output_to_operand_aliasing={{0}: (6, {}), {1}: (7, {}), {2}: (8, {})} | custom-call | tf_op jit(solution)/shard_map/first_stage_odd/pallas_call | solution.py:575
  6.3 0.6 %collective-permute-start.5 = (f32[40,128]{1,0:T(8,128)S(1)}, f32[40,128]{1,0:T(8,128)S(1)}, u32[]{:S(2)}, u32[]{:S(2)}) collective-permute-start(f32[40,128]{1,0:T(8,128)S(1)} %get-tuple-element.30), channel_id=1, source_target_pairs={{0,1},{1,0},{2,4},{3,5},{4,2},{5,3},{6,8},{7,9},{8,6},{9,7},{10,12... | collective-permute-start | bytes 61448 | tf_op jit(solution)/shard_map/ppermute | solution.py:46
  6.9 0.2 %collective-permute-start.3 = (f32[32,128]{1,0:T(8,128)S(1)}, f32[32,128]{1,0:T(8,128)S(1)}, u32[]{:S(2)}, u32[]{:S(2)}) collective-permute-start(f32[32,128]{1,0:T(8,128)S(1)} %get-tuple-element.28.refs_0_), channel_id=1, source_target_pairs={{0,2},{1,3},{2,0},{3,1},{4,6},{5,7},{6,4},{7,5},{8,10},{9,11},{10,... | collective-permute-start | bytes 49160 | tf_op jit(solution)/shard_map/ppermute | solution.py:46
  7.0 0.3 %collective-permute-start.4 = (f32[8,128]{1,0:T(8,128)S(1)}, f32[8,128]{1,0:T(8,128)S(1)}, u32[]{:S(2)}, u32[]{:S(2)}) collective-permute-start(f32[8,128]{1,0:T(8,128)S(1)} %get-tuple-element.29.refs_1_), channel_id=1, source_target_pairs={{0,2},{1,3},{2,0},{3,1},{4,6},{5,7},{6,4},{7,5},{8,10},{9,11},{10,... | collective-permute-start | bytes 12296 | tf_op jit(solution)/shard_map/ppermute | solution.py:46
  8.0 0.1 %fold.3.ready_ref = f32[720,128]{1,0:T(8,128)S(1)} custom-call(f32[120,128]{1,0:T(8,128)S(1)} %interpolate.1.ghost_ref, s32[24,128]{1,0:T(8,128)S(1)} %get-tuple-element.23.pick_ref, f32[32,128]{1,0:T(8,128)S(1)} %get-tuple-element.28.refs_0_, f32[8,128]{1,0:T(8,128)S(1)} %get-tuple-element.29.refs_1_), custom_call_target="tpu_custom_call" | custom-call | tf_op jit(solution)/shard_map/fold/pallas_call | solution.py:557
  8.1 0.0 collective-permute-done.4.refs_3_
  8.2 0.0 collective-permute-done.3.refs_2_
  8.2 2.2 %collective-permute-done.5.refs_4_ = f32[40,128]{1,0:T(8,128)S(1)} collective-permute-done((f32[40,128]{1,0:T(8,128)S(1)}, f32[40,128]{1,0:T(8,128)S(1)}, u32[]{:S(2)}, u32[]{:S(2)}) %collective-permute-start.5) | collective-permute-done | bytes 20512 | tf_op jit(solution)/shard_map/ppermute | solution.py:46
  10.4 1.0 %second_stage_odd.1 = f32[40,128]{1,0:T(8,128)} custom-call(s32[2,6]{1,0:T(2,128)S(4)} %get-tuple-element.20.waits_ref, s32[1,1]{1,0:T(1,128)S(6)} %copy.16.count_ref, f32[720,128]{1,0:T(8,128)S(1)} %fold.3.ready_ref, s32[24,128]{1,0:T(8,128)S(1)} %get-tuple-element.23.pick_ref, ...), custom_call_target="tpu_custom_call", output_to_operand_aliasing={{}: (10, {})} | custom-call | tf_op jit(solution)/shard_map/second_stage_odd/pallas_call | solution.py:597
  (2 shorter events, 0.0 us)
Async XLA Ops:
  0.0 4.2 %collective-permute-start = (f32[20,1,128]{2,1,0:T(1,128)}, f32[20,1,128]{2,1,0:T(1,128)S(1)}, u32[]{:S(2)}, u32[]{:S(2)}) collective-permute-start(f32[20,1,128]{2,1,0:T(1,128)} %bitcast.17), channel_id=1, source_target_pairs={{0,1},{1,0},{2,3},{3,2},{4,5},{5,4},{6,7},{7,6},{8,9},{9,8},{10,11... | collective-permute-start | bytes 30728 | tf_op jit(solution)/shard_map/ppermute | solution.py:46
  1.5 4.3 %collective-permute-start.2 = (f32[40,128]{1,0:T(8,128)}, f32[40,128]{1,0:T(8,128)S(1)}, u32[]{:S(2)}, u32[]{:S(2)}) collective-permute-start(f32[40,128]{1,0:T(8,128)} %bitcast.15), channel_id=1, source_target_pairs={{0,1},{1,0},{2,4},{3,5},{4,2},{5,3},{6,8},{7,9},{8,6},{9,7},{10,12... | collective-permute-start | bytes 61448 | tf_op jit(solution)/shard_map/ppermute | solution.py:46
  2.9 2.0 %collective-permute-start.1 = (f32[40,128]{1,0:T(8,128)S(1)}, f32[40,128]{1,0:T(8,128)S(1)}, u32[]{:S(2)}, u32[]{:S(2)}) collective-permute-start(f32[40,128]{1,0:T(8,128)S(1)} %get-tuple-element.24.refs_0_.own_ref.start_ref), channel_id=1, source_target_pairs={{0,2},{1,3},{2,0},{3,1},{4,6},{5,7},{6,4},{7,5},{8,10},{9,11},{10,... | collective-permute-start | bytes 61448 | tf_op jit(solution)/shard_map/ppermute | solution.py:46
  6.3 4.2 %collective-permute-start.5 = (f32[40,128]{1,0:T(8,128)S(1)}, f32[40,128]{1,0:T(8,128)S(1)}, u32[]{:S(2)}, u32[]{:S(2)}) collective-permute-start(f32[40,128]{1,0:T(8,128)S(1)} %get-tuple-element.30), channel_id=1, source_target_pairs={{0,1},{1,0},{2,4},{3,5},{4,2},{5,3},{6,8},{7,9},{8,6},{9,7},{10,12... | collective-permute-start | bytes 61448 | tf_op jit(solution)/shard_map/ppermute | solution.py:46
  6.9 1.3 %collective-permute-start.3 = (f32[32,128]{1,0:T(8,128)S(1)}, f32[32,128]{1,0:T(8,128)S(1)}, u32[]{:S(2)}, u32[]{:S(2)}) collective-permute-start(f32[32,128]{1,0:T(8,128)S(1)} %get-tuple-element.28.refs_0_), channel_id=1, source_target_pairs={{0,2},{1,3},{2,0},{3,1},{4,6},{5,7},{6,4},{7,5},{8,10},{9,11},{10,... | collective-permute-start | bytes 49160 | tf_op jit(solution)/shard_map/ppermute | solution.py:46
  7.0 1.2 %collective-permute-start.4 = (f32[8,128]{1,0:T(8,128)S(1)}, f32[8,128]{1,0:T(8,128)S(1)}, u32[]{:S(2)}, u32[]{:S(2)}) collective-permute-start(f32[8,128]{1,0:T(8,128)S(1)} %get-tuple-element.29.refs_1_), channel_id=1, source_target_pairs={{0,2},{1,3},{2,0},{3,1},{4,6},{5,7},{6,4},{7,5},{8,10},{9,11},{10,... | collective-permute-start | bytes 12296 | tf_op jit(solution)/shard_map/ppermute | solution.py:46

commit v9 on v7

--- a/solution.py
+++ b/solution.py
@@ -267,8 +267,10 @@
     speed_left = jnp.minimum(ul - cl, ur - cr)
     speed_right = jnp.maximum(ul + cl, ur + cr)
     ml, mr = rl * (speed_left - ul), rr * (speed_right - ur)
-    contact = (pr - pl_ + ml * ul - mr * ur) * reciprocal(ml - mr)
-    from_left = (speed_left >= 0.0) | (contact >= 0.0)
+    top, bottom = pr - pl_ + ml * ul - mr * ur, ml - mr
+    contact = top * reciprocal(bottom)
+    ahead = top <= 0.0
+    from_left = (speed_left >= 0.0) | ahead
     r = jnp.where(from_left, rl, rr)
     u = jnp.where(from_left, ul, ur)
     v = jnp.where(from_left, vl, vr)
@@ -276,7 +278,7 @@
     p = jnp.where(from_left, pl_, pr)
     s = jnp.where(from_left, speed_left, speed_right)
     m = jnp.where(from_left, ml, mr)
-    star = (speed_left < 0.0) & ((contact >= 0.0) | (speed_right >= 0.0))
+    star = (speed_left < 0.0) & (ahead | (speed_right >= 0.0))
     energy = p * (1.0 / (GAMMA - 1.0)) + 0.5 * r * (u * u + v * v + w * w)
     inverse = reciprocal(s - contact)
     star_p = p + m * (contact - u)

time: 11.6 us -> 11.7 us (level)
  no operation moved by 1% of the time
where the time goes in v9:
time: 11.7 us; the launch traced here: 11.5 us
  starting transfers between devices  4.3 us (37%)
  waiting for transfers between devices  3.35 us (29%)
  Pallas kernels  3.12 us (27%)
  between operations  0.7 us (6%)
    ppermute x6, starting transfers between devices, exchange(): return lax.ppermute(value, ('sfc', 'sub'), pairs)  4.3 us
    ppermute x6, waiting for transfers between devices, exchange(): return lax.ppermute(value, ('sfc', 'sub'), pairs)  3.35 us
    pallas_call x1, Pallas kernels, body(): pl.pallas_call(second_stage_odd, out_shape=jax.ShapeDtypeStruct(tiles, jn...  1.04 us
    pallas_call x1, Pallas kernels, body(): pl.pallas_call(fetch, out_shape=(pltpu.SMEM((2, 6), jnp.int32), pltpu.SME...  0.8 us
    pallas_call x1, Pallas kernels, body(): pl.pallas_call(interpolate, out_shape=pltpu.VMEM((3 * tile_rows, LANES),...  0.42 us
    pallas_call x1, Pallas kernels, body(): pl.pallas_call(first_stage_odd, out_shape=made, in_specs=[smem_spec()] +...  0.42 us
    pallas_call x2, Pallas kernels, fold(): pl.pallas_call(make_ready, out_shape=pltpu.VMEM((READY * ROWS, LANES), jn...  0.26 us
  transfers between devices with their start and end apart: 6, of which 3 were waited for; matrix products, arithmetic and copies ran while one was open for 0% of the time, Pallas kernels for 14%

profile of v9, /device:TPU:16, one launch (start us, length us, event | category | flops | bytes accessed | tf_op | source)
XLA Modules:
  0.0 11.5 jit_solution(7279171116275688678)
XLA Ops:
  0.0 1.5 %collective-permute-start = (f32[20,1,128]{2,1,0:T(1,128)}, f32[20,1,128]{2,1,0:T(1,128)S(1)}, u32[]{:S(2)}, u32[]{:S(2)}) collective-permute-start(f32[20,1,128]{2,1,0:T(1,128)} %bitcast.17), channel_id=1, source_target_pairs={{0,1},{1,0},{2,3},{3,2},{4,5},{5,4},{6,7},{7,6},{8,9},{9,8},{10,11... | collective-permute-start | bytes 30728 | tf_op jit(solution)/shard_map/ppermute | solution.py:46
  1.5 0.5 %collective-permute-start.2 = (f32[40,128]{1,0:T(8,128)}, f32[40,128]{1,0:T(8,128)S(1)}, u32[]{:S(2)}, u32[]{:S(2)}) collective-permute-start(f32[40,128]{1,0:T(8,128)} %bitcast.15), channel_id=1, source_target_pairs={{0,1},{1,0},{2,4},{3,5},{4,2},{5,3},{6,8},{7,9},{8,6},{9,7},{10,12... | collective-permute-start | bytes 61448 | tf_op jit(solution)/shard_map/ppermute | solution.py:46
  2.1 0.8 %fetch.1 = (s32[2,6]{1,0:T(2,128)S(4)}, s32[2,4,6]{2,1,0:T(4,128)S(4)}, f32[20,1,128]{2,1,0:T(1,128)S(1)}, f32[40,128]{1,0:T(8,128)S(1)}) custom-call(s32[2,6]{1,0:T(2,128)} %bitcast.20, s32[2,4,6]{2,1,0:T(4,128)} %bitcast.19, f32[20,1,128]{2,1,0:T(1,128)} %bitcast.18, f32[40,128]{1,0:T(8,128)} %bitcast.16), custom_call_target="tpu_custom_call" | custom-call | tf_op jit(solution)/shard_map/fetch/pallas_call | solution.py:509
  2.9 1.1 %collective-permute-start.1 = (f32[40,128]{1,0:T(8,128)S(1)}, f32[40,128]{1,0:T(8,128)S(1)}, u32[]{:S(2)}, u32[]{:S(2)}) collective-permute-start(f32[40,128]{1,0:T(8,128)S(1)} %get-tuple-element.24.refs_0_.own_ref.start_ref), channel_id=1, source_target_pairs={{0,2},{1,3},{2,0},{3,1},{4,6},{5,7},{6,4},{7,5},{8,10},{9,11},{10,... | collective-permute-start | bytes 61448 | tf_op jit(solution)/shard_map/ppermute | solution.py:46
  4.0 0.2 %read_links.1 = (s32[24,128]{1,0:T(8,128)S(1)}, f32[16,8,128]{2,1,0:T(8,128)S(1)}, s32[2,6]{1,0:T(2,128)S(4)}) custom-call(s32[2,6]{1,0:T(2,128)S(4)} %get-tuple-element.18.links_ref, f32[20,1,128]{2,1,0:T(1,128)S(1)} %get-tuple-element.19.coarse_ref), custom_call_target="tpu_custom_call" | custom-call | tf_op jit(solution)/shard_map/read_links/pallas_call | solution.py:529
  4.2 0.0 collective-permute-done.refs_0_
  4.2 0.4 %interpolate.1.ghost_ref = f32[120,128]{1,0:T(8,128)S(1)} custom-call(s32[2,4,6]{2,1,0:T(4,128)S(4)} %get-tuple-element.21.corner_ref, f32[16,8,128]{2,1,0:T(8,128)S(1)} %get-tuple-element.22.own_table, f32[20,1,128]{2,1,0:T(1,128)S(1)} %collective-permute-done.refs_0_), custom_call_target="tpu_custom_call" | custom-call | flops 10000000000 | bytes 10000000000 | tf_op jit(solution)/shard_map/interpolate/pallas_call | solution.py:542
  4.6 0.1 %fold.2.ready_ref = f32[720,128]{1,0:T(8,128)S(1)} custom-call(f32[120,128]{1,0:T(8,128)S(1)} %interpolate.1.ghost_ref, s32[24,128]{1,0:T(8,128)S(1)} %get-tuple-element.23.pick_ref, f32[40,128]{1,0:T(8,128)S(1)} %get-tuple-element.24.refs_0_.own_ref.start_ref), custom_call_target="tpu_custom_call" | custom-call | tf_op jit(solution)/shard_map/fold/pallas_call | solution.py:562
  4.7 0.1 collective-permute-done.1.even_ref
  4.8 1.0 %collective-permute-done.2.odd_ref = f32[40,128]{1,0:T(8,128)S(1)} collective-permute-done((f32[40,128]{1,0:T(8,128)}, f32[40,128]{1,0:T(8,128)S(1)}, u32[]{:S(2)}, u32[]{:S(2)}) %collective-permute-start.2) | collective-permute-done | bytes 20512 | tf_op jit(solution)/shard_map/ppermute | solution.py:46
  5.8 0.4 %first_stage_odd.1 = (f32[40,128]{1,0:T(8,128)S(1)}, f32[32,128]{1,0:T(8,128)S(1)}, f32[8,128]{1,0:T(8,128)S(1)}) custom-call(s32[2,6]{1,0:T(2,128)S(4)} %get-tuple-element.20.waits_ref, f32[720,128]{1,0:T(8,128)S(1)} %fold.2.ready_ref, s32[24,128]{1,0:T(8,128)S(1)} %get-tuple-element.23.pick_ref, ...), custom_call_target="tpu_custom_call", output_to_operand_aliasing={{0}: (6, {}), {1}: (7, {}), {2}: (8, {})} | custom-call | tf_op jit(solution)/shard_map/first_stage_odd/pallas_call | solution.py:580
  6.3 0.6 %collective-permute-start.5 = (f32[40,128]{1,0:T(8,128)S(1)}, f32[40,128]{1,0:T(8,128)S(1)}, u32[]{:S(2)}, u32[]{:S(2)}) collective-permute-start(f32[40,128]{1,0:T(8,128)S(1)} %get-tuple-element.30), channel_id=1, source_target_pairs={{0,1},{1,0},{2,4},{3,5},{4,2},{5,3},{6,8},{7,9},{8,6},{9,7},{10,12... | collective-permute-start | bytes 61448 | tf_op jit(solution)/shard_map/ppermute | solution.py:46
  6.9 0.2 %collective-permute-start.3 = (f32[32,128]{1,0:T(8,128)S(1)}, f32[32,128]{1,0:T(8,128)S(1)}, u32[]{:S(2)}, u32[]{:S(2)}) collective-permute-start(f32[32,128]{1,0:T(8,128)S(1)} %get-tuple-element.28.refs_0_), channel_id=1, source_target_pairs={{0,2},{1,3},{2,0},{3,1},{4,6},{5,7},{6,4},{7,5},{8,10},{9,11},{10,... | collective-permute-start | bytes 49160 | tf_op jit(solution)/shard_map/ppermute | solution.py:46
  7.0 0.3 %collective-permute-start.4 = (f32[8,128]{1,0:T(8,128)S(1)}, f32[8,128]{1,0:T(8,128)S(1)}, u32[]{:S(2)}, u32[]{:S(2)}) collective-permute-start(f32[8,128]{1,0:T(8,128)S(1)} %get-tuple-element.29.refs_1_), channel_id=1, source_target_pairs={{0,2},{1,3},{2,0},{3,1},{4,6},{5,7},{6,4},{7,5},{8,10},{9,11},{10,... | collective-permute-start | bytes 12296 | tf_op jit(solution)/shard_map/ppermute | solution.py:46
  8.0 0.1 %fold.3.ready_ref = f32[720,128]{1,0:T(8,128)S(1)} custom-call(f32[120,128]{1,0:T(8,128)S(1)} %interpolate.1.ghost_ref, s32[24,128]{1,0:T(8,128)S(1)} %get-tuple-element.23.pick_ref, f32[32,128]{1,0:T(8,128)S(1)} %get-tuple-element.28.refs_0_, f32[8,128]{1,0:T(8,128)S(1)} %get-tuple-element.29.refs_1_), custom_call_target="tpu_custom_call" | custom-call | tf_op jit(solution)/shard_map/fold/pallas_call | solution.py:562
  8.2 0.0 collective-permute-done.4.refs_3_
  8.2 0.0 collective-permute-done.3.refs_2_
  8.2 2.2 %collective-permute-done.5.refs_4_ = f32[40,128]{1,0:T(8,128)S(1)} collective-permute-done((f32[40,128]{1,0:T(8,128)S(1)}, f32[40,128]{1,0:T(8,128)S(1)}, u32[]{:S(2)}, u32[]{:S(2)}) %collective-permute-start.5) | collective-permute-done | bytes 20512 | tf_op jit(solution)/shard_map/ppermute | solution.py:46
  10.4 1.0 %second_stage_odd.1 = f32[40,128]{1,0:T(8,128)} custom-call(s32[2,6]{1,0:T(2,128)S(4)} %get-tuple-element.20.waits_ref, s32[1,1]{1,0:T(1,128)S(6)} %copy.16.count_ref, f32[720,128]{1,0:T(8,128)S(1)} %fold.3.ready_ref, s32[24,128]{1,0:T(8,128)S(1)} %get-tuple-element.23.pick_ref, ...), custom_call_target="tpu_custom_call", output_to_operand_aliasing={{}: (10, {})} | custom-call | tf_op jit(solution)/shard_map/second_stage_odd/pallas_call | solution.py:602
  (2 shorter events, 0.0 us)
Async XLA Ops:
  0.0 4.2 %collective-permute-start = (f32[20,1,128]{2,1,0:T(1,128)}, f32[20,1,128]{2,1,0:T(1,128)S(1)}, u32[]{:S(2)}, u32[]{:S(2)}) collective-permute-start(f32[20,1,128]{2,1,0:T(1,128)} %bitcast.17), channel_id=1, source_target_pairs={{0,1},{1,0},{2,3},{3,2},{4,5},{5,4},{6,7},{7,6},{8,9},{9,8},{10,11... | collective-permute-start | bytes 30728 | tf_op jit(solution)/shard_map/ppermute | solution.py:46
  1.5 4.3 %collective-permute-start.2 = (f32[40,128]{1,0:T(8,128)}, f32[40,128]{1,0:T(8,128)S(1)}, u32[]{:S(2)}, u32[]{:S(2)}) collective-permute-start(f32[40,128]{1,0:T(8,128)} %bitcast.15), channel_id=1, source_target_pairs={{0,1},{1,0},{2,4},{3,5},{4,2},{5,3},{6,8},{7,9},{8,6},{9,7},{10,12... | collective-permute-start | bytes 61448 | tf_op jit(solution)/shard_map/ppermute | solution.py:46
  2.9 2.0 %collective-permute-start.1 = (f32[40,128]{1,0:T(8,128)S(1)}, f32[40,128]{1,0:T(8,128)S(1)}, u32[]{:S(2)}, u32[]{:S(2)}) collective-permute-start(f32[40,128]{1,0:T(8,128)S(1)} %get-tuple-element.24.refs_0_.own_ref.start_ref), channel_id=1, source_target_pairs={{0,2},{1,3},{2,0},{3,1},{4,6},{5,7},{6,4},{7,5},{8,10},{9,11},{10,... | collective-permute-start | bytes 61448 | tf_op jit(solution)/shard_map/ppermute | solution.py:46
  6.3 4.2 %collective-permute-start.5 = (f32[40,128]{1,0:T(8,128)S(1)}, f32[40,128]{1,0:T(8,128)S(1)}, u32[]{:S(2)}, u32[]{:S(2)}) collective-permute-start(f32[40,128]{1,0:T(8,128)S(1)} %get-tuple-element.30), channel_id=1, source_target_pairs={{0,1},{1,0},{2,4},{3,5},{4,2},{5,3},{6,8},{7,9},{8,6},{9,7},{10,12... | collective-permute-start | bytes 61448 | tf_op jit(solution)/shard_map/ppermute | solution.py:46
  6.9 1.3 %collective-permute-start.3 = (f32[32,128]{1,0:T(8,128)S(1)}, f32[32,128]{1,0:T(8,128)S(1)}, u32[]{:S(2)}, u32[]{:S(2)}) collective-permute-start(f32[32,128]{1,0:T(8,128)S(1)} %get-tuple-element.28.refs_0_), channel_id=1, source_target_pairs={{0,2},{1,3},{2,0},{3,1},{4,6},{5,7},{6,4},{7,5},{8,10},{9,11},{10,... | collective-permute-start | bytes 49160 | tf_op jit(solution)/shard_map/ppermute | solution.py:46
  7.0 1.2 %collective-permute-start.4 = (f32[8,128]{1,0:T(8,128)S(1)}, f32[8,128]{1,0:T(8,128)S(1)}, u32[]{:S(2)}, u32[]{:S(2)}) collective-permute-start(f32[8,128]{1,0:T(8,128)S(1)} %get-tuple-element.29.refs_1_), channel_id=1, source_target_pairs={{0,2},{1,3},{2,0},{3,1},{4,6},{5,7},{6,4},{7,5},{8,10},{9,11},{10,... | collective-permute-start | bytes 12296 | tf_op jit(solution)/shard_map/ppermute | solution.py:46
